TPU v7x, 128 devices: a whole 4x4x4 slice. The times are simulated.
128 devices in a mesh: section: 2 (over y_lo), dp: 64 (over z, x, y_hi, core).
Axes of the slice: x: 4, y: 4 (y_hi: 2, y_lo: 2; y = y_hi * 2 + y_lo), z: 4, core: 2. Of those that a mesh axis runs over, the one named last changes fastest.
Arguments:
- boundary: bfloat16 [2, 65536, 512], P('section', 'dp'), may hold values from -6 to 6
- in_weights: bfloat16 [2, 512, 4096], P('section'), as said below
- down_weight: bfloat16 [2, 2048, 512], P('section'), may hold values from -0.25 to 0.25
- gains: bfloat16 [2, 2, 512], P('section'), may hold values from 0.5 to 1.5
- proj: bfloat16 [2, 512, 8], P('section'), as said below
- codebook: bfloat16 [8, 8192], P(None, ('section', 'dp')), may hold values from -4 to 4
- codes: int32 [65536], P('dp'), may hold values from 0 to 8191
- grids: int32 [128], P('dp'), may hold values from 0 to 2
- orders: int32 [128, 2], P('dp'), may hold values from 0 to 1, each once within a row
- avg_in: float32 [2, 512, 4096], P('section', 'dp'), may hold values from -0.3 to 0.3
- avg_down: float32 [2, 2048, 512], P('section', 'dp'), may hold values from -0.3 to 0.3
Outputs:
- boundary_out: bfloat16 [2, 65536, 512], P('section', 'dp')
- grad_in_weights: float32 [2, 512, 4096], P('section', 'dp')
- grad_down: float32 [2, 2048, 512], P('section', 'dp')
- grad_gains: float32 [2, 2, 512], P('section', None, 'dp')
- grad_proj: float32 [2, 512, 8], P('section', 'dp')
- grad_codebook: float32 [8, 8192], P(None, ('section', 'dp'))
- avg_in_new: float32 [2, 512, 4096], P('section', 'dp')
- avg_down_new: float32 [2, 2048, 512], P('section', 'dp')
Inputs may be any that keep to these rules, and one draw needn't show every extreme that they name: grids: 0, 1 and 2 name the grids of 16 x 16, 8 x 32 and 32 x 8 patches (rows x columns). in_weights: independent entries, fan-in scaled. proj: independent entries, fan-in scaled.
All inputs are finite; a program needn't handle non-finite values.
Results may differ from a plain program's by a relative error of at most 0.025.
Values may be sent and summed in bfloat16 or wider, within the bound.
A program may use at most 192 MiB of HBM per device.

v0:
```python
import jax
import jax.numpy as jnp
from jax import lax
from jax.sharding import PartitionSpec as P

HEADS = 8
HEAD = 64
WINDOW = 64
GRID = 256


MASKED_SCORE = -1e30
NORM_EPS = 1e-05
AVG_DECAY = 0.9
LEARN_RATE = 0.0005


def shifted(shard, axis, by):
    length = lax.axis_size(axis)
    pairs = [(i, i + by) for i in range(length) if 0 <= i + by < length]
    return lax.ppermute(shard, axis, pairs)


def layer_norm(values, gain):
    row_mean = jnp.mean(values, axis=-1, keepdims=True)
    centred = values - row_mean
    spread = jnp.mean(centred * centred, axis=-1, keepdims=True)
    return centred * lax.rsqrt(spread + NORM_EPS) * gain


def gelu_tanh(values):
    return jax.nn.gelu(values, approximate=True)


def contract(left, right, left_dim, right_dim):
    return lax.dot_general(
        left, right, (((left_dim,), (right_dim,)), ((), ())), preferred_element_type=jnp.float32
    )


def place_rows(store, new_rows, chosen, is_valid, clip_rows):
    old_rows = lax.dynamic_slice_in_dim(store, chosen * clip_rows, clip_rows, 0)
    return lax.dynamic_update_slice_in_dim(
        store, jnp.where(is_valid, new_rows, old_rows), chosen * clip_rows, 0
    )


def layout(is_first, grid_id, order_row, clip_rows, frame_count):
    row_ids = jnp.arange(clip_rows, dtype=jnp.int32)
    frame_no = row_ids // GRID
    cell_no = row_ids % GRID
    inner_no = row_ids % WINDOW
    group_no = row_ids // WINDOW
    window_no = cell_no // WINDOW
    width_cells = jnp.where(grid_id == 0, 16, jnp.where(grid_id == 1, 32, 8)).astype(jnp.int32)
    across = width_cells // 8
    enc_source = (
        frame_no * GRID
        + (window_no // across * 8 + inner_no // 8) * width_cells
        + window_no % across * 8
        + inner_no % 8
    )
    row_no = cell_no // width_cells
    col_no = cell_no % width_cells
    enc_target = (
        frame_no * GRID
        + (row_no // 8 * across + col_no // 8) * WINDOW
        + row_no % 8 * 8
        + col_no % 8
    )
    span_cells = WINDOW // frame_count
    dec_source = inner_no % frame_count * GRID + group_no * span_cells + inner_no // frame_count
    dec_target = cell_no // span_cells * WINDOW + cell_no % span_cells * frame_count + frame_no
    slot_no = jnp.arange(WINDOW, dtype=jnp.int32)
    frame_ids = jnp.arange(frame_count, dtype=jnp.int32)
    time_of = jnp.sum(
        jnp.where(frame_ids[None, :] == (slot_no % frame_count)[:, None], order_row[None, :], 0),
        axis=1,
    )
    allowed = (slot_no[:, None] // frame_count == slot_no[None, :] // frame_count) & (
        time_of[None, :] <= time_of[:, None]
    )
    source = jnp.where(is_first, enc_source, dec_source)
    target = jnp.where(is_first, enc_target, dec_target)
    return (source, target, allowed | is_first)


def block_forward(hidden, gain_pair, w_in, w_down, allowed):
    feature_dim = hidden.shape[1]
    groups = hidden.shape[0] // WINDOW
    score_scale = HEAD ** (-0.5)
    norm_one = layer_norm(hidden, gain_pair[0]).astype(jnp.bfloat16)
    packed = jnp.dot(
        norm_one, w_in[:, : 3 * feature_dim], preferred_element_type=jnp.float32
    ).astype(jnp.bfloat16)
    shaped = packed.reshape(groups, WINDOW, 3, HEADS, HEAD)
    queries = shaped[:, :, 0]
    keys_now = shaped[:, :, 1]
    values_now = shaped[:, :, 2]
    scores = (
        jnp.einsum("gqhd,gkhd->ghqk", queries, keys_now, preferred_element_type=jnp.float32)
        * score_scale
    )
    scores = jnp.where(allowed[None, None], scores, MASKED_SCORE)
    top_row = jnp.max(scores, axis=-1, keepdims=True)
    expo_rows = jnp.exp(scores - top_row)
    prob_rows = expo_rows / jnp.sum(expo_rows, axis=-1, keepdims=True)
    weights = prob_rows.astype(jnp.bfloat16)
    attended = jnp.einsum(
        "ghqk,gkhd->gqhd", weights, values_now, preferred_element_type=jnp.float32
    )
    attended = attended.reshape(-1, feature_dim).astype(jnp.bfloat16)
    mixed_rows = hidden + jnp.dot(
        attended, w_in[:, 3 * feature_dim : 4 * feature_dim], preferred_element_type=jnp.float32
    )
    norm_two = layer_norm(mixed_rows, gain_pair[1]).astype(jnp.bfloat16)
    up_proj = jnp.dot(norm_two, w_in[:, 4 * feature_dim :], preferred_element_type=jnp.float32)
    activated = gelu_tanh(up_proj).astype(jnp.bfloat16)
    result = mixed_rows + jnp.dot(activated, w_down, preferred_element_type=jnp.float32)
    saved_all = (
        hidden,
        norm_one,
        queries,
        keys_now,
        values_now,
        prob_rows,
        weights,
        attended,
        mixed_rows,
        norm_two,
        up_proj,
        activated,
    )
    return (result, saved_all)


def block_backward(saved_all, grad_out, gain_pair, w_in, w_down):
    (
        hidden,
        norm_one,
        queries,
        keys_now,
        values_now,
        prob_rows,
        weights,
        attended,
        mixed_rows,
        norm_two,
        up_proj,
        activated,
    ) = saved_all
    feature_dim = hidden.shape[1]
    rows_all = hidden.shape[0]
    score_scale = HEAD ** (-0.5)
    grad_z = grad_out.astype(jnp.bfloat16)
    grad_w_down = contract(activated, grad_z, 0, 0)
    grad_act = contract(grad_z, w_down, 1, 1)
    unused_value, gelu_pull = jax.vjp(gelu_tanh, up_proj)
    grad_up = gelu_pull(grad_act)[0].astype(jnp.bfloat16)
    grad_w_up = contract(norm_two, grad_up, 0, 0)
    grad_norm_two = contract(grad_up, w_in[:, 4 * feature_dim :], 1, 1)
    unused_norm, second_pull = jax.vjp(layer_norm, mixed_rows, gain_pair[1])
    grad_mixed_part, grad_gain_two = second_pull(grad_norm_two)
    grad_mixed = grad_out + grad_mixed_part
    grad_y = grad_mixed.astype(jnp.bfloat16)
    grad_w_out = contract(attended, grad_y, 0, 0)
    grad_att = (
        contract(grad_y, w_in[:, 3 * feature_dim : 4 * feature_dim], 1, 1)
        .astype(jnp.bfloat16)
        .reshape(queries.shape)
    )
    grad_prob = jnp.einsum(
        "gqhd,gkhd->ghqk", grad_att, values_now, preferred_element_type=jnp.float32
    )
    grad_values = jnp.einsum(
        "ghqk,gqhd->gkhd", weights, grad_att, preferred_element_type=jnp.float32
    )
    grad_scores = prob_rows * (grad_prob - jnp.sum(grad_prob * prob_rows, axis=-1, keepdims=True))
    grad_scores = grad_scores.astype(jnp.bfloat16)
    grad_queries = (
        jnp.einsum("ghqk,gkhd->gqhd", grad_scores, keys_now, preferred_element_type=jnp.float32)
        * score_scale
    )
    grad_keys = (
        jnp.einsum("ghqk,gqhd->gkhd", grad_scores, queries, preferred_element_type=jnp.float32)
        * score_scale
    )
    grad_packed = jnp.concatenate(
        [
            grad_queries.reshape(rows_all, feature_dim),
            grad_keys.reshape(rows_all, feature_dim),
            grad_values.reshape(rows_all, feature_dim),
        ],
        axis=1,
    ).astype(jnp.bfloat16)
    grad_w_qkv = contract(norm_one, grad_packed, 0, 0)
    grad_norm_one = contract(grad_packed, w_in[:, : 3 * feature_dim], 1, 1)
    unused_first, first_pull = jax.vjp(layer_norm, hidden, gain_pair[0])
    grad_hidden_part, grad_gain_one = first_pull(grad_norm_one)
    grad_hidden = grad_mixed + grad_hidden_part
    grad_w_in = jnp.concatenate([grad_w_qkv, grad_w_out, grad_w_up], axis=1)
    grad_gain = jnp.stack([grad_gain_one, grad_gain_two])
    return (grad_hidden, grad_w_in, grad_w_down, grad_gain)


def body(
    boundary, in_weights, down_weight, gains, proj, codebook, codes, grids, orders, avg_in, avg_down
):
    section_id = lax.axis_index("section")
    is_first = section_id == 0
    count_micro = grids.shape[0]
    clip_rows = codes.shape[0] // count_micro
    frame_count = orders.shape[1]
    feature_dim = in_weights.shape[1]
    w_in = in_weights[0]
    w_down = down_weight[0]
    gain_pair = gains[0].astype(jnp.float32)
    proj_w = proj[0]
    code_dim = proj_w.shape[1]
    book_half = lax.all_gather(codebook, "dp", axis=1, tiled=True)
    half_codes = book_half.shape[1]
    local_rows = boundary[0]

    def prepare(chosen):
        codes_now = lax.dynamic_slice_in_dim(codes, chosen * clip_rows, clip_rows, 0)
        grid_now = lax.dynamic_index_in_dim(grids, chosen, 0, keepdims=False)
        order_now = lax.dynamic_index_in_dim(orders, chosen, 0, keepdims=False)
        source, target, allowed = layout(is_first, grid_now, order_now, clip_rows, frame_count)
        code_ids = lax.broadcasted_iota(jnp.int32, (half_codes, clip_rows), 0)
        onehot = (code_ids == (codes_now - section_id * half_codes)[None, :]).astype(jnp.bfloat16)
        entry = jnp.dot(book_half, onehot, preferred_element_type=jnp.float32)
        return (source, target, allowed, onehot, entry)

    arriving = jnp.zeros((code_dim, clip_rows), jnp.bfloat16)
    kept_inputs = []
    kept_codes = []
    produced = jnp.zeros((count_micro * clip_rows, feature_dim), jnp.float32)
    for section_step in range(count_micro + 1):
        step_micro = section_step - section_id
        is_valid = (step_micro >= 0) & (step_micro < count_micro)
        chosen = jnp.clip(step_micro, 0, count_micro - 1)
        source, target, allowed, onehot, entry = prepare(chosen)
        patch_rows = lax.dynamic_slice_in_dim(local_rows, chosen * clip_rows, clip_rows, 0).astype(
            jnp.float32
        )
        quantized = (arriving.astype(jnp.float32) + entry).astype(jnp.bfloat16)
        dec_start = contract(quantized, proj_w, 0, 1)
        block_in = jnp.where(is_first, patch_rows, dec_start)
        grouped, unused_saved = block_forward(
            jnp.take(block_in, source, axis=0), gain_pair, w_in, w_down, allowed
        )
        block_out = jnp.take(grouped, target, axis=0)
        code_vec = contract(proj_w, block_out.astype(jnp.bfloat16), 0, 1)
        outgoing = (code_vec + entry).astype(jnp.bfloat16)
        kept_inputs.append(block_in)
        kept_codes.append(arriving)
        produced = place_rows(produced, block_out, chosen, is_valid, clip_rows)
        if section_step < count_micro:
            arriving = shifted(outgoing, "section", 1)
    inputs_all = jnp.stack(kept_inputs)
    codes_all = jnp.stack(kept_codes)
    returning = jnp.zeros((code_dim, clip_rows), jnp.bfloat16)
    patch_grads = jnp.zeros((count_micro * clip_rows, feature_dim), jnp.float32)
    totals = None
    for section_step in range(count_micro + 1):
        step_micro = count_micro - section_step - section_id
        is_valid = (step_micro >= 0) & (step_micro < count_micro)
        chosen = jnp.clip(step_micro, 0, count_micro - 1)
        source, target, allowed, onehot, entry = prepare(chosen)
        forward_step = chosen + section_id
        block_in = lax.dynamic_index_in_dim(inputs_all, forward_step, 0, keepdims=False)
        arrived = lax.dynamic_index_in_dim(codes_all, forward_step, 0, keepdims=False)
        quantized = (arrived.astype(jnp.float32) + entry).astype(jnp.bfloat16)
        grouped, saved_all = block_forward(
            jnp.take(block_in, source, axis=0), gain_pair, w_in, w_down, allowed
        )
        block_out = jnp.take(grouped, target, axis=0)
        cotangent = lax.dynamic_slice_in_dim(local_rows, chosen * clip_rows, clip_rows, 0).astype(
            jnp.float32
        )
        from_codes = contract(returning, proj_w, 0, 1)
        grad_out = jnp.where(is_first, from_codes, cotangent)
        grad_group, grad_w_in, grad_w_down, grad_gain = block_backward(
            saved_all, jnp.take(grad_out, source, axis=0), gain_pair, w_in, w_down
        )
        grad_block = jnp.take(grad_group, target, axis=0)
        grad_start = grad_block.astype(jnp.bfloat16)
        grad_quant = contract(proj_w, grad_start, 0, 1).astype(jnp.bfloat16)
        code_grad = jnp.where(is_first, returning, grad_quant)
        grad_book = contract(code_grad, onehot, 1, 1)
        grad_proj = jnp.where(
            is_first,
            contract(block_out.astype(jnp.bfloat16), returning, 0, 1),
            contract(grad_start, quantized, 0, 1),
        )
        weight_on = is_valid.astype(jnp.float32)
        terms = (
            grad_w_in[None] * weight_on,
            grad_w_down[None] * weight_on,
            grad_proj[None] * weight_on,
            grad_gain[None] * weight_on,
            grad_book * weight_on,
        )
        patch_grads = place_rows(patch_grads, grad_block, chosen, is_valid, clip_rows)
        totals = terms if totals is None else jax.tree.map(jnp.add, totals, terms)
        if section_step < count_micro:
            returning = shifted(grad_quant, "section", -1)
    totals = (
        lax.psum_scatter(totals[0], "dp", scatter_dimension=1, tiled=True),
        lax.psum_scatter(totals[1], "dp", scatter_dimension=1, tiled=True),
        lax.psum_scatter(totals[2], "dp", scatter_dimension=1, tiled=True),
        lax.psum_scatter(totals[3], "dp", scatter_dimension=2, tiled=True),
        lax.psum_scatter(totals[4], "dp", scatter_dimension=1, tiled=True),
    )
    grad_in_share, grad_down_share, grad_proj_share, grad_gain_share, grad_book_share = totals
    boundary_out = jnp.where(is_first, patch_grads, produced).astype(jnp.bfloat16)[None]
    dp_index = lax.axis_index("dp")
    rows_in = avg_in.shape[1]
    piece_in = lax.dynamic_slice_in_dim(in_weights, dp_index * rows_in, rows_in, 1).astype(
        jnp.float32
    )
    avg_in_new = AVG_DECAY * avg_in + (1.0 - AVG_DECAY) * (piece_in - LEARN_RATE * grad_in_share)
    rows_down = avg_down.shape[1]
    piece_down = lax.dynamic_slice_in_dim(down_weight, dp_index * rows_down, rows_down, 1).astype(
        jnp.float32
    )
    avg_down_new = AVG_DECAY * avg_down + (1.0 - AVG_DECAY) * (
        piece_down - LEARN_RATE * grad_down_share
    )
    return (
        boundary_out,
        grad_in_share,
        grad_down_share,
        grad_gain_share,
        grad_proj_share,
        grad_book_share,
        avg_in_new,
        avg_down_new,
    )


def solution(mesh):
    placed = (
        P("section", "dp", None),
        P("section", None, None),
        P("section", None, None),
        P("section", None, None),
        P("section", None, None),
        P(None, ("section", "dp")),
        P("dp"),
        P("dp"),
        P("dp", None),
        P("section", "dp", None),
        P("section", "dp", None),
    )
    return jax.shard_map(
        body,
        mesh=mesh,
        in_specs=placed,
        out_specs=(
            P("section", "dp", None),
            P("section", "dp", None),
            P("section", "dp", None),
            P("section", None, "dp"),
            P("section", "dp", None),
            P(None, ("section", "dp")),
            P("section", "dp", None),
            P("section", "dp", None),
        ),
        check_vma=False,
    )
```

profile of v0, /device:TPU:1, one launch (start us, length us, event | category | flops | bytes accessed | tf_op | source)
XLA Modules:
  0.0 1534.6 jit_solution(6517028321326505273)
XLA Ops:
  11.9 98.9 %all-gather = bf16[64,64,8]{1,2,0:T(8,128)(2,1)S(1)} all-gather(bf16[1,64,8]{1,2,0:T(8,128)(2,1)} %bitcast.532), channel_id=1, replica_groups=mesh['section'=2,'dp'=64] {'dp'}, dimensions={0}, use_global_device_ids=true | all-gather | bytes 66560 | tf_op jit(solution)/shard_map/all_gather | solution.py:220
  121.8 5.1 reshape.895
  133.1 4.0 fusion.493
  148.3 5.9 fusion.127
  178.1 5.1 reshape.896
  204.8 6.7 fusion.132
  237.3 5.1 reshape.897
  306.6 5.4 reshape.902
  321.8 5.1 reshape.907
  388.6 5.2 fusion.275
  403.2 6.3 fusion.32
  465.2 6.3 fusion.39
  523.0 9.2 add_bitcast_fusion
  534.8 4.2 convolution_bitcast_fusion.5
  557.6 13.3 fusion.7
  576.5 4.9 fusion.142
  589.3 5.0 reshape.912
  599.3 4.2 fusion.499
  611.8 6.2 fusion.137
  621.9 4.8 fusion.145
  629.6 4.8 fusion.148
  640.5 316.8 %all-reduce.2 = (f32[1,2,512]{2,1,0:T(2,128)S(1)}, f32[1,512,8]{1,2,0:T(8,128)S(1)}) all-reduce(f32[1,2,512]{2,1,0:T(2,128)S(1)} %fusion.345, f32[1,512,8]{1,2,0:T(8,128)S(1)} %fusion.156), channel_id=4, replica_groups=mesh['section'=2,'dp'=64] {'dp'}, use_global_device_ids=true, to_apply=%region_62.64.clone | all-reduce | flops 5120 | bytes 40960
  961.4 220.9 %reduce-scatter.10.cloned.1.call-done = f32[1,32,512]{2,1,0:T(8,128)} async-done(((f32[1,2048,512]{2,1,0:T(8,128)}), f32[1,32,512]{2,1,0:T(8,128)}) %reduce-scatter.10.cloned.1.call-update) | async-done | bytes 65552 | tf_op jit(solution)/shard_map/reduce_scatter | solution.py:310
  1183.8 342.5 %reduce-scatter.8.cloned.1.call-done = f32[1,8,4096]{2,1,0:T(8,128)} async-done(((f32[1,512,4096]{2,1,0:T(8,128)}), f32[1,8,4096]{2,1,0:T(8,128)}) %reduce-scatter.8.cloned.1.call-update) | async-done | bytes 131088 | tf_op jit(solution)/shard_map/reduce_scatter | solution.py:309
  (538 shorter events, 418.4 us)
Async XLA Ops:
  7.2 106.1 %copy-start = (bf16[1,512,8]{1,2,0:T(8,128)(2,1)S(1)}, bf16[1,512,8]{1,2,0:T(8,128)(2,1)}, u32[]{:S(2)}) copy-start(bf16[1,512,8]{1,2,0:T(8,128)(2,1)} %param.17) | copy-start | bytes 24580
  7.2 106.1 %copy-start.34 = (bf16[1,1024,512]{2,1,0:T(8,128)(2,1)S(1)}, bf16[1,1024,512]{2,1,0:T(8,128)(2,1)}, u32[]{:S(2)}) copy-start(bf16[1,1024,512]{2,1,0:T(8,128)(2,1)} %param.13) | copy-start | bytes 3145732
  7.2 952.8 %reduce-scatter.12.cloned.1.call-start = ((), (), s32[]{:S(2)}) async-start(), calls=%async_computation.5 | async-start | bytes 2129920
  10.9 145.6 %copy-start.108 = (pred[512]{0:T(512)(128)(4,1)}, pred[512]{0:T(512)(128)(4,1)S(1)}, u32[]{:S(2)}) copy-start(pred[512]{0:T(512)(128)(4,1)S(1)} %get-tuple-element.73) | copy-start | bytes 1540
  10.9 143.5 %copy-start.97 = (s32[1024]{0:T(1024)}, s32[1024]{0:T(1024)S(1)}, u32[]{:S(2)}) copy-start(s32[1024]{0:T(1024)S(1)} %pad_clamp_fusion.3) | copy-start | bytes 12292
  111.9 51.3 %copy-start.112 = (s32[512]{0:T(512)}, s32[512]{0:T(512)S(1)}, u32[]{:S(2)}) copy-start(s32[512]{0:T(512)S(1)} %get-tuple-element.100) | copy-start | bytes 6148
  113.3 43.2 %copy-start.99 = (f32[8,512]{1,0:T(8,128)}, f32[8,512]{1,0:T(8,128)S(1)}, u32[]{:S(2)}) copy-start(f32[8,512]{1,0:T(8,128)S(1)} %fusion.151) | copy-start | bytes 49156
  133.1 115.3 %copy-start.106 = (pred[64,64]{0,1:T(8,128)(4,1)}, pred[64,64]{0,1:T(8,128)(4,1)S(1)}, u32[]{:S(2)}) copy-start(pred[64,64]{0,1:T(8,128)(4,1)S(1)} %get-tuple-element.108) | copy-start | bytes 12292
  156.8 9.3 collective-permute-start
  162.8 224.0 %copy-start.115 = (pred[512]{0:T(512)(128)(4,1)}, pred[512]{0:T(512)(128)(4,1)S(1)}, u32[]{:S(2)}) copy-start(pred[512]{0:T(512)(128)(4,1)S(1)} %get-tuple-element.63) | copy-start | bytes 1540
  164.6 52.7 %copy-start.101 = (f32[8,512]{1,0:T(8,128)}, f32[8,512]{1,0:T(8,128)S(1)}, u32[]{:S(2)}) copy-start(f32[8,512]{1,0:T(8,128)S(1)} %fusion.152) | copy-start | bytes 49156
  166.0 59.1 %copy-start.103 = (f32[8,512]{1,0:T(8,128)}, f32[8,512]{1,0:T(8,128)S(1)}, u32[]{:S(2)}) copy-start(f32[8,512]{1,0:T(8,128)S(1)} %fusion.153) | copy-start | bytes 49156
  218.7 6.4 collective-permute-start.1
  262.6 12.5 copy-start.4
  300.0 60.4 %copy-start.1 = (f32[512,512]{0,1:T(8,128)}, f32[512,512]{0,1:T(8,128)S(1)}, u32[]{:S(2)}) copy-start(f32[512,512]{0,1:T(8,128)S(1)} %copy.330) | copy-start | bytes 3145732
  363.3 10.6 copy-start.41
  387.1 11.6 collective-permute-start.2
  403.2 12.4 copy-start.26
  456.2 4.5 collective-permute-start.3
  465.1 47.8 %copy-start.24 = (f32[512,512]{0,1:T(8,128)}, f32[512,512]{0,1:T(8,128)S(1)}, u32[]{:S(2)}) copy-start(f32[512,512]{0,1:T(8,128)S(1)} %copy.350) | copy-start | bytes 3145732
  522.9 659.4 %reduce-scatter.10.cloned.1.call-start = ((), (), s32[]{:S(2)}) async-start(), calls=%async_computation.4 | async-start | bytes 4259840 | tf_op jit(solution)/shard_map/reduce_scatter | solution.py:310
  532.1 994.1 %reduce-scatter.8.cloned.1.call-start = ((), (), s32[]{:S(2)}) async-start(), calls=%async_computation.3 | async-start | bytes 8519680 | tf_op jit(solution)/shard_map/reduce_scatter | solution.py:309
  639.9 542.4 %copy-start.92 = (f32[1,32,512]{2,1,0:T(8,128)S(1)}, f32[1,32,512]{2,1,0:T(8,128)}, u32[]{:S(2)}) copy-start(f32[1,32,512]{2,1,0:T(8,128)} %param.23) | copy-start | bytes 196612
  640.2 886.0 %copy-start.91 = (f32[1,8,4096]{2,1,0:T(8,128)S(1)}, f32[1,8,4096]{2,1,0:T(8,128)}, u32[]{:S(2)}) copy-start(f32[1,8,4096]{2,1,0:T(8,128)} %param.22) | copy-start | bytes 393220
  (104 other events, 325.7 us)
Sparse Core Ops, SparseCore 0:
  523.0 322.7 reduce-scatter.11
  848.9 333.3 reduce-scatter.9
  1185.2 340.9 reduce-scatter.7
where the time goes:
time: 1550 us; the launch traced here: 1530 us
  waiting for transfers between devices  564 us (36%)
  blocking collectives  416 us (27%)
  local copies, waits for them, and re-layouts  255 us (16%)
  matrix products  234 us (15%)
  other arithmetic  37.9 us (2%)
  between operations  20.4 us (1%)
    reduce_scatter x1, waiting for transfers between devices, body(): lax.psum_scatter(totals[0], 'dp', scatter_dimension=1, tiled=True)  342 us
    unnamed x1, blocking collectives  317 us
    reduce_scatter x1, waiting for transfers between devices, body(): lax.psum_scatter(totals[1], 'dp', scatter_dimension=1, tiled=True)  221 us
    all_gather x1, blocking collectives, body(): book_half = lax.all_gather(codebook, 'dp', axis=1, tiled=True)  98.9 us
    dot_general x43, matrix products, contract(): lax.dot_general(left, right, (((left_dim,), (right_dim,)), ((), ())), pre...  88.4 us
    unnamed x261, local copies, waits for them, and re-layouts  40.6 us
    dot_general x6, matrix products, block_forward(): jnp.dot(activated, w_down, preferred_element_type=jnp.float32)  33.3 us
  transfers between devices with their start and end apart: 7, of which 3 were waited for; matrix products, arithmetic and copies ran while one was open for 9% of the time, Pallas kernels for 0%

commit v1 on v0

v1 whole, which is shorter than its diff:
```python
import functools

import jax
import jax.numpy as jnp
from jax import lax
from jax.experimental import pallas as pl
from jax.experimental.pallas import tpu as pltpu
from jax.sharding import PartitionSpec as P

BF = jnp.bfloat16
F32 = jnp.float32
I32 = jnp.int32
MESH = pl.DeviceIdType.MESH

D = 512
FF = 2048
CLIP = 512
GRID = 256
WINDOW = 64
HALF = 4096
NORM_EPS = 1e-05
AVG_DECAY = 0.9
LEARN_RATE = 0.0005
SCALE = 0.125
RC = 256

CHUNKS = {"a": (128, 256), "b": (32, 1024), "c": (32, 1024)}


def nn(left, right):
    return lax.dot_general(left, right, (((1,), (0,)), ((), ())), preferred_element_type=F32)


def nt(left, right):
    return lax.dot_general(left, right, (((1,), (1,)), ((), ())), preferred_element_type=F32)


def tn(left, right):
    return lax.dot_general(left, right, (((0,), (0,)), ((), ())), preferred_element_type=F32)


def tt(left, right):
    return lax.dot_general(left, right, (((0,), (1,)), ((), ())), preferred_element_type=F32)


def iota(shape, axis):
    return lax.broadcasted_iota(I32, shape, axis)


def normed(h):
    mean = jnp.mean(h, axis=-1, keepdims=True)
    c = h - mean
    var = jnp.mean(c * c, axis=-1, keepdims=True)
    r = lax.rsqrt(var + NORM_EPS)
    return c * r, r


def normed_back(grad, xhat, r, gain):
    t = grad * gain
    m1 = jnp.mean(t, axis=-1, keepdims=True)
    m2 = jnp.mean(t * xhat, axis=-1, keepdims=True)
    return r * (t - m1 - xhat * m2)


def gelu_pair(u):
    c0 = 0.7978845608028654
    c1 = 0.7978845608028654 * 0.044715
    u2 = u * u
    t = jnp.tanh(u * (c0 + c1 * u2))
    hu = 0.5 * u
    ht = 0.5 + 0.5 * t
    value = hu + hu * t
    slope = ht + hu * (1.0 - t * t) * (c0 + (3.0 * c1) * u2)
    return value, slope


def ten_shapes():
    shapes = {
        "xs": ((2, CLIP, D), BF),
        "win": ((D, 4 * D + FF), BF),
        "wdn": ((FF, D), BF),
        "perm": ((2, GRID, GRID), BF),
        "bd1": ((256, 256), BF),
        "bds": ((256, 256), BF),
        "bdf": ((256, 256), F32),
        "tbl": ((64, 8, 128), F32),
        "cds": ((2, 8, CLIP), I32),
        "cxs": ((2, 16, CLIP), BF),
        "cxr": ((2, 16, CLIP), BF),
        "ent": ((2, 8, CLIP), F32),
        "cvec": ((2, 16, CLIP), BF),
        "hb": ((CLIP, D), F32),
        "gg": ((CLIP, D), F32),
        "gob": ((CLIP, D), BF),
        "xh1": ((2, CLIP, D), F32),
        "xh2": ((2, CLIP, D), F32),
        "r1": ((2, CLIP, 1), F32),
        "r2": ((2, CLIP, 1), F32),
        "a1": ((2, CLIP, D), BF),
        "a2": ((2, CLIP, D), BF),
        "qkv": ((2, CLIP, 3 * D), BF),
        "prob": ((2, CLIP, D), F32),
        "att": ((2, CLIP, D), BF),
        "act": ((2, CLIP, FF), BF),
        "gel": ((2, CLIP, FF), BF),
        "gy": ((2, CLIP, D), BF),
        "eb": ((2, CLIP, D), BF),
        "acc_dn": ((FF, D), F32),
        "acc_up": ((D, FF), F32),
        "acc_qkv": ((D, 3 * D), F32),
        "acc_out": ((D, D), F32),
        "s_acc": ((4, 8, 2, 8, 128), F32),
        "gacc": ((2, 8, D), F32),
        "s0": ((4, 8, 8, 128), F32),
        "s1": ((3, 8, 8, 128), F32),
        "s2": ((3, 2, 8, 128), F32),
        "s3": ((8, 128), F32),
    }
    for k, (rows, w) in CHUNKS.items():
        h = w // 2
        shapes["sb0" + k] = ((4, 4, rows, w), BF)
        shapes["r0" + k] = ((4, 4, rows, w), BF)
        shapes["r1z" + k] = ((3, 4, rows, h), BF)
        shapes["r1x" + k] = ((3, 4, rows, h), BF)
        shapes["r2a" + k] = ((3, rows, h), BF)
        shapes["r2b" + k] = ((3, rows, h), BF)
        shapes["t3" + k] = ((rows, w), F32)
        shapes["sb3" + k] = ((rows // 2, w), BF)
        shapes["r3" + k] = ((rows // 2, w), BF)
        shapes["t4" + k] = ((rows // 2, w), F32)
        shapes["r4" + k] = ((rows // 4, w), F32)
    return shapes


SHAPES = ten_shapes()
N_SEM = 80


class Refs:
    pass


def mega(
    x_hbm, win_hbm, wdn_hbm, gains_ref, proj_ref, book_ref, codes_ref, grids_ref, orders_ref,
    avgin_ref, avgdn_ref,
    bout_ref, gin_ref, gdn_ref, ggain_ref, gproj_ref, gbook_ref, ain_ref, adn_ref,
    *scratch,
):
    s = Refs()
    for name, ref in zip(SHAPES, scratch):
        setattr(s, name, ref)
    send_sems, recv_sems, load_sems = scratch[len(SHAPES):]

    sec = lax.axis_index("section")
    dp = lax.axis_index("dp")
    core = dp % 2
    yh = (dp // 2) % 2
    x = (dp // 4) % 4
    z = dp // 16
    is_e = sec == 0
    is_d = sec == 1

    def place(zz, xx, yy, cc):
        return (sec, ((zz * 4 + xx) * 2 + yy) * 2 + cc)

    core_dev = place(z, x, yh, 1 - core)
    y_dev = place(z, x, 1 - yh, core)
    z_dev = [place((z + d) % 4, x, yh, core) for d in (1, 2, 3)]
    x_dev = [place(z, (x + d) % 4, yh, core) for d in (1, 2, 3)]
    sec_dev = (1 - sec, dp)

    counter = [0]
    slots = {}

    def rcopy(key, src, dst, dev):
        if key not in slots:
            slots[key] = counter[0]
            counter[0] += 1
        i = slots[key]
        return pltpu.make_async_remote_copy(
            src_ref=src, dst_ref=dst, send_sem=send_sems.at[i], recv_sem=recv_sems.at[i],
            device_id=dev, device_id_type=MESH,
        )

    loads = [
        pltpu.make_async_copy(x_hbm.at[0, pl.ds(0, CLIP)], s.xs.at[0], load_sems.at[0]),
        pltpu.make_async_copy(x_hbm.at[0, pl.ds(CLIP, CLIP)], s.xs.at[1], load_sems.at[1]),
        pltpu.make_async_copy(win_hbm.at[0], s.win, load_sems.at[2]),
        pltpu.make_async_copy(wdn_hbm.at[0], s.wdn, load_sems.at[3]),
    ]
    for load in loads:
        load.start()

    barrier = pltpu.get_barrier_semaphore()
    peers = [core_dev, y_dev, sec_dev] + z_dev + x_dev
    for dev in peers:
        pl.semaphore_signal(barrier, inc=1, device_id=dev, device_id_type=MESH)

    rows_i = iota((256, 256), 0)
    cols_i = iota((256, 256), 1)
    same = ((rows_i >> 6) == (cols_i >> 6)).astype(F32)
    s.bdf[...] = same * SCALE
    s.bd1[...] = same.astype(BF)
    s.bds[...] = (same * SCALE).astype(BF)
    for c in range(2):
        code_row = jnp.concatenate([codes_ref[4 * c + k : 4 * c + k + 1, :] for k in range(4)], axis=1)
        s.cds[c] = jnp.broadcast_to(code_row - sec * HALF, (8, CLIP))

    gain_one = gains_ref[0, 0:1, :].astype(F32)
    gain_two = gains_ref[0, 1:2, :].astype(F32)
    book = book_ref[...].astype(F32)
    s.tbl[dp] = jnp.concatenate([book, jnp.zeros((8, 64), F32)], axis=1)
    s.gacc[...] = jnp.zeros((2, 8, D), F32)
    s.s_acc[...] = jnp.zeros((4, 8, 2, 8, 128), F32)

    pl.semaphore_wait(barrier, len(peers))

    def ag_copies(step):
        if step == 0:
            part = s.tbl.at[dp]
            return [rcopy("ag0", part, part, core_dev)]
        if step == 1:
            part = s.tbl.at[pl.ds((dp // 2) * 2, 2)]
            return [rcopy("ag1", part, part, y_dev)]
        if step == 2:
            part = s.tbl.at[pl.ds((dp // 4) * 4, 4)]
            return [rcopy("ag2%d" % i, part, part, x_dev[i]) for i in range(3)]
        part = s.tbl.at[pl.ds((dp // 16) * 16, 16)]
        return [rcopy("ag3%d" % i, part, part, z_dev[i]) for i in range(3)]

    def ag_arrivals(step):
        if step == 0:
            part = s.tbl.at[dp + 1 - 2 * core]
            return [rcopy("ag0", part, part, core_dev)]
        if step == 1:
            part = s.tbl.at[pl.ds((dp // 4) * 4 + (1 - yh) * 2, 2)]
            return [rcopy("ag1", part, part, y_dev)]
        if step == 2:
            parts = [s.tbl.at[pl.ds(z * 16 + ((x + 3 - i) % 4) * 4, 4)] for i in range(3)]
            return [rcopy("ag2%d" % i, parts[i], parts[i], x_dev[i]) for i in range(3)]
        parts = [s.tbl.at[pl.ds(((z + 3 - i) % 4) * 16, 16)] for i in range(3)]
        return [rcopy("ag3%d" % i, parts[i], parts[i], z_dev[i]) for i in range(3)]

    def ag_start(step):
        for cp in ag_copies(step):
            cp.start()

    def ag_wait(step):
        for cp in ag_arrivals(step):
            cp.wait_recv()
        for cp in ag_copies(step):
            cp.wait_send()

    def onehots(c):
        code_row = s.cds[c][0:1, :]
        hi = code_row >> 6
        lo = code_row & 63
        lo_one = (iota((128, CLIP), 0) == lo).astype(F32).astype(BF)
        hi_mask = (iota((CLIP, CLIP), 0) >> 3) == hi
        return lo_one, hi_mask

    def entries(c):
        lo_one, hi_mask = onehots(c)
        table = s.tbl[...].reshape(CLIP, 128).astype(BF)
        picked = jnp.where(hi_mask, nn(table, lo_one), 0.0)
        s.ent[c] = jnp.sum(picked.reshape(64, 8, CLIP), axis=0)

    def pad16(v):
        return jnp.concatenate([v, jnp.zeros((8, v.shape[1]), F32)], axis=0).astype(BF)

    def book_proj_terms(c, code_grad, wide_rows, narrow):
        lo_one, hi_mask = onehots(c)
        spread = jnp.broadcast_to(code_grad[None], (64, 8, CLIP)).reshape(CLIP, CLIP)
        left = jnp.where(hi_mask, spread, 0.0).astype(BF)
        total = nt(left, lo_one)
        narrow_wide = jnp.concatenate(
            [jnp.zeros((64, CLIP), F32), narrow, jnp.zeros((56, CLIP), F32)], axis=0
        ).astype(BF)
        total = total + tt(wide_rows, narrow_wide)
        s.s_acc[...] += total.reshape(4, 8, 2, 8, 128)

    def norm_qkv(c, rows, h):
        s.hb[rows] = h
        xh, r = normed(h)
        s.xh1[c, rows] = xh
        s.r1[c, rows] = r
        a = (xh * gain_one).astype(BF)
        s.a1[c, rows] = a
        for j in range(3):
            s.qkv[c, rows, 512 * j : 512 * j + 512] = nn(a, s.win[:, 512 * j : 512 * j + 512]).astype(BF)

    def feed_forward(c, put):
        def step(i, carry):
            rows = pl.ds(i * RC, RC)
            m = s.hb[rows] + nn(s.att[c, rows], s.win[:, 1536:2048])
            xh, r = normed(m)
            s.xh2[c, rows] = xh
            s.r2[c, rows] = r
            a = (xh * gain_two).astype(BF)
            s.a2[c, rows] = a
            acc = m
            for j in range(4):
                cols = slice(512 * j, 512 * j + 512)
                u = nn(a, s.win[:, 2048 + 512 * j : 2560 + 512 * j])
                value, slope = gelu_pair(u)
                value = value.astype(BF)
                s.act[c, rows, cols] = value
                s.gel[c, rows, cols] = slope.astype(BF)
                acc = acc + nn(value, s.wdn[cols, :])
            put(rows, acc)
            return carry

        lax.fori_loop(0, CLIP // RC, step, 0)

    def window_forward(c):
        def step(w, carry):
            rows = pl.ds(w * WINDOW, WINDOW)
            for quad in range(2):
                cols = slice(256 * quad, 256 * quad + 256)
                q4 = s.qkv[c, rows, 256 * quad : 256 * quad + 256]
                k4 = s.qkv[c, rows, 512 + 256 * quad : 768 + 256 * quad]
                v4 = s.qkv[c, rows, 1024 + 256 * quad : 1280 + 256 * quad]
                q_wide = jnp.concatenate([q4] * 4, axis=0) * s.bds[...]
                scores = nt(k4, q_wide)
                top = jnp.max(scores, axis=0, keepdims=True)
                e = jnp.exp(scores - top)
                p = e * (1.0 / jnp.sum(e, axis=0, keepdims=True))
                s.prob[c, rows, cols] = p
                wide = tn(p.astype(BF), v4) * s.bdf[...]
                out = (wide[0:64] + wide[64:128]) + (wide[128:192] + wide[192:256])
                s.att[c, rows, cols] = (out * (1.0 / SCALE)).astype(BF)
            return carry

        lax.fori_loop(0, CLIP // WINDOW, step, 0)

    def window_backward(c):
        def step(w, carry):
            rows = pl.ds(w * WINDOW, WINDOW)
            for quad in range(2):
                cols = slice(256 * quad, 256 * quad + 256)
                qc = slice(256 * quad, 256 * quad + 256)
                kc = slice(512 + 256 * quad, 768 + 256 * quad)
                vc = slice(1024 + 256 * quad, 1280 + 256 * quad)
                q4 = s.qkv[c, rows, qc]
                k4 = s.qkv[c, rows, kc]
                v4 = s.qkv[c, rows, vc]
                go = s.gob[rows, cols]
                p = s.prob[c, rows, cols]
                go_wide = jnp.concatenate([go] * 4, axis=0) * s.bd1[...]
                q_wide = jnp.concatenate([q4] * 4, axis=0) * s.bds[...]
                gp = nt(v4, go_wide)
                gs = (p * (gp - jnp.sum(gp * p, axis=0, keepdims=True))).astype(BF)
                s.qkv[c, rows, vc] = nn(p.astype(BF), go_wide).astype(BF)
                s.qkv[c, rows, kc] = nn(gs, q_wide).astype(BF)
                wide = tn(gs, k4) * s.bdf[...]
                out = (wide[0:64] + wide[64:128]) + (wide[128:192] + wide[192:256])
                s.qkv[c, rows, qc] = out.astype(BF)
            return carry

        lax.fori_loop(0, CLIP // WINDOW, step, 0)

    def head_sums(v):
        hi = v.astype(BF)
        lo = (v - hi.astype(F32)).astype(BF)
        return nn(hi, s.bd1[...]) + nn(lo, s.bd1[...])

    CR = 128

    def frames_forward(c):
        late0 = orders_ref[c, 0] > orders_ref[c, 1]
        sign = jnp.where(late0, 1.0, -1.0).astype(F32)

        def step(i, carry):
            r0 = pl.ds(i * CR, CR)
            r1 = pl.ds(GRID + i * CR, CR)
            for quad in range(2):
                qc = slice(256 * quad, 256 * quad + 256)
                kc = slice(512 + 256 * quad, 768 + 256 * quad)
                vc = slice(1024 + 256 * quad, 1280 + 256 * quad)
                q_late = jnp.where(late0, s.qkv[c, r0, qc].astype(F32), s.qkv[c, r1, qc].astype(F32))
                k_diff = sign * (s.qkv[c, r1, kc].astype(F32) - s.qkv[c, r0, kc].astype(F32))
                v0 = s.qkv[c, r0, vc].astype(F32)
                v1 = s.qkv[c, r1, vc].astype(F32)
                d = head_sums(q_late * k_diff) * SCALE
                e = jnp.exp(-jnp.abs(d))
                big = 1.0 / (1.0 + e)
                small = e * big
                p_other = jnp.where(d > 0.0, big, small)
                p_self = jnp.where(d > 0.0, small, big)
                s.prob[c, r0, qc] = p_other
                s.prob[c, r1, qc] = p_self
                po = p_other.astype(BF).astype(F32)
                ps = p_self.astype(BF).astype(F32)
                v_late = jnp.where(late0, v0, v1)
                v_early = jnp.where(late0, v1, v0)
                mix = ps * v_late + po * v_early
                s.att[c, r0, qc] = jnp.where(late0, mix, v0).astype(BF)
                s.att[c, r1, qc] = jnp.where(late0, v1, mix).astype(BF)
            return carry

        lax.fori_loop(0, GRID // CR, step, 0)

    def frames_backward(c):
        late0 = orders_ref[c, 0] > orders_ref[c, 1]
        sign = jnp.where(late0, 1.0, -1.0).astype(F32)

        def step(i, carry):
            r0 = pl.ds(i * CR, CR)
            r1 = pl.ds(GRID + i * CR, CR)
            for quad in range(2):
                qc = slice(256 * quad, 256 * quad + 256)
                kc = slice(512 + 256 * quad, 768 + 256 * quad)
                vc = slice(1024 + 256 * quad, 1280 + 256 * quad)
                q_late = jnp.where(late0, s.qkv[c, r0, qc].astype(F32), s.qkv[c, r1, qc].astype(F32))
                k_diff = sign * (s.qkv[c, r1, kc].astype(F32) - s.qkv[c, r0, kc].astype(F32))
                v_diff = sign * (s.qkv[c, r1, vc].astype(F32) - s.qkv[c, r0, vc].astype(F32))
                go0 = s.gob[r0, qc].astype(F32)
                go1 = s.gob[r1, qc].astype(F32)
                go_late = jnp.where(late0, go0, go1)
                go_early = jnp.where(late0, go1, go0)
                p_other = s.prob[c, r0, qc]
                p_self = s.prob[c, r1, qc]
                gs = p_other * p_self * head_sums(go_late * v_diff)
                gs = gs.astype(BF).astype(F32) * SCALE
                gq = gs * k_diff
                gk = gs * q_late
                gv_late = p_self.astype(BF).astype(F32) * go_late
                gv_early = go_early + p_other.astype(BF).astype(F32) * go_late
                s.qkv[c, r0, qc] = jnp.where(late0, gq, 0.0).astype(BF)
                s.qkv[c, r1, qc] = jnp.where(late0, 0.0, gq).astype(BF)
                s.qkv[c, r0, kc] = (-sign * gk).astype(BF)
                s.qkv[c, r1, kc] = (sign * gk).astype(BF)
                s.qkv[c, r0, vc] = jnp.where(late0, gv_late, gv_early).astype(BF)
                s.qkv[c, r1, vc] = jnp.where(late0, gv_early, gv_late).astype(BF)
            return carry

        lax.fori_loop(0, GRID // CR, step, 0)

    def gain_terms(which, grad, xhat):
        part = jnp.sum((grad * xhat).reshape(-1, 8, D), axis=0)
        s.gacc[which] += part

    def back_ff(c, grad_of):
        def step(i, carry):
            rows = pl.ds(i * RC, RC)
            gz = s.xs[c, rows]
            acc = None
            for j in range(4):
                cols = slice(512 * j, 512 * j + 512)
                gu = (nt(gz, s.wdn[cols, :]) * s.gel[c, rows, cols].astype(F32)).astype(BF)
                s.gel[c, rows, cols] = gu
                term = nt(gu, s.win[:, 2048 + 512 * j : 2560 + 512 * j])
                acc = term if acc is None else acc + term
            xh = s.xh2[c, rows]
            gain_terms(1, acc, xh)
            gm = grad_of(rows) + normed_back(acc, xh, s.r2[c, rows], gain_two)
            s.hb[rows] = gm
            gy = gm.astype(BF)
            s.gy[c, rows] = gy
            s.gob[rows] = nt(gy, s.win[:, 1536:2048]).astype(BF)
            return carry

        lax.fori_loop(0, CLIP // RC, step, 0)

    def back_in(c, put):
        def step(i, carry):
            rows = pl.ds(i * RC, RC)
            acc = None
            for j in range(3):
                cols = slice(512 * j, 512 * j + 512)
                term = nt(s.qkv[c, rows, cols], s.win[:, cols])
                acc = term if acc is None else acc + term
            xh = s.xh1[c, rows]
            gain_terms(0, acc, xh)
            put(rows, s.hb[rows] + normed_back(acc, xh, s.r1[c, rows], gain_one))
            return carry

        lax.fori_loop(0, CLIP // RC, step, 0)

    def add_into(ref, rows, cols, c, value):
        ref[rows, cols] = jnp.where(c == 0, value, ref[rows, cols] + value)

    def grad_down(c):
        for j in range(4):
            cols = slice(512 * j, 512 * j + 512)
            add_into(s.acc_dn, cols, slice(None), c, tn(s.act[c, :, cols], s.xs[c]))

    def grad_up(c):
        for j in range(4):
            cols = slice(512 * j, 512 * j + 512)
            add_into(s.acc_up, slice(None), cols, c, tn(s.a2[c], s.gel[c, :, cols]))

    def grad_attn(c):
        for j in range(3):
            cols = slice(512 * j, 512 * j + 512)
            add_into(s.acc_qkv, slice(None), cols, c, tn(s.a1[c], s.qkv[c, :, cols]))
        add_into(s.acc_out, slice(None), slice(None), c, tn(s.att[c], s.gy[c]))

    def load_half(k, i, half):
        if k == "a":
            return s.acc_dn[pl.ds(i * 128, 128), pl.ds(pl.multiple_of(half * 256, 128), 256)]
        rows = pl.ds(i * 32, 32)
        if k == "b":
            return s.acc_up[rows, pl.ds(pl.multiple_of(half * 1024, 128), 1024)]
        return jnp.concatenate(
            [
                s.acc_qkv[rows, pl.ds(pl.multiple_of(half * 768, 128), 768)],
                s.acc_out[rows, pl.ds(pl.multiple_of(half * 256, 128), 256)],
            ],
            axis=1,
        )

    def buf(name, k):
        return getattr(s, name + k)

    def copies(k, step):
        if k == "s":
            if step == 0:
                return [rcopy("s0", s.s_acc.at[:, :, 1 - core], s.s0, core_dev)]
            if step == 1:
                return [rcopy("s1%d" % i, s.s0.at[(z + 1 + i) % 4], s.s1.at[i], z_dev[i]) for i in range(3)]
            if step == 2:
                return [
                    rcopy("s2%d" % i, s.s0.at[z, pl.ds(2 * ((x + 1 + i) % 4), 2)], s.s2.at[i], x_dev[i])
                    for i in range(3)
                ]
            if step == 3:
                return [rcopy("s3", s.s0.at[z, 2 * x + 1 - yh], s.s3, y_dev)]
            return []
        rows, w = CHUNKS[k]
        h = w // 2
        r0 = buf("r0", k)
        if step == 0:
            return [rcopy(k + "0", buf("sb0", k), r0, core_dev)]
        if step == 1:
            return [
                rcopy(k + "1z%d" % i, r0.at[(z + 1 + i) % 4, :, :, pl.ds(0, h)], buf("r1z", k).at[i], z_dev[i])
                for i in range(3)
            ] + [
                rcopy(k + "1x%d" % i, r0.at[:, (x + 1 + i) % 4, :, pl.ds(h, h)], buf("r1x", k).at[i], x_dev[i])
                for i in range(3)
            ]
        if step == 2:
            return [
                rcopy(k + "2x%d" % i, r0.at[z, (x + 1 + i) % 4, :, pl.ds(0, h)], buf("r2a", k).at[i], x_dev[i])
                for i in range(3)
            ] + [
                rcopy(k + "2z%d" % i, r0.at[(z + 1 + i) % 4, x, :, pl.ds(h, h)], buf("r2b", k).at[i], z_dev[i])
                for i in range(3)
            ]
        if step == 3:
            return [rcopy(k + "3", buf("sb3", k), buf("r3", k), y_dev)]
        quarter = rows // 4
        return [rcopy(k + "4", buf("t4", k).at[pl.ds((1 - core) * quarter, quarter)], buf("r4", k), core_dev)]

    def arrived(k, step):
        for cp in copies(k, step):
            cp.wait_recv()

    def send(k, step):
        for cp in copies(k, step):
            cp.start()

    def reduce_step(k, step):
        if step > 0:
            arrived(k, step - 1)
        if k == "s":
            if step == 1:
                s.s0[...] += s.s_acc[:, :, core]
            elif step == 2:
                s.s0[z] += (s.s1[0] + s.s1[1]) + s.s1[2]
            elif step == 3:
                here = pl.ds(2 * x, 2)
                s.s0[z, here] += (s.s2[0] + s.s2[1]) + s.s2[2]
            elif step == 4:
                final = s.s0[z, 2 * x + yh] + s.s3[...]
                gbook_ref[...] = final[:, 0:64]
                gproj_ref[0] = final[:, 64:72]
                ggain_ref[0] = jnp.transpose(jnp.concatenate([final] * 16, axis=0))[72:74, 0:8]
                return
            send(k, step)
            return
        rows, w = CHUNKS[k]
        h = w // 2
        r0 = buf("r0", k)
        if step == 0:
            sb0 = buf("sb0", k)

            def body(i, carry):
                sb0[i // 4, i % 4] = load_half(k, i, 1 - core).astype(BF)
                return carry

            lax.fori_loop(0, 16, body, 0)
        elif step == 1:

            def body(i, carry):
                r0[i // 4, i % 4] = (load_half(k, i, core) + r0[i // 4, i % 4].astype(F32)).astype(BF)
                return carry

            lax.fori_loop(0, 16, body, 0)
        elif step == 2:
            rz = buf("r1z", k)
            rx = buf("r1x", k)

            def body(i, carry):
                r0[z, i, :, pl.ds(0, h)] = (
                    (r0[z, i, :, pl.ds(0, h)].astype(F32) + rz[0, i].astype(F32))
                    + (rz[1, i].astype(F32) + rz[2, i].astype(F32))
                ).astype(BF)
                r0[i, x, :, pl.ds(h, h)] = (
                    (r0[i, x, :, pl.ds(h, h)].astype(F32) + rx[0, i].astype(F32))
                    + (rx[1, i].astype(F32) + rx[2, i].astype(F32))
                ).astype(BF)
                return carry

            lax.fori_loop(0, 4, body, 0)
        elif step == 3:
            ra = buf("r2a", k)
            rb = buf("r2b", k)
            t3 = buf("t3", k)
            t3[:, :h] = (r0[z, x, :, pl.ds(0, h)].astype(F32) + ra[0].astype(F32)) + (
                ra[1].astype(F32) + ra[2].astype(F32)
            )
            t3[:, h:] = (r0[z, x, :, pl.ds(h, h)].astype(F32) + rb[0].astype(F32)) + (
                rb[1].astype(F32) + rb[2].astype(F32)
            )
            buf("sb3", k)[...] = t3[pl.ds((1 - yh) * (rows // 2), rows // 2), :].astype(BF)
        elif step == 4:
            t3 = buf("t3", k)
            buf("t4", k)[...] = t3[pl.ds(yh * (rows // 2), rows // 2), :] + buf("r3", k)[...].astype(F32)
        else:
            quarter = rows // 4
            mine = buf("t4", k)[pl.ds(core * quarter, quarter), :]
            other = buf("r4", k)[...]
            if k == "a":
                gdn_ref[0, :, pl.ds(pl.multiple_of(core * 256, 128), 256)] = mine
                gdn_ref[0, :, pl.ds(pl.multiple_of((1 - core) * 256, 128), 256)] = other
                piece = s.wdn[pl.ds(dp * 32, 32), :].astype(F32)
                adn_ref[0] = AVG_DECAY * avgdn_ref[0] + (1.0 - AVG_DECAY) * (
                    piece - LEARN_RATE * gdn_ref[0]
                )
            elif k == "b":
                gin_ref[0, :, pl.ds(pl.multiple_of(2048 + core * 1024, 128), 1024)] = mine
                gin_ref[0, :, pl.ds(pl.multiple_of(2048 + (1 - core) * 1024, 128), 1024)] = other
            else:
                gin_ref[0, :, pl.ds(pl.multiple_of(core * 768, 128), 768)] = mine[:, :768]
                gin_ref[0, :, pl.ds(pl.multiple_of((1 - core) * 768, 128), 768)] = other[:, :768]
                gin_ref[0, :, pl.ds(pl.multiple_of(1536 + core * 256, 128), 256)] = mine[:, 768:]
                gin_ref[0, :, pl.ds(pl.multiple_of(1536 + (1 - core) * 256, 128), 256)] = other[:, 768:]
            return
        send(k, step)

    def code_copy(c):
        return pltpu.make_async_remote_copy(
            src_ref=s.cxs.at[c], dst_ref=s.cxr.at[c], send_sem=send_sems.at[N_SEM - 2 + c],
            recv_sem=recv_sems.at[N_SEM - 2 + c], device_id=sec_dev, device_id_type=MESH,
        )

    for load in loads:
        load.wait()
    ag_start(0)

    @pl.when(is_e)
    def _():
        for c in range(2):
            grid_now = grids_ref[c]
            width = jnp.where(grid_now == 0, 16, jnp.where(grid_now == 1, 32, 8)).astype(I32)
            log_across = jnp.where(grid_now == 0, 1, jnp.where(grid_now == 1, 2, 0)).astype(I32)
            across_mask = jnp.where(grid_now == 0, 1, jnp.where(grid_now == 1, 3, 0)).astype(I32)
            window_no = rows_i >> 6
            inner = rows_i & 63
            source = (
                ((window_no >> log_across) * 8 + (inner >> 3)) * width
                + (window_no & across_mask) * 8
                + (inner & 7)
            )
            s.perm[c] = (source == cols_i).astype(F32).astype(BF)

        def forward(c, carry):
            for f in range(2):
                rows = slice(GRID * f, GRID * f + GRID)
                norm_qkv(c, rows, nn(s.perm[c], s.xs[c, rows]))

            @pl.when(c == 0)
            def _():
                ag_wait(0)
                ag_start(1)

            window_forward(c)

            @pl.when(c == 0)
            def _():
                ag_wait(1)
                ag_start(2)

            def put(rows, acc):
                s.eb[c, rows] = acc.astype(BF)

            feed_forward(c, put)

            @pl.when(c == 0)
            def _():
                ag_wait(2)
                ag_start(3)
                ag_wait(3)

            entries(c)
            entry = s.ent[c]
            vec = tt(proj_ref[0], s.eb[c])
            for f in range(2):
                cols = slice(GRID * f, GRID * f + GRID)
                entry_enc = nt(pad16(entry[:, cols]), s.perm[c])[0:8]
                sent = pad16(vec[:, cols] + entry_enc)
                s.cxs[c, :, cols] = nn(sent, s.perm[c]).astype(BF)
            code_copy(c).start()
            return carry

        lax.fori_loop(0, 2, forward, 0)

    @pl.when(is_d)
    def _():
        for step in range(4):
            ag_wait(step)
            if step < 3:
                ag_start(step + 1)
        for c in range(2):
            entries(c)

        def both(c, carry):
            code_copy(c).wait_recv()
            quant = s.cxr[c][0:8].astype(F32) + s.ent[c]
            s.cvec[c] = pad16(quant)
            for f in range(2):
                rows = slice(GRID * f, GRID * f + GRID)
                h = tt(s.cvec[c][0:8, rows], proj_ref[0])
                norm_qkv(c, rows, h)
            frames_forward(c)

            def put(rows, acc):
                bout_ref[0, pl.ds(c * CLIP + rows.start, rows.size), :] = acc.astype(BF)

            feed_forward(c, put)
            back_ff(c, lambda rows: s.xs[c, rows].astype(F32))
            frames_backward(c)

            def put_back(rows, acc):
                s.eb[c, rows] = acc.astype(BF)

            back_in(c, put_back)
            grad_code = tt(proj_ref[0], s.eb[c])
            s.cxs[c] = pad16(grad_code)
            code_copy(c).start()
            book_proj_terms(
                c, s.cxs[c][0:8].astype(F32), s.eb[c], s.cvec[c][0:8].astype(F32)
            )
            return carry

        lax.fori_loop(0, 2, both, 0)

    def last(c, carry):
        @pl.when(is_e)
        def _():
            code_copy(c).wait_recv()
            for f in range(2):
                cols = slice(GRID * f, GRID * f + GRID)
                s.cvec[c, :, cols] = nt(s.cxr[c, :, cols], s.perm[c]).astype(BF)
            g = tt(s.cvec[c][0:8], proj_ref[0])
            s.gg[...] = g
            s.xs[c] = g.astype(BF)
            book_proj_terms(
                c, s.cxr[c][0:8].astype(F32), s.eb[c], s.cvec[c][0:8].astype(F32)
            )

        grad_down(c)

        @pl.when(c == 1)
        def _():
            reduce_step("a", 0)

        @pl.when(is_e)
        def _():
            back_ff(c, lambda rows: s.gg[rows])

        grad_up(c)

        @pl.when(c == 1)
        def _():
            reduce_step("b", 0)
            reduce_step("a", 1)

        @pl.when(is_e)
        def _():
            window_backward(c)

            def put_back(rows, acc):
                s.gob[rows] = acc.astype(BF)

            back_in(c, put_back)
            for f in range(2):
                back = tn(s.perm[c], s.gob[GRID * f : GRID * f + GRID])
                bout_ref[0, pl.ds(c * CLIP + GRID * f, GRID), :] = back.astype(BF)

        grad_attn(c)
        return carry

    lax.fori_loop(0, 2, last, 0)

    reduce_step("c", 0)
    sums = jnp.concatenate(
        [
            jnp.sum(s.gacc[0], axis=0, keepdims=True),
            jnp.sum(s.gacc[1], axis=0, keepdims=True),
            jnp.zeros((6, D), F32),
        ],
        axis=0,
    )
    wide_sums = jnp.concatenate([jnp.zeros((72, D), F32), sums, jnp.zeros((48, D), F32)], axis=0)
    s.s_acc[...] += jnp.transpose(wide_sums).reshape(4, 8, 2, 8, 128)
    order = [
        "s0", "b1", "c1", "s1", "a2", "b2", "s2", "c2", "a3", "s3", "b3", "c3", "a4", "b4", "s4", "c4",
        "a5", "b5", "c5",
    ]
    for item in order:
        reduce_step(item[0], int(item[1]))

    half_rows = s.win[pl.ds(16 * (dp // 2), 16), :].astype(F32)
    piece = jnp.where(core == 0, half_rows[0:8], half_rows[8:16])
    ain_ref[0] = AVG_DECAY * avgin_ref[0] + (1.0 - AVG_DECAY) * (piece - LEARN_RATE * gin_ref[0])

    for c in range(2):
        code_copy(c).wait_send()
    for k in ("a", "b", "c", "s"):
        for step in range(5):
            for cp in copies(k, step):
                cp.wait_send()


def body(
    boundary, in_weights, down_weight, gains, proj, codebook, codes, grids, orders, avg_in, avg_down
):
    vmem = pl.BlockSpec(memory_space=pltpu.VMEM)
    smem = pl.BlockSpec(memory_space=pltpu.SMEM)
    hbm = pl.BlockSpec(memory_space=pl.ANY)
    outs = (
        jax.ShapeDtypeStruct(boundary.shape, BF),
        jax.ShapeDtypeStruct(avg_in.shape, F32),
        jax.ShapeDtypeStruct(avg_down.shape, F32),
        jax.ShapeDtypeStruct((1, 2, 8), F32),
        jax.ShapeDtypeStruct((1, 8, 8), F32),
        jax.ShapeDtypeStruct(codebook.shape, F32),
        jax.ShapeDtypeStruct(avg_in.shape, F32),
        jax.ShapeDtypeStruct(avg_down.shape, F32),
    )
    scratch = [pltpu.VMEM(shape, dtype) for shape, dtype in SHAPES.values()]
    scratch += [pltpu.SemaphoreType.DMA((N_SEM,)), pltpu.SemaphoreType.DMA((N_SEM,)), pltpu.SemaphoreType.DMA((4,))]
    return pl.pallas_call(
        mega,
        out_shape=outs,
        in_specs=[hbm, hbm, hbm, vmem, vmem, vmem, vmem, smem, smem, vmem, vmem],
        out_specs=[vmem] * 8,
        scratch_shapes=scratch,
        compiler_params=pltpu.CompilerParams(
            collective_id=0, has_side_effects=True, vmem_limit_bytes=63 << 20
        ),
        name="both_sections",
    )(
        boundary, in_weights, down_weight, gains, proj, codebook, codes.reshape(8, 128), grids, orders,
        avg_in, avg_down,
    )


def solution(mesh):
    placed = (
        P("section", "dp", None),
        P("section", None, None),
        P("section", None, None),
        P("section", None, None),
        P("section", None, None),
        P(None, ("section", "dp")),
        P("dp"),
        P("dp"),
        P("dp", None),
        P("section", "dp", None),
        P("section", "dp", None),
    )
    return jax.shard_map(
        body,
        mesh=mesh,
        in_specs=placed,
        out_specs=(
            P("section", "dp", None),
            P("section", "dp", None),
            P("section", "dp", None),
            P("section", None, "dp"),
            P("section", "dp", None),
            P(None, ("section", "dp")),
            P("section", "dp", None),
            P("section", "dp", None),
        ),
        check_vma=False,
    )
```

time: 1550 us -> 125 us (0.08)
  waiting for transfers between devices: 564 us -> 0 us
  blocking collectives: 416 us -> 0 us
  local copies, waits for them, and re-layouts: 255 us -> 13.6 us
  matrix products: 234 us -> 0 us
  Pallas kernels: 0 us -> 110 us
  other arithmetic: 37.9 us -> 0 us
  between operations: 20.4 us -> 0.65 us
    reduce_scatter x2 -> x0, waiting for transfers between devices: 563 us -> none  [the longest x1 342 us: body(): lax.psum_scatter(totals[0], 'dp', scatter_dimension=1, tiled=True)]
    unnamed x1 -> x0, blocking collectives: 317 us -> none
    dot_general x85 -> x0, matrix products: 210 us -> none  [the longest x43 88.4 us: contract(): lax.dot_general(left, right, (((left_dim,), (right_dim,)), ((), ())), pre...]
    pallas_call x0 -> x1, Pallas kernels: none -> 110 us  [body(): pl.pallas_call(mega, out_shape=outs, in_specs=[hbm, hbm, hbm, vmem, vmem,...]
    all_gather x1 -> x0, blocking collectives: 98.9 us -> none  [body(): book_half = lax.all_gather(codebook, 'dp', axis=1, tiled=True)]
    reshape x21 -> x0, local copies, waits for them, and re-layouts: 66.6 us -> none  [the longest x6 30.7 us: block_forward(): shaped = packed.reshape(groups, WINDOW, 3, HEADS, HEAD)]
    gather x27 -> x0, local copies, waits for them, and re-layouts: 61.8 us -> none  [the longest x12 25.6 us: body(): jnp.take(block_in, source, axis=0)]
    convert_element_type x12 -> x0, local copies, waits for them, and re-layouts: 28.1 us -> none  [block_forward(): attended = attended.reshape(-1, feature_dim).astype(jnp.bfloat16)]
  transfers between devices with their start and end apart: 7 -> 0, of which waited for: 3 -> 0; matrix products, arithmetic and copies ran while one was open for 9% -> 0% of each run, Pallas kernels for 0% -> 0%
where the time goes in v1:
time: 125 us; the launch traced here: 124 us
  Pallas kernels  110 us (88%)
  local copies, waits for them, and re-layouts  13.6 us (11%)
    pallas_call x1, Pallas kernels, body(): pl.pallas_call(mega, out_shape=outs, in_specs=[hbm, hbm, hbm, vmem, vmem,...  110 us
    unnamed x9, local copies, waits for them, and re-layouts  13.6 us

profile of v1, /device:TPU:1, one launch (start us, length us, event | category | flops | bytes accessed | tf_op | source)
XLA Modules:
  0.0 124.3 jit_solution(8544342977445124912)
XLA Ops:
  0.6 1.5 %copy.19.proj_ref = bf16[1,512,8]{2,1,0:T(8,128)(2,1)} copy(bf16[1,512,8]{1,2,0:T(8,128)(2,1)} %param.15) | data formatting | bytes 16384 | tf_op args[4]
  2.1 110.1 %both_sections.1 = (bf16[1,1024,512]{2,1,0:T(8,128)(2,1)}, f32[1,8,4096]{2,1,0:T(8,128)}, f32[1,32,512]{2,1,0:T(8,128)}, f32[1,2,8]{2,1,0:T(2,128)}, f32[1,8,8]{...) custom-call(bf16[1,1024,512]{2,1,0:T(8,128)(2,1)} %x_hbm.1, ...), custom_call_target="tpu_custom_call" | custom-call | tf_op jit(solution)/shard_map/both_sections/pallas_call | solution.py:856
  112.2 2.3 %copy.28 = bf16[1,1024,512]{2,1,0:T(8,128)(2,1)} copy(bf16[1,1024,512]{2,1,0:T(8,128)(2,1)} %get-tuple-element.16) | data formatting | bytes 2097152
  114.5 1.6 %copy.29 = f32[1,8,4096]{2,1,0:T(8,128)} copy(f32[1,8,4096]{2,1,0:T(8,128)} %get-tuple-element.17) | data formatting | bytes 262144
  116.0 1.5 %copy.30 = f32[1,32,512]{2,1,0:T(8,128)} copy(f32[1,32,512]{2,1,0:T(8,128)} %get-tuple-element.18) | data formatting | bytes 131072
  117.5 1.2 copy.31
  118.7 1.3 %copy.32 = f32[1,8,8]{2,1,0:T(8,128)} copy(f32[1,8,8]{2,1,0:T(8,128)} %get-tuple-element.20) | data formatting | bytes 512
  120.0 1.3 %copy.33 = f32[8,64]{1,0:T(8,128)} copy(f32[8,64]{1,0:T(8,128)} %get-tuple-element.21) | data formatting | bytes 4096
  121.3 1.6 %copy.34 = f32[1,8,4096]{2,1,0:T(8,128)} copy(f32[1,8,4096]{2,1,0:T(8,128)} %get-tuple-element.22) | data formatting | bytes 262144
  122.9 1.5 %copy.35 = f32[1,32,512]{2,1,0:T(8,128)} copy(f32[1,32,512]{2,1,0:T(8,128)} %get-tuple-element.23) | data formatting | bytes 131072

commit v2 on v1

--- a/solution.py
+++ b/solution.py
@@ -22,9 +22,10 @@
 AVG_DECAY = 0.9
 LEARN_RATE = 0.0005
 SCALE = 0.125
-RC = 256
-
-CHUNKS = {"a": (128, 256), "b": (32, 1024), "c": (32, 1024)}
+RC = 512
+WB = 4
+
+CHUNKS = {"a": (128, 256), "b": (32, 1280), "c": (32, 768)}
 
 
 def nn(left, right):
@@ -65,12 +66,10 @@
 def gelu_pair(u):
     c0 = 0.7978845608028654
     c1 = 0.7978845608028654 * 0.044715
-    u2 = u * u
-    t = jnp.tanh(u * (c0 + c1 * u2))
-    hu = 0.5 * u
-    ht = 0.5 + 0.5 * t
-    value = hu + hu * t
-    slope = ht + hu * (1.0 - t * t) * (c0 + (3.0 * c1) * u2)
+    m = c1 * (u * u)
+    half = 0.5 + 0.5 * jnp.tanh(u * (c0 + m))
+    value = u * half
+    slope = half + (value - value * half) * (2.0 * c0 + 6.0 * m)
     return value, slope
 
 
@@ -90,7 +89,7 @@
         "ent": ((2, 8, CLIP), F32),
         "cvec": ((2, 16, CLIP), BF),
         "hb": ((CLIP, D), F32),
-        "gg": ((CLIP, D), F32),
+        "bo": ((2 * CLIP, D), BF),
         "gob": ((CLIP, D), BF),
         "xh1": ((2, CLIP, D), F32),
         "xh2": ((2, CLIP, D), F32),
@@ -118,22 +117,23 @@
     }
     for k, (rows, w) in CHUNKS.items():
         h = w // 2
-        shapes["sb0" + k] = ((4, 4, rows, w), BF)
-        shapes["r0" + k] = ((4, 4, rows, w), BF)
-        shapes["r1z" + k] = ((3, 4, rows, h), BF)
-        shapes["r1x" + k] = ((3, 4, rows, h), BF)
-        shapes["r2a" + k] = ((3, rows, h), BF)
-        shapes["r2b" + k] = ((3, rows, h), BF)
-        shapes["t3" + k] = ((rows, w), F32)
-        shapes["sb3" + k] = ((rows // 2, w), BF)
-        shapes["r3" + k] = ((rows // 2, w), BF)
-        shapes["t4" + k] = ((rows // 2, w), F32)
-        shapes["r4" + k] = ((rows // 4, w), F32)
+        half = rows // 2
+        shapes["sb0" + k] = ((4, 4, 2, half, w), BF)
+        shapes["r0" + k] = ((4, 4, 2, half, w), BF)
+        for ax in "zx":
+            for slot in "012":
+                shapes["q" + slot + ax + k] = ((2, 4, half, h), BF)
+            shapes["r2" + ax + k] = ((3, 2, half, h), BF)
+        shapes["t3" + k] = ((2, half, w), F32)
+        shapes["sb3" + k] = ((half, w), BF)
+        shapes["r3" + k] = ((half, w), BF)
+        shapes["t4" + k] = ((half, w), F32)
+        shapes["r4" + k] = ((half // 2, w), F32)
     return shapes
 
 
 SHAPES = ten_shapes()
-N_SEM = 80
+N_SEM = 120
 
 
 class Refs:
@@ -143,7 +143,7 @@
 def mega(
     x_hbm, win_hbm, wdn_hbm, gains_ref, proj_ref, book_ref, codes_ref, grids_ref, orders_ref,
     avgin_ref, avgdn_ref,
-    bout_ref, gin_ref, gdn_ref, ggain_ref, gproj_ref, gbook_ref, ain_ref, adn_ref,
+    bout_hbm, gin_ref, gdn_ref, small_ref, ain_ref, adn_ref,
     *scratch,
 ):
     s = Refs()
@@ -165,6 +165,10 @@
 
     core_dev = place(z, x, yh, 1 - core)
     y_dev = place(z, x, 1 - yh, core)
+    def flips(v):
+        return {1: v + 1 - 2 * (v % 2), 2: (v + 2) % 4, 3: 3 - v}
+
+    z_flip, x_flip = flips(z), flips(x)
     z_dev = [place((z + d) % 4, x, yh, core) for d in (1, 2, 3)]
     x_dev = [place(z, (x + d) % 4, yh, core) for d in (1, 2, 3)]
     sec_dev = (1 - sec, dp)
@@ -184,12 +188,19 @@
 
     loads = [
         pltpu.make_async_copy(x_hbm.at[0, pl.ds(0, CLIP)], s.xs.at[0], load_sems.at[0]),
-        pltpu.make_async_copy(x_hbm.at[0, pl.ds(CLIP, CLIP)], s.xs.at[1], load_sems.at[1]),
-        pltpu.make_async_copy(win_hbm.at[0], s.win, load_sems.at[2]),
+        pltpu.make_async_copy(win_hbm.at[0, :, pl.ds(0, 3 * D)], s.win.at[:, pl.ds(0, 3 * D)], load_sems.at[1]),
+        pltpu.make_async_copy(
+            win_hbm.at[0, :, pl.ds(3 * D, D + FF)], s.win.at[:, pl.ds(3 * D, D + FF)], load_sems.at[2]
+        ),
         pltpu.make_async_copy(wdn_hbm.at[0], s.wdn, load_sems.at[3]),
+        pltpu.make_async_copy(x_hbm.at[0, pl.ds(CLIP, CLIP)], s.xs.at[1], load_sems.at[4]),
     ]
     for load in loads:
         load.start()
+
+    def bout_copy(c):
+        rows = pl.ds(c * CLIP, CLIP)
+        return pltpu.make_async_copy(s.bo.at[rows], bout_hbm.at[0, rows], load_sems.at[5 + c])
 
     barrier = pltpu.get_barrier_semaphore()
     peers = [core_dev, y_dev, sec_dev] + z_dev + x_dev
@@ -206,6 +217,7 @@
         code_row = jnp.concatenate([codes_ref[4 * c + k : 4 * c + k + 1, :] for k in range(4)], axis=1)
         s.cds[c] = jnp.broadcast_to(code_row - sec * HALF, (8, CLIP))
 
+    proj_t = proj_ref[...]
     gain_one = gains_ref[0, 0:1, :].astype(F32)
     gain_two = gains_ref[0, 1:2, :].astype(F32)
     book = book_ref[...].astype(F32)
@@ -299,65 +311,75 @@
             a = (xh * gain_two).astype(BF)
             s.a2[c, rows] = a
             acc = m
-            for j in range(4):
-                cols = slice(512 * j, 512 * j + 512)
-                u = nn(a, s.win[:, 2048 + 512 * j : 2560 + 512 * j])
-                value, slope = gelu_pair(u)
-                value = value.astype(BF)
+            nxt = nn(a, s.win[:, 2048:2304])
+            for j in range(8):
+                cols = slice(256 * j, 256 * j + 256)
+                u = nxt
+                if j < 7:
+                    nxt = nn(a, s.win[:, 2304 + 256 * j : 2560 + 256 * j])
+                value, slope = gelu_pair(u.astype(BF))
                 s.act[c, rows, cols] = value
-                s.gel[c, rows, cols] = slope.astype(BF)
+                s.gel[c, rows, cols] = slope
                 acc = acc + nn(value, s.wdn[cols, :])
             put(rows, acc)
             return carry
 
         lax.fori_loop(0, CLIP // RC, step, 0)
 
-    def window_forward(c):
-        def step(w, carry):
-            rows = pl.ds(w * WINDOW, WINDOW)
+    def units(c, w, count):
+        out = []
+        for n in range(count):
+            rows = pl.ds((w * count + n) * WINDOW, WINDOW)
             for quad in range(2):
-                cols = slice(256 * quad, 256 * quad + 256)
-                q4 = s.qkv[c, rows, 256 * quad : 256 * quad + 256]
-                k4 = s.qkv[c, rows, 512 + 256 * quad : 768 + 256 * quad]
-                v4 = s.qkv[c, rows, 1024 + 256 * quad : 1280 + 256 * quad]
-                q_wide = jnp.concatenate([q4] * 4, axis=0) * s.bds[...]
-                scores = nt(k4, q_wide)
-                top = jnp.max(scores, axis=0, keepdims=True)
-                e = jnp.exp(scores - top)
-                p = e * (1.0 / jnp.sum(e, axis=0, keepdims=True))
-                s.prob[c, rows, cols] = p
-                wide = tn(p.astype(BF), v4) * s.bdf[...]
-                out = (wide[0:64] + wide[64:128]) + (wide[128:192] + wide[192:256])
-                s.att[c, rows, cols] = (out * (1.0 / SCALE)).astype(BF)
-            return carry
-
-        lax.fori_loop(0, CLIP // WINDOW, step, 0)
-
-    def window_backward(c):
-        def step(w, carry):
-            rows = pl.ds(w * WINDOW, WINDOW)
-            for quad in range(2):
-                cols = slice(256 * quad, 256 * quad + 256)
-                qc = slice(256 * quad, 256 * quad + 256)
-                kc = slice(512 + 256 * quad, 768 + 256 * quad)
-                vc = slice(1024 + 256 * quad, 1280 + 256 * quad)
-                q4 = s.qkv[c, rows, qc]
-                k4 = s.qkv[c, rows, kc]
-                v4 = s.qkv[c, rows, vc]
-                go = s.gob[rows, cols]
-                p = s.prob[c, rows, cols]
-                go_wide = jnp.concatenate([go] * 4, axis=0) * s.bd1[...]
-                q_wide = jnp.concatenate([q4] * 4, axis=0) * s.bds[...]
-                gp = nt(v4, go_wide)
-                gs = (p * (gp - jnp.sum(gp * p, axis=0, keepdims=True))).astype(BF)
-                s.qkv[c, rows, vc] = nn(p.astype(BF), go_wide).astype(BF)
-                s.qkv[c, rows, kc] = nn(gs, q_wide).astype(BF)
-                wide = tn(gs, k4) * s.bdf[...]
-                out = (wide[0:64] + wide[64:128]) + (wide[128:192] + wide[192:256])
-                s.qkv[c, rows, qc] = out.astype(BF)
-            return carry
-
-        lax.fori_loop(0, CLIP // WINDOW, step, 0)
+                out.append((rows, 256 * quad))
+        return out
+
+    def widened(v, mask):
+        return jnp.concatenate([v] * 4, axis=0) * mask
+
+    def heads_of(wide):
+        return (wide[0:64] + wide[64:128]) + (wide[128:192] + wide[192:256])
+
+    def window_forward(c, w):
+        if True:
+            us = units(c, w, WB)
+            bds = s.bds[...]
+            bdf = s.bdf[...]
+            q = [s.qkv[c, r, o : o + 256] for r, o in us]
+            k = [s.qkv[c, r, 512 + o : 768 + o] for r, o in us]
+            v = [s.qkv[c, r, 1024 + o : 1280 + o] for r, o in us]
+            scores = [nt(kk, widened(qq, bds)) for kk, qq in zip(k, q)]
+            e = [jnp.exp(x - jnp.max(x, axis=0, keepdims=True)) for x in scores]
+            p = [x * (1.0 / jnp.sum(x, axis=0, keepdims=True)) for x in e]
+            wide = [tn(x.astype(BF), vv) for x, vv in zip(p, v)]
+            att = [(heads_of(x * bdf) * (1.0 / SCALE)).astype(BF) for x in wide]
+            for (r, o), pp, aa in zip(us, p, att):
+                s.prob[c, r, o : o + 256] = pp
+                s.att[c, r, o : o + 256] = aa
+
+    def window_backward(c, w):
+        if True:
+            us = units(c, w, WB)
+            bds = s.bds[...]
+            bd1 = s.bd1[...]
+            bdf = s.bdf[...]
+            q = [s.qkv[c, r, o : o + 256] for r, o in us]
+            k = [s.qkv[c, r, 512 + o : 768 + o] for r, o in us]
+            v = [s.qkv[c, r, 1024 + o : 1280 + o] for r, o in us]
+            go = [widened(s.gob[r, o : o + 256], bd1) for r, o in us]
+            p = [s.prob[c, r, o : o + 256] for r, o in us]
+            gp = [nt(vv, gg) for vv, gg in zip(v, go)]
+            gv = [nn(pp.astype(BF), gg).astype(BF) for pp, gg in zip(p, go)]
+            gs = [
+                (pp * (x - jnp.sum(x * pp, axis=0, keepdims=True))).astype(BF)
+                for pp, x in zip(p, gp)
+            ]
+            gk = [nn(x, widened(qq, bds)).astype(BF) for x, qq in zip(gs, q)]
+            gq = [heads_of(tn(x, kk) * bdf).astype(BF) for x, kk in zip(gs, k)]
+            for (r, o), a, b, d in zip(us, gq, gk, gv):
+                s.qkv[c, r, o : o + 256] = a
+                s.qkv[c, r, 512 + o : 768 + o] = b
+                s.qkv[c, r, 1024 + o : 1280 + o] = d
 
     def head_sums(v):
         hi = v.astype(BF)
@@ -490,25 +512,29 @@
             cols = slice(512 * j, 512 * j + 512)
             add_into(s.acc_up, slice(None), cols, c, tn(s.a2[c], s.gel[c, :, cols]))
 
+        add_into(s.acc_out, slice(None), slice(None), c, tn(s.att[c], s.gy[c]))
+
     def grad_attn(c):
         for j in range(3):
             cols = slice(512 * j, 512 * j + 512)
             add_into(s.acc_qkv, slice(None), cols, c, tn(s.a1[c], s.qkv[c, :, cols]))
-        add_into(s.acc_out, slice(None), slice(None), c, tn(s.att[c], s.gy[c]))
 
     def load_half(k, i, half):
         if k == "a":
-            return s.acc_dn[pl.ds(i * 128, 128), pl.ds(pl.multiple_of(half * 256, 128), 256)]
+            v = s.acc_dn[pl.ds(i * 128, 128), pl.ds(pl.multiple_of(half * 256, 128), 256)]
+            return v.reshape(2, 64, 256)
         rows = pl.ds(i * 32, 32)
-        if k == "b":
-            return s.acc_up[rows, pl.ds(pl.multiple_of(half * 1024, 128), 1024)]
-        return jnp.concatenate(
+        if k == "c":
+            v = s.acc_qkv[rows, pl.ds(pl.multiple_of(half * 768, 128), 768)]
+            return v.reshape(2, 16, 768)
+        v = jnp.concatenate(
             [
-                s.acc_qkv[rows, pl.ds(pl.multiple_of(half * 768, 128), 768)],
+                s.acc_up[rows, pl.ds(pl.multiple_of(half * 1024, 128), 1024)],
                 s.acc_out[rows, pl.ds(pl.multiple_of(half * 256, 128), 256)],
             ],
             axis=1,
         )
+        return v.reshape(2, 16, 1280)
 
     def buf(name, k):
         return getattr(s, name + k)
@@ -532,26 +558,44 @@
         r0 = buf("r0", k)
         if step == 0:
             return [rcopy(k + "0", buf("sb0", k), r0, core_dev)]
-        if step == 1:
-            return [
-                rcopy(k + "1z%d" % i, r0.at[(z + 1 + i) % 4, :, :, pl.ds(0, h)], buf("r1z", k).at[i], z_dev[i])
-                for i in range(3)
-            ] + [
-                rcopy(k + "1x%d" % i, r0.at[:, (x + 1 + i) % 4, :, pl.ds(h, h)], buf("r1x", k).at[i], x_dev[i])
-                for i in range(3)
-            ]
-        if step == 2:
-            return [
-                rcopy(k + "2x%d" % i, r0.at[z, (x + 1 + i) % 4, :, pl.ds(0, h)], buf("r2a", k).at[i], x_dev[i])
-                for i in range(3)
-            ] + [
-                rcopy(k + "2z%d" % i, r0.at[(z + 1 + i) % 4, x, :, pl.ds(h, h)], buf("r2b", k).at[i], z_dev[i])
-                for i in range(3)
-            ]
-        if step == 3:
-            return [rcopy(k + "3", buf("sb3", k), buf("r3", k), y_dev)]
+        lo, hi = pl.ds(0, h), pl.ds(h, h)
+        out = []
+        if step in (1, 2, 3):
+            for y in range(2):
+                first, second = ((1, 3), (3, 1))[y]
+                hop = second if step == 3 else first
+                block = {1: 2, 2: first, 3: second}[step]
+                slot = {1: "q1", 2: "q0", 3: "q2"}[step]
+                out.append(
+                    rcopy(
+                        "%s%dz%d" % (k, step, y), r0.at[z_flip[block], :, y, :, lo],
+                        buf(slot + "z", k).at[y], place(z_flip[hop], x, yh, core),
+                    )
+                )
+                out.append(
+                    rcopy(
+                        "%s%dx%d" % (k, step, y), r0.at[:, x_flip[block], y, :, hi],
+                        buf(slot + "x", k).at[y], place(z, x_flip[hop], yh, core),
+                    )
+                )
+            return out
+        if step == 4:
+            for i in range(3):
+                out.append(
+                    rcopy(
+                        "%s4x%d" % (k, i), r0.at[z, (x + 1 + i) % 4, :, :, lo], buf("r2x", k).at[i], x_dev[i]
+                    )
+                )
+                out.append(
+                    rcopy(
+                        "%s4z%d" % (k, i), r0.at[(z + 1 + i) % 4, x, :, :, hi], buf("r2z", k).at[i], z_dev[i]
+                    )
+                )
+            return out
+        if step == 5:
+            return [rcopy(k + "5", buf("sb3", k), buf("r3", k), y_dev)]
         quarter = rows // 4
-        return [rcopy(k + "4", buf("t4", k).at[pl.ds((1 - core) * quarter, quarter)], buf("r4", k), core_dev)]
+        return [rcopy(k + "6", buf("t4", k).at[pl.ds((1 - core) * quarter, quarter)], buf("r4", k), core_dev)]
 
     def arrived(k, step):
         for cp in copies(k, step):
@@ -562,9 +606,9 @@
             cp.start()
 
     def reduce_step(k, step):
-        if step > 0:
-            arrived(k, step - 1)
         if k == "s":
+            if step > 0:
+                arrived(k, step - 1)
             if step == 1:
                 s.s0[...] += s.s_acc[:, :, core]
             elif step == 2:
@@ -573,16 +617,15 @@
                 here = pl.ds(2 * x, 2)
                 s.s0[z, here] += (s.s2[0] + s.s2[1]) + s.s2[2]
             elif step == 4:
-                final = s.s0[z, 2 * x + yh] + s.s3[...]
-                gbook_ref[...] = final[:, 0:64]
-                gproj_ref[0] = final[:, 64:72]
-                ggain_ref[0] = jnp.transpose(jnp.concatenate([final] * 16, axis=0))[72:74, 0:8]
+                small_ref[...] = s.s0[z, 2 * x + yh] + s.s3[...]
                 return
             send(k, step)
             return
         rows, w = CHUNKS[k]
         h = w // 2
+        half = rows // 2
         r0 = buf("r0", k)
+        lo, hi = pl.ds(0, h), pl.ds(h, h)
         if step == 0:
             sb0 = buf("sb0", k)
 
@@ -591,64 +634,80 @@
                 return carry
 
             lax.fori_loop(0, 16, body, 0)
+            send(k, 0)
         elif step == 1:
+            arrived(k, 0)
 
             def body(i, carry):
                 r0[i // 4, i % 4] = (load_half(k, i, core) + r0[i // 4, i % 4].astype(F32)).astype(BF)
                 return carry
 
             lax.fori_loop(0, 16, body, 0)
+            send(k, 1)
+            send(k, 2)
         elif step == 2:
-            rz = buf("r1z", k)
-            rx = buf("r1x", k)
-
-            def body(i, carry):
-                r0[z, i, :, pl.ds(0, h)] = (
-                    (r0[z, i, :, pl.ds(0, h)].astype(F32) + rz[0, i].astype(F32))
-                    + (rz[1, i].astype(F32) + rz[2, i].astype(F32))
+            arrived(k, 1)
+            for y in range(2):
+                second = (3, 1)[y]
+                zb, xb = z_flip[second], x_flip[second]
+                r0[zb, :, y, :, lo] = (
+                    r0[zb, :, y, :, lo].astype(F32) + buf("q1z", k)[y].astype(F32)
                 ).astype(BF)
-                r0[i, x, :, pl.ds(h, h)] = (
-                    (r0[i, x, :, pl.ds(h, h)].astype(F32) + rx[0, i].astype(F32))
-                    + (rx[1, i].astype(F32) + rx[2, i].astype(F32))
+                r0[:, xb, y, :, hi] = (
+                    r0[:, xb, y, :, hi].astype(F32) + buf("q1x", k)[y].astype(F32)
                 ).astype(BF)
-                return carry
-
-            lax.fori_loop(0, 4, body, 0)
+            send(k, 3)
         elif step == 3:
-            ra = buf("r2a", k)
-            rb = buf("r2b", k)
+            arrived(k, 2)
+            arrived(k, 3)
+            for y in range(2):
+                r0[z, :, y, :, lo] = (
+                    r0[z, :, y, :, lo].astype(F32) + buf("q0z", k)[y].astype(F32)
+                    + buf("q2z", k)[y].astype(F32)
+                ).astype(BF)
+                r0[:, x, y, :, hi] = (
+                    r0[:, x, y, :, hi].astype(F32) + buf("q0x", k)[y].astype(F32)
+                    + buf("q2x", k)[y].astype(F32)
+                ).astype(BF)
+            send(k, 4)
+        elif step == 4:
+            arrived(k, 4)
+            ra = buf("r2x", k)
+            rb = buf("r2z", k)
             t3 = buf("t3", k)
-            t3[:, :h] = (r0[z, x, :, pl.ds(0, h)].astype(F32) + ra[0].astype(F32)) + (
+            t3[:, :, lo] = (r0[z, x, :, :, lo].astype(F32) + ra[0].astype(F32)) + (
                 ra[1].astype(F32) + ra[2].astype(F32)
             )
-            t3[:, h:] = (r0[z, x, :, pl.ds(h, h)].astype(F32) + rb[0].astype(F32)) + (
+            t3[:, :, hi] = (r0[z, x, :, :, hi].astype(F32) + rb[0].astype(F32)) + (
                 rb[1].astype(F32) + rb[2].astype(F32)
             )
-            buf("sb3", k)[...] = t3[pl.ds((1 - yh) * (rows // 2), rows // 2), :].astype(BF)
-        elif step == 4:
-            t3 = buf("t3", k)
-            buf("t4", k)[...] = t3[pl.ds(yh * (rows // 2), rows // 2), :] + buf("r3", k)[...].astype(F32)
+            buf("sb3", k)[...] = t3[1 - yh].astype(BF)
+            send(k, 5)
+        elif step == 5:
+            arrived(k, 5)
+            buf("t4", k)[...] = buf("t3", k)[yh] + buf("r3", k)[...].astype(F32)
+            send(k, 6)
         else:
+            arrived(k, 6)
             quarter = rows // 4
             mine = buf("t4", k)[pl.ds(core * quarter, quarter), :]
             other = buf("r4", k)[...]
+
+            def put(ref, start, width, part):
+                for c, v in ((core, mine), (1 - core, other)):
+                    ref[0, :, pl.ds(pl.multiple_of(start + c * width, 128), width)] = v[:, part : part + width]
+
             if k == "a":
-                gdn_ref[0, :, pl.ds(pl.multiple_of(core * 256, 128), 256)] = mine
-                gdn_ref[0, :, pl.ds(pl.multiple_of((1 - core) * 256, 128), 256)] = other
+                put(gdn_ref, 0, 256, 0)
                 piece = s.wdn[pl.ds(dp * 32, 32), :].astype(F32)
                 adn_ref[0] = AVG_DECAY * avgdn_ref[0] + (1.0 - AVG_DECAY) * (
                     piece - LEARN_RATE * gdn_ref[0]
                 )
             elif k == "b":
-                gin_ref[0, :, pl.ds(pl.multiple_of(2048 + core * 1024, 128), 1024)] = mine
-                gin_ref[0, :, pl.ds(pl.multiple_of(2048 + (1 - core) * 1024, 128), 1024)] = other
+                put(gin_ref, 2048, 1024, 0)
+                put(gin_ref, 1536, 256, 1024)
             else:
-                gin_ref[0, :, pl.ds(pl.multiple_of(core * 768, 128), 768)] = mine[:, :768]
-                gin_ref[0, :, pl.ds(pl.multiple_of((1 - core) * 768, 128), 768)] = other[:, :768]
-                gin_ref[0, :, pl.ds(pl.multiple_of(1536 + core * 256, 128), 256)] = mine[:, 768:]
-                gin_ref[0, :, pl.ds(pl.multiple_of(1536 + (1 - core) * 256, 128), 256)] = other[:, 768:]
-            return
-        send(k, step)
+                put(gin_ref, 0, 768, 0)
 
     def code_copy(c):
         return pltpu.make_async_remote_copy(
@@ -656,8 +715,6 @@
             recv_sem=recv_sems.at[N_SEM - 2 + c], device_id=sec_dev, device_id_type=MESH,
         )
 
-    for load in loads:
-        load.wait()
     ag_start(0)
 
     @pl.when(is_e)
@@ -675,8 +732,14 @@
                 + (inner & 7)
             )
             s.perm[c] = (source == cols_i).astype(F32).astype(BF)
+        loads[0].wait()
+        loads[1].wait()
 
         def forward(c, carry):
+            @pl.when(c == 1)
+            def _():
+                loads[4].wait()
+
             for f in range(2):
                 rows = slice(GRID * f, GRID * f + GRID)
                 norm_qkv(c, rows, nn(s.perm[c], s.xs[c, rows]))
@@ -686,13 +749,22 @@
                 ag_wait(0)
                 ag_start(1)
 
-            window_forward(c)
+            window_forward(c, 0)
 
             @pl.when(c == 0)
             def _():
                 ag_wait(1)
                 ag_start(2)
 
+            window_forward(c, 1)
+
+            @pl.when(c == 0)
+            def _():
+                ag_wait(2)
+                ag_start(3)
+                loads[2].wait()
+                loads[3].wait()
+
             def put(rows, acc):
                 s.eb[c, rows] = acc.astype(BF)
 
@@ -700,13 +772,11 @@
 
             @pl.when(c == 0)
             def _():
-                ag_wait(2)
-                ag_start(3)
                 ag_wait(3)
 
             entries(c)
             entry = s.ent[c]
-            vec = tt(proj_ref[0], s.eb[c])
+            vec = nt(proj_t, s.eb[c])
             for f in range(2):
                 cols = slice(GRID * f, GRID * f + GRID)
                 entry_enc = nt(pad16(entry[:, cols]), s.perm[c])[0:8]
@@ -725,6 +795,8 @@
                 ag_start(step + 1)
         for c in range(2):
             entries(c)
+        for load in loads:
+            load.wait()
 
         def both(c, carry):
             code_copy(c).wait_recv()
@@ -732,14 +804,15 @@
             s.cvec[c] = pad16(quant)
             for f in range(2):
                 rows = slice(GRID * f, GRID * f + GRID)
-                h = tt(s.cvec[c][0:8, rows], proj_ref[0])
+                h = tn(s.cvec[c][0:8, rows], proj_t)
                 norm_qkv(c, rows, h)
             frames_forward(c)
 
             def put(rows, acc):
-                bout_ref[0, pl.ds(c * CLIP + rows.start, rows.size), :] = acc.astype(BF)
+                s.bo[pl.ds(c * CLIP + rows.start, rows.size), :] = acc.astype(BF)
 
             feed_forward(c, put)
+            bout_copy(c).start()
             back_ff(c, lambda rows: s.xs[c, rows].astype(F32))
             frames_backward(c)
 
@@ -747,50 +820,88 @@
                 s.eb[c, rows] = acc.astype(BF)
 
             back_in(c, put_back)
-            grad_code = tt(proj_ref[0], s.eb[c])
-            s.cxs[c] = pad16(grad_code)
+            s.cxs[c] = pad16(nt(proj_t, s.eb[c]))
             code_copy(c).start()
-            book_proj_terms(
-                c, s.cxs[c][0:8].astype(F32), s.eb[c], s.cvec[c][0:8].astype(F32)
-            )
             return carry
 
         lax.fori_loop(0, 2, both, 0)
 
-    def last(c, carry):
-        @pl.when(is_e)
-        def _():
+        def downs(c, carry):
+            grad_down(c)
+            return carry
+
+        lax.fori_loop(0, 2, downs, 0)
+        reduce_step("a", 0)
+
+        def ups(c, carry):
+            grad_up(c)
+
+            @pl.when(c == 0)
+            def _():
+                reduce_step("a", 1)
+
+            return carry
+
+        lax.fori_loop(0, 2, ups, 0)
+        reduce_step("b", 0)
+        reduce_step("a", 2)
+
+        def attns(c, carry):
+            grad_attn(c)
+
+            @pl.when(c == 0)
+            def _():
+                reduce_step("b", 1)
+
+            return carry
+
+        lax.fori_loop(0, 2, attns, 0)
+        reduce_step("c", 0)
+        reduce_step("a", 3)
+        reduce_step("b", 2)
+        for c in range(2):
+            book_proj_terms(c, s.cxs[c][0:8].astype(F32), s.eb[c], s.cvec[c][0:8].astype(F32))
+
+    @pl.when(is_e)
+    def _():
+        def backward(c, carry):
             code_copy(c).wait_recv()
             for f in range(2):
                 cols = slice(GRID * f, GRID * f + GRID)
                 s.cvec[c, :, cols] = nt(s.cxr[c, :, cols], s.perm[c]).astype(BF)
-            g = tt(s.cvec[c][0:8], proj_ref[0])
-            s.gg[...] = g
+            g = tn(s.cvec[c][0:8], proj_t)
+            s.hb[...] = g
             s.xs[c] = g.astype(BF)
-            book_proj_terms(
-                c, s.cxr[c][0:8].astype(F32), s.eb[c], s.cvec[c][0:8].astype(F32)
-            )
-
-        grad_down(c)
-
-        @pl.when(c == 1)
-        def _():
-            reduce_step("a", 0)
-
-        @pl.when(is_e)
-        def _():
-            back_ff(c, lambda rows: s.gg[rows])
-
-        grad_up(c)
-
-        @pl.when(c == 1)
-        def _():
-            reduce_step("b", 0)
-            reduce_step("a", 1)
-
-        @pl.when(is_e)
-        def _():
-            window_backward(c)
+            grad_down(c)
+
+            @pl.when(c == 1)
+            def _():
+                reduce_step("a", 0)
+
+            back_ff(c, lambda rows: s.hb[rows])
+
+            @pl.when(c == 1)
+            def _():
+                reduce_step("a", 1)
+
+            grad_up(c)
+
+            @pl.when(c == 1)
+            def _():
+                reduce_step("b", 0)
+                reduce_step("a", 2)
+
+            window_backward(c, 0)
+
+            @pl.when(c == 1)
+            def _():
+                reduce_step("b", 1)
+
+            window_backward(c, 1)
+
+            @pl.when(c == 1)
+            def _():
+                reduce_step("a", 3)
 
             def put_back(rows, acc):
                 s.gob[rows] = acc.astype(BF)
@@ -798,14 +909,21 @@
             back_in(c, put_back)
             for f in range(2):
                 back = tn(s.perm[c], s.gob[GRID * f : GRID * f + GRID])
-                bout_ref[0, pl.ds(c * CLIP + GRID * f, GRID), :] = back.astype(BF)
-
-        grad_attn(c)
-        return carry
-
-    lax.fori_loop(0, 2, last, 0)
-
-    reduce_step("c", 0)
+                s.bo[pl.ds(c * CLIP + GRID * f, GRID), :] = back.astype(BF)
+            bout_copy(c).start()
+            grad_attn(c)
+
+            @pl.when(c == 1)
+            def _():
+                reduce_step("c", 0)
+                reduce_step("b", 2)
+
+            book_proj_terms(c, s.cxr[c][0:8].astype(F32), s.eb[c], s.cvec[c][0:8].astype(F32))
+            return carry
+
+        lax.fori_loop(0, 2, backward, 0)
+
+    reduce_step("c", 1)
     sums = jnp.concatenate(
         [
             jnp.sum(s.gacc[0], axis=0, keepdims=True),
@@ -817,8 +935,7 @@
     wide_sums = jnp.concatenate([jnp.zeros((72, D), F32), sums, jnp.zeros((48, D), F32)], axis=0)
     s.s_acc[...] += jnp.transpose(wide_sums).reshape(4, 8, 2, 8, 128)
     order = [
-        "s0", "b1", "c1", "s1", "a2", "b2", "s2", "c2", "a3", "s3", "b3", "c3", "a4", "b4", "s4", "c4",
-        "a5", "b5", "c5",
+        "s0", "a4", "b3", "s1", "c2", "a5", "s2", "c3", "b4", "s3", "a6", "b5", "c4", "s4", "b6", "c5", "c6",
     ]
     for item in order:
         reduce_step(item[0], int(item[1]))
@@ -829,8 +946,9 @@
 
     for c in range(2):
         code_copy(c).wait_send()
+        bout_copy(c).wait()
     for k in ("a", "b", "c", "s"):
-        for step in range(5):
+        for step in range(4 if k == "s" else 7):
             for cp in copies(k, step):
                 cp.wait_send()
 
@@ -845,28 +963,54 @@
         jax.ShapeDtypeStruct(boundary.shape, BF),
         jax.ShapeDtypeStruct(avg_in.shape, F32),
         jax.ShapeDtypeStruct(avg_down.shape, F32),
-        jax.ShapeDtypeStruct((1, 2, 8), F32),
-        jax.ShapeDtypeStruct((1, 8, 8), F32),
-        jax.ShapeDtypeStruct(codebook.shape, F32),
+        jax.ShapeDtypeStruct((8, 128), F32),
         jax.ShapeDtypeStruct(avg_in.shape, F32),
         jax.ShapeDtypeStruct(avg_down.shape, F32),
     )
     scratch = [pltpu.VMEM(shape, dtype) for shape, dtype in SHAPES.values()]
-    scratch += [pltpu.SemaphoreType.DMA((N_SEM,)), pltpu.SemaphoreType.DMA((N_SEM,)), pltpu.SemaphoreType.DMA((4,))]
-    return pl.pallas_call(
+    scratch += [pltpu.SemaphoreType.DMA((N_SEM,)), pltpu.SemaphoreType.DMA((N_SEM,)), pltpu.SemaphoreType.DMA((8,))]
+    made = pl.pallas_call(
         mega,
         out_shape=outs,
         in_specs=[hbm, hbm, hbm, vmem, vmem, vmem, vmem, smem, smem, vmem, vmem],
-        out_specs=[vmem] * 8,
+        out_specs=[hbm] + [vmem] * 5,
         scratch_shapes=scratch,
         compiler_params=pltpu.CompilerParams(
             collective_id=0, has_side_effects=True, vmem_limit_bytes=63 << 20
         ),
         name="both_sections",
     )(
-        boundary, in_weights, down_weight, gains, proj, codebook, codes.reshape(8, 128), grids, orders,
+        boundary, in_weights, down_weight, gains, proj[0].T, codebook, codes.reshape(8, 128), grids, orders,
         avg_in, avg_down,
     )
+    return pl.pallas_call(
+        split_outputs,
+        out_shape=(
+            outs[0], outs[1], outs[2],
+            jax.ShapeDtypeStruct((1, 2, 8), F32),
+            jax.ShapeDtypeStruct((1, 8, 8), F32),
+            jax.ShapeDtypeStruct(codebook.shape, F32),
+            outs[4], outs[5],
+        ),
+        in_specs=[vmem] * 6,
+        out_specs=[vmem] * 8,
+        name="split_outputs",
+    )(*made)
+
+
+def split_outputs(
+    bout_in, gin_in, gdn_in, small_in, ain_in, adn_in,
+    bout, gin, gdn, ggain, gproj, gbook, ain, adn,
+):
+    bout[...] = bout_in[...]
+    gin[...] = gin_in[...]
+    gdn[...] = gdn_in[...]
+    ain[...] = ain_in[...]
+    adn[...] = adn_in[...]
+    small = small_in[...]
+    gbook[...] = small[:, 0:64]
+    gproj[0] = small[:, 64:72]
+    ggain[0] = jnp.transpose(jnp.concatenate([small] * 16, axis=0))[72:74, 0:8]
 
 
 def solution(mesh):

time: 125 us -> 94 us (0.75)
  Pallas kernels: 110 us -> 93.1 us
  local copies, waits for them, and re-layouts: 13.6 us -> 0 us
    pallas_call x1, Pallas kernels: 110 us -> 90.6 us  [body(): pl.pallas_call(mega, out_shape=outs, in_specs=[hbm, hbm, hbm, vmem, vmem,...]
    unnamed x9 -> x0, local copies, waits for them, and re-layouts: 13.6 us -> none
    pallas_call x0 -> x1, Pallas kernels: none -> 2.44 us  [body(): pl.pallas_call(split_outputs, out_shape=(outs[0], outs[1], outs[2], jax.S...]
where the time goes in v2:
time: 94 us; the launch traced here: 93.8 us
  Pallas kernels  93.1 us (99%)
    pallas_call x1, Pallas kernels, body(): pl.pallas_call(mega, out_shape=outs, in_specs=[hbm, hbm, hbm, vmem, vmem,...  90.6 us
    pallas_call x1, Pallas kernels, body(): pl.pallas_call(split_outputs, out_shape=(outs[0], outs[1], outs[2], jax.S...  2.44 us

profile of v2, /device:TPU:1, one launch (start us, length us, event | category | flops | bytes accessed | tf_op | source)
XLA Modules:
  0.0 93.8 jit_solution(13639017851329634027)
XLA Ops:
  0.6 90.6 %both_sections.1 = (bf16[1,1024,512]{2,1,0:T(8,128)(2,1)}, f32[1,8,4096]{2,1,0:T(8,128)}, f32[1,32,512]{2,1,0:T(8,128)}, f32[8,128]{1,0:T(8,128)}, f32[1,8,4096]{2,1,0:T(8,128)}, /*index=5*/f32[1,32,512]{2,1,0:T(8,128)}) custom-call(bf16[1,1024,512]{2,1,0:T(8,128)(2,1)} %x_hbm.1, bf16[1,512,4096]{2,1,0:T(8,128)(2,1)} %win_hbm.1, ...), custom_call_target="tpu_custom_call" | custom-call | tf_op jit(solution)/shard_map/both_sections/pallas_call | solution.py:972
  91.3 2.4 %split_outputs.1 = (bf16[1,1024,512]{2,1,0:T(8,128)(2,1)}, f32[1,8,4096]{2,1,0:T(8,128)}, f32[1,32,512]{2,1,0:T(8,128)}, f32[1,2,8]{2,1,0:T(2,128)}, f32[1,8,8]{...) custom-call(bf16[1,1024,512]{2,1,0:T(8,128)(2,1)} %get-tuple-element.14.bout_in, ...), custom_call_target="tpu_custom_call" | custom-call | tf_op jit(solution)/shard_map/split_outputs/pallas_call | solution.py:986

commit v3 on v2

--- a/solution.py
+++ b/solution.py
@@ -22,10 +22,9 @@
 AVG_DECAY = 0.9
 LEARN_RATE = 0.0005
 SCALE = 0.125
-RC = 512
 WB = 4
 
-CHUNKS = {"a": (128, 256), "b": (32, 1280), "c": (32, 768)}
+CHUNKS = {"a": (32, 512), "b": (16, 1024), "c": (16, 1024)}
 
 
 def nn(left, right):
@@ -82,11 +81,14 @@
         "bd1": ((256, 256), BF),
         "bds": ((256, 256), BF),
         "bdf": ((256, 256), F32),
-        "tbl": ((64, 8, 128), F32),
+        "tbl": ((32, 2, 16, 128), BF),
+        "pre": ((2, 2, 8, 128), F32),
         "cds": ((2, 8, CLIP), I32),
         "cxs": ((2, 16, CLIP), BF),
         "cxr": ((2, 16, CLIP), BF),
-        "ent": ((2, 8, CLIP), F32),
+        "fcs": ((2, 8, CLIP), F32),
+        "fcr": ((2, 8, CLIP), F32),
+        "ent": ((2, 2, 8, CLIP), F32),
         "cvec": ((2, 16, CLIP), BF),
         "hb": ((CLIP, D), F32),
         "bo": ((2 * CLIP, D), BF),
@@ -112,28 +114,24 @@
         "gacc": ((2, 8, D), F32),
         "s0": ((4, 8, 8, 128), F32),
         "s1": ((3, 8, 8, 128), F32),
-        "s2": ((3, 2, 8, 128), F32),
-        "s3": ((8, 128), F32),
+        "s2": ((7, 8, 128), F32),
     }
     for k, (rows, w) in CHUNKS.items():
         h = w // 2
-        half = rows // 2
-        shapes["sb0" + k] = ((4, 4, 2, half, w), BF)
-        shapes["r0" + k] = ((4, 4, 2, half, w), BF)
+        shapes["sb0" + k] = ((4, 4, 2, rows, w), BF)
+        shapes["r0" + k] = ((4, 4, 2, rows, w), BF)
         for ax in "zx":
-            for slot in "012":
-                shapes["q" + slot + ax + k] = ((2, 4, half, h), BF)
-            shapes["r2" + ax + k] = ((3, 2, half, h), BF)
-        shapes["t3" + k] = ((2, half, w), F32)
-        shapes["sb3" + k] = ((half, w), BF)
-        shapes["r3" + k] = ((half, w), BF)
-        shapes["t4" + k] = ((half, w), F32)
-        shapes["r4" + k] = ((half // 2, w), F32)
+            if k == "c":
+                shapes["q" + ax + k] = ((3, 4, 2, rows, h), BF)
+            else:
+                for slot in "012":
+                    shapes["q" + slot + ax + k] = ((2, 4, rows, h), BF)
+            shapes["p" + ax + k] = ((7, rows, h), BF)
     return shapes
 
 
 SHAPES = ten_shapes()
-N_SEM = 120
+N_SEM = 130
 
 
 class Refs:
@@ -172,6 +170,10 @@
     z_dev = [place((z + d) % 4, x, yh, core) for d in (1, 2, 3)]
     x_dev = [place(z, (x + d) % 4, yh, core) for d in (1, 2, 3)]
     sec_dev = (1 - sec, dp)
+    sec_core_dev = (1 - sec, dp + 1 - 2 * core)
+    around = [(d, y) for d in range(4) for y in range(2) if d + y > 0]
+    zy_dev = [place((z + d) % 4, x, (yh + y) % 2, core) for d, y in around]
+    xy_dev = [place(z, (x + d) % 4, (yh + y) % 2, core) for d, y in around]
 
     counter = [0]
     slots = {}
@@ -203,7 +205,7 @@
         return pltpu.make_async_copy(s.bo.at[rows], bout_hbm.at[0, rows], load_sems.at[5 + c])
 
     barrier = pltpu.get_barrier_semaphore()
-    peers = [core_dev, y_dev, sec_dev] + z_dev + x_dev
+    peers = [core_dev, sec_dev, sec_core_dev] + zy_dev + xy_dev[1:]
     for dev in peers:
         pl.semaphore_signal(barrier, inc=1, device_id=dev, device_id_type=MESH)
 
@@ -215,56 +217,70 @@
     s.bds[...] = (same * SCALE).astype(BF)
     for c in range(2):
         code_row = jnp.concatenate([codes_ref[4 * c + k : 4 * c + k + 1, :] for k in range(4)], axis=1)
-        s.cds[c] = jnp.broadcast_to(code_row - sec * HALF, (8, CLIP))
+        s.cds[c] = jnp.broadcast_to(code_row, (8, CLIP))
 
     proj_t = proj_ref[...]
     gain_one = gains_ref[0, 0:1, :].astype(F32)
     gain_two = gains_ref[0, 1:2, :].astype(F32)
     book = book_ref[...].astype(F32)
-    s.tbl[dp] = jnp.concatenate([book, jnp.zeros((8, 64), F32)], axis=1)
+    s.pre[sec, core] = jnp.concatenate([book, jnp.zeros((8, 64), F32)], axis=1)
     s.gacc[...] = jnp.zeros((2, 8, D), F32)
     s.s_acc[...] = jnp.zeros((4, 8, 2, 8, 128), F32)
 
     pl.semaphore_wait(barrier, len(peers))
 
-    def ag_copies(step):
-        if step == 0:
-            part = s.tbl.at[dp]
-            return [rcopy("ag0", part, part, core_dev)]
-        if step == 1:
-            part = s.tbl.at[pl.ds((dp // 2) * 2, 2)]
-            return [rcopy("ag1", part, part, y_dev)]
-        if step == 2:
-            part = s.tbl.at[pl.ds((dp // 4) * 4, 4)]
-            return [rcopy("ag2%d" % i, part, part, x_dev[i]) for i in range(3)]
-        part = s.tbl.at[pl.ds((dp // 16) * 16, 16)]
-        return [rcopy("ag3%d" % i, part, part, z_dev[i]) for i in range(3)]
-
-    def ag_arrivals(step):
-        if step == 0:
-            part = s.tbl.at[dp + 1 - 2 * core]
-            return [rcopy("ag0", part, part, core_dev)]
-        if step == 1:
-            part = s.tbl.at[pl.ds((dp // 4) * 4 + (1 - yh) * 2, 2)]
-            return [rcopy("ag1", part, part, y_dev)]
-        if step == 2:
-            parts = [s.tbl.at[pl.ds(z * 16 + ((x + 3 - i) % 4) * 4, 4)] for i in range(3)]
-            return [rcopy("ag2%d" % i, parts[i], parts[i], x_dev[i]) for i in range(3)]
-        parts = [s.tbl.at[pl.ds(((z + 3 - i) % 4) * 16, 16)] for i in range(3)]
-        return [rcopy("ag3%d" % i, parts[i], parts[i], z_dev[i]) for i in range(3)]
-
-    def ag_start(step):
-        for cp in ag_copies(step):
-            cp.start()
-
-    def ag_wait(step):
-        for cp in ag_arrivals(step):
-            cp.wait_recv()
-        for cp in ag_copies(step):
-            cp.wait_send()
-
-    def onehots(c):
-        code_row = s.cds[c][0:1, :]
+    def book_start():
+        mine = s.pre.at[sec, core]
+
+        @pl.when(is_e)
+        def _():
+            rcopy("ag0", mine, mine, sec_dev).start()
+            rcopy("ag1", mine, mine, sec_core_dev).start()
+
+        @pl.when(is_d)
+        def _():
+            rcopy("ag2", mine, mine, core_dev).start()
+
+    def gather_book():
+        chip = dp // 2
+        rcopy("ag0", s.pre.at[0, core], s.pre.at[0, core], sec_dev).wait_recv()
+        rcopy("ag1", s.pre.at[0, 1 - core], s.pre.at[0, 1 - core], sec_core_dev).wait_recv()
+        rcopy("ag2", s.pre.at[1, 1 - core], s.pre.at[1, 1 - core], core_dev).wait_recv()
+        for half in range(2):
+            s.tbl[chip, half] = jnp.concatenate([s.pre[half, 0], s.pre[half, 1]], axis=0).astype(BF)
+        part = s.tbl.at[chip]
+        for i in range(7):
+            rcopy("ag3%d" % i, part, part, xy_dev[i]).start()
+        for i, (d, y) in enumerate(around):
+            part = s.tbl.at[(z * 4 + (x + 4 - d) % 4) * 2 + (yh + 2 - y) % 2]
+            rcopy("ag3%d" % i, part, part, xy_dev[i]).wait_recv()
+        part = s.tbl.at[pl.ds(z * 8, 8)]
+        for i in range(3):
+            rcopy("ag4%d" % i, part, part, z_dev[i]).start()
+        for i in range(3):
+            part = s.tbl.at[pl.ds(((z + 3 - i) % 4) * 8, 8)]
+            rcopy("ag4%d" % i, part, part, z_dev[i]).wait_recv()
+
+    def book_finish():
+        mine = s.pre.at[sec, core]
+
+        @pl.when(is_e)
+        def _():
+            rcopy("ag0", mine, mine, sec_dev).wait_send()
+            rcopy("ag1", mine, mine, sec_core_dev).wait_send()
+
+        @pl.when(is_d)
+        def _():
+            rcopy("ag2", mine, mine, core_dev).wait_send()
+            part = s.tbl.at[dp // 2]
+            for i in range(7):
+                rcopy("ag3%d" % i, part, part, xy_dev[i]).wait_send()
+            part = s.tbl.at[pl.ds(z * 8, 8)]
+            for i in range(3):
+                rcopy("ag4%d" % i, part, part, z_dev[i]).wait_send()
+
+    def onehots(c, half):
+        code_row = s.cds[c][0:1, :] - half * HALF
         hi = code_row >> 6
         lo = code_row & 63
         lo_one = (iota((128, CLIP), 0) == lo).astype(F32).astype(BF)
@@ -272,16 +288,17 @@
         return lo_one, hi_mask
 
     def entries(c):
-        lo_one, hi_mask = onehots(c)
-        table = s.tbl[...].reshape(CLIP, 128).astype(BF)
-        picked = jnp.where(hi_mask, nn(table, lo_one), 0.0)
-        s.ent[c] = jnp.sum(picked.reshape(64, 8, CLIP), axis=0)
+        for half in range(2):
+            lo_one, hi_mask = onehots(c, half)
+            table = s.tbl[:, half].reshape(CLIP, 128)
+            picked = jnp.where(hi_mask, nn(table, lo_one), 0.0)
+            s.ent[c, half] = jnp.sum(picked.reshape(64, 8, CLIP), axis=0)
 
     def pad16(v):
         return jnp.concatenate([v, jnp.zeros((8, v.shape[1]), F32)], axis=0).astype(BF)
 
     def book_proj_terms(c, code_grad, wide_rows, narrow):
-        lo_one, hi_mask = onehots(c)
+        lo_one, hi_mask = onehots(c, sec)
         spread = jnp.broadcast_to(code_grad[None], (64, 8, CLIP)).reshape(CLIP, CLIP)
         left = jnp.where(hi_mask, spread, 0.0).astype(BF)
         total = nt(left, lo_one)
@@ -291,40 +308,35 @@
         total = total + tt(wide_rows, narrow_wide)
         s.s_acc[...] += total.reshape(4, 8, 2, 8, 128)
 
-    def norm_qkv(c, rows, h):
-        s.hb[rows] = h
+    def norm_qkv(c, h):
+        s.hb[...] = h
         xh, r = normed(h)
-        s.xh1[c, rows] = xh
-        s.r1[c, rows] = r
+        s.xh1[c] = xh
+        s.r1[c] = r
         a = (xh * gain_one).astype(BF)
-        s.a1[c, rows] = a
+        s.a1[c] = a
         for j in range(3):
-            s.qkv[c, rows, 512 * j : 512 * j + 512] = nn(a, s.win[:, 512 * j : 512 * j + 512]).astype(BF)
+            s.qkv[c, :, 512 * j : 512 * j + 512] = nn(a, s.win[:, 512 * j : 512 * j + 512]).astype(BF)
 
     def feed_forward(c, put):
-        def step(i, carry):
-            rows = pl.ds(i * RC, RC)
-            m = s.hb[rows] + nn(s.att[c, rows], s.win[:, 1536:2048])
-            xh, r = normed(m)
-            s.xh2[c, rows] = xh
-            s.r2[c, rows] = r
-            a = (xh * gain_two).astype(BF)
-            s.a2[c, rows] = a
-            acc = m
-            nxt = nn(a, s.win[:, 2048:2304])
-            for j in range(8):
-                cols = slice(256 * j, 256 * j + 256)
-                u = nxt
-                if j < 7:
-                    nxt = nn(a, s.win[:, 2304 + 256 * j : 2560 + 256 * j])
-                value, slope = gelu_pair(u.astype(BF))
-                s.act[c, rows, cols] = value
-                s.gel[c, rows, cols] = slope
-                acc = acc + nn(value, s.wdn[cols, :])
-            put(rows, acc)
-            return carry
-
-        lax.fori_loop(0, CLIP // RC, step, 0)
+        m = s.hb[...] + nn(s.att[c], s.win[:, 1536:2048])
+        xh, r = normed(m)
+        s.xh2[c] = xh
+        s.r2[c] = r
+        a = (xh * gain_two).astype(BF)
+        s.a2[c] = a
+        acc = m
+        nxt = nn(a, s.win[:, 2048:2304])
+        for j in range(8):
+            cols = slice(256 * j, 256 * j + 256)
+            u = nxt
+            if j < 7:
+                nxt = nn(a, s.win[:, 2304 + 256 * j : 2560 + 256 * j])
+            value, slope = gelu_pair(u.astype(BF))
+            s.act[c, :, cols] = value
+            s.gel[c, :, cols] = slope
+            acc = acc + nn(value, s.wdn[cols, :])
+        put(acc)
 
     def units(c, w, count):
         out = []
@@ -462,42 +474,34 @@
         part = jnp.sum((grad * xhat).reshape(-1, 8, D), axis=0)
         s.gacc[which] += part
 
-    def back_ff(c, grad_of):
-        def step(i, carry):
-            rows = pl.ds(i * RC, RC)
-            gz = s.xs[c, rows]
-            acc = None
-            for j in range(4):
-                cols = slice(512 * j, 512 * j + 512)
-                gu = (nt(gz, s.wdn[cols, :]) * s.gel[c, rows, cols].astype(F32)).astype(BF)
-                s.gel[c, rows, cols] = gu
-                term = nt(gu, s.win[:, 2048 + 512 * j : 2560 + 512 * j])
-                acc = term if acc is None else acc + term
-            xh = s.xh2[c, rows]
-            gain_terms(1, acc, xh)
-            gm = grad_of(rows) + normed_back(acc, xh, s.r2[c, rows], gain_two)
-            s.hb[rows] = gm
-            gy = gm.astype(BF)
-            s.gy[c, rows] = gy
-            s.gob[rows] = nt(gy, s.win[:, 1536:2048]).astype(BF)
-            return carry
-
-        lax.fori_loop(0, CLIP // RC, step, 0)
-
-    def back_in(c, put):
-        def step(i, carry):
-            rows = pl.ds(i * RC, RC)
-            acc = None
-            for j in range(3):
-                cols = slice(512 * j, 512 * j + 512)
-                term = nt(s.qkv[c, rows, cols], s.win[:, cols])
-                acc = term if acc is None else acc + term
-            xh = s.xh1[c, rows]
-            gain_terms(0, acc, xh)
-            put(rows, s.hb[rows] + normed_back(acc, xh, s.r1[c, rows], gain_one))
-            return carry
-
-        lax.fori_loop(0, CLIP // RC, step, 0)
+    def back_down(c):
+        gz = s.xs[c]
+        for j in range(4):
+            cols = slice(512 * j, 512 * j + 512)
+            s.gel[c, :, cols] = (nt(gz, s.wdn[cols, :]) * s.gel[c, :, cols].astype(F32)).astype(BF)
+
+    def back_up(c, grad_of):
+        acc = None
+        for j in range(4):
+            term = nt(s.gel[c, :, 512 * j : 512 * j + 512], s.win[:, 2048 + 512 * j : 2560 + 512 * j])
+            acc = term if acc is None else acc + term
+        xh = s.xh2[c]
+        gain_terms(1, acc, xh)
+        gm = grad_of() + normed_back(acc, xh, s.r2[c], gain_two)
+        s.hb[...] = gm
+        gy = gm.astype(BF)
+        s.gy[c] = gy
+        s.gob[...] = nt(gy, s.win[:, 1536:2048]).astype(BF)
+
+    def back_in(c):
+        acc = None
+        for j in range(3):
+            cols = slice(512 * j, 512 * j + 512)
+            term = nt(s.qkv[c, :, cols], s.win[:, cols])
+            acc = term if acc is None else acc + term
+        xh = s.xh1[c]
+        gain_terms(0, acc, xh)
+        return s.hb[...] + normed_back(acc, xh, s.r1[c], gain_one)
 
     def add_into(ref, rows, cols, c, value):
         ref[rows, cols] = jnp.where(c == 0, value, ref[rows, cols] + value)
@@ -512,29 +516,26 @@
             cols = slice(512 * j, 512 * j + 512)
             add_into(s.acc_up, slice(None), cols, c, tn(s.a2[c], s.gel[c, :, cols]))
 
-        add_into(s.acc_out, slice(None), slice(None), c, tn(s.att[c], s.gy[c]))
-
     def grad_attn(c):
         for j in range(3):
             cols = slice(512 * j, 512 * j + 512)
             add_into(s.acc_qkv, slice(None), cols, c, tn(s.a1[c], s.qkv[c, :, cols]))
-
-    def load_half(k, i, half):
+        add_into(s.acc_out, slice(None), slice(None), c, tn(s.att[c], s.gy[c]))
+
+    def share(k, i, to_core):
+        n = 2 * i + to_core
         if k == "a":
-            v = s.acc_dn[pl.ds(i * 128, 128), pl.ds(pl.multiple_of(half * 256, 128), 256)]
-            return v.reshape(2, 64, 256)
-        rows = pl.ds(i * 32, 32)
-        if k == "c":
-            v = s.acc_qkv[rows, pl.ds(pl.multiple_of(half * 768, 128), 768)]
-            return v.reshape(2, 16, 768)
-        v = jnp.concatenate(
+            return s.acc_dn[pl.ds(pl.multiple_of(n * 32, 32), 32), :]
+        rows = pl.ds(pl.multiple_of(n * 8, 8), 8)
+        if k == "b":
+            return jnp.concatenate([s.acc_up[rows, 0:1024], s.acc_up[rows, 1024:2048]], axis=0)
+        return jnp.concatenate(
             [
-                s.acc_up[rows, pl.ds(pl.multiple_of(half * 1024, 128), 1024)],
-                s.acc_out[rows, pl.ds(pl.multiple_of(half * 256, 128), 256)],
+                jnp.concatenate([s.acc_qkv[rows, 0:768], s.acc_out[rows, 0:256]], axis=1),
+                jnp.concatenate([s.acc_qkv[rows, 768:1536], s.acc_out[rows, 256:512]], axis=1),
             ],
-            axis=1,
+            axis=0,
         )
-        return v.reshape(2, 16, 1280)
 
     def buf(name, k):
         return getattr(s, name + k)
@@ -545,14 +546,12 @@
                 return [rcopy("s0", s.s_acc.at[:, :, 1 - core], s.s0, core_dev)]
             if step == 1:
                 return [rcopy("s1%d" % i, s.s0.at[(z + 1 + i) % 4], s.s1.at[i], z_dev[i]) for i in range(3)]
-            if step == 2:
-                return [
-                    rcopy("s2%d" % i, s.s0.at[z, pl.ds(2 * ((x + 1 + i) % 4), 2)], s.s2.at[i], x_dev[i])
-                    for i in range(3)
-                ]
-            if step == 3:
-                return [rcopy("s3", s.s0.at[z, 2 * x + 1 - yh], s.s3, y_dev)]
-            return []
+            return [
+                rcopy(
+                    "s2%d" % i, s.s0.at[z, 2 * ((x + d) % 4) + (yh + y) % 2], s.s2.at[i], xy_dev[i]
+                )
+                for i, (d, y) in enumerate(around)
+            ]
         rows, w = CHUNKS[k]
         h = w // 2
         r0 = buf("r0", k)
@@ -560,42 +559,48 @@
             return [rcopy(k + "0", buf("sb0", k), r0, core_dev)]
         lo, hi = pl.ds(0, h), pl.ds(h, h)
         out = []
-        if step in (1, 2, 3):
-            for y in range(2):
-                first, second = ((1, 3), (3, 1))[y]
-                hop = second if step == 3 else first
-                block = {1: 2, 2: first, 3: second}[step]
-                slot = {1: "q1", 2: "q0", 3: "q2"}[step]
+        if step == 4:
+            for i, (d, y) in enumerate(around):
                 out.append(
                     rcopy(
-                        "%s%dz%d" % (k, step, y), r0.at[z_flip[block], :, y, :, lo],
-                        buf(slot + "z", k).at[y], place(z_flip[hop], x, yh, core),
+                        "%s4x%d" % (k, i), r0.at[z, (x + d) % 4, (yh + y) % 2, :, lo],
+                        buf("px", k).at[i], xy_dev[i],
                     )
                 )
                 out.append(
                     rcopy(
-                        "%s%dx%d" % (k, step, y), r0.at[:, x_flip[block], y, :, hi],
-                        buf(slot + "x", k).at[y], place(z, x_flip[hop], yh, core),
+                        "%s4z%d" % (k, i), r0.at[(z + d) % 4, x, (yh + y) % 2, :, hi],
+                        buf("pz", k).at[i], zy_dev[i],
                     )
                 )
             return out
-        if step == 4:
+        if k == "c":
             for i in range(3):
                 out.append(
-                    rcopy(
-                        "%s4x%d" % (k, i), r0.at[z, (x + 1 + i) % 4, :, :, lo], buf("r2x", k).at[i], x_dev[i]
-                    )
+                    rcopy("%s1z%d" % (k, i), r0.at[(z + 1 + i) % 4, :, :, :, lo], buf("qz", k).at[i], z_dev[i])
                 )
                 out.append(
-                    rcopy(
-                        "%s4z%d" % (k, i), r0.at[(z + 1 + i) % 4, x, :, :, hi], buf("r2z", k).at[i], z_dev[i]
-                    )
+                    rcopy("%s1x%d" % (k, i), r0.at[:, (x + 1 + i) % 4, :, :, hi], buf("qx", k).at[i], x_dev[i])
                 )
             return out
-        if step == 5:
-            return [rcopy(k + "5", buf("sb3", k), buf("r3", k), y_dev)]
-        quarter = rows // 4
-        return [rcopy(k + "6", buf("t4", k).at[pl.ds((1 - core) * quarter, quarter)], buf("r4", k), core_dev)]
+        for y in range(2):
+            first, second = ((1, 3), (3, 1))[y]
+            hop = second if step == 3 else first
+            block = {1: 2, 2: first, 3: second}[step]
+            slot = {1: "q1", 2: "q0", 3: "q2"}[step]
+            out.append(
+                rcopy(
+                    "%s%dz%d" % (k, step, y), r0.at[z_flip[block], :, y, :, lo],
+                    buf(slot + "z", k).at[y], place(z_flip[hop], x, yh, core),
+                )
+            )
+            out.append(
+                rcopy(
+                    "%s%dx%d" % (k, step, y), r0.at[:, x_flip[block], y, :, hi],
+                    buf(slot + "x", k).at[y], place(z, x_flip[hop], yh, core),
+                )
+            )
+        return out
 
     def arrived(k, step):
         for cp in copies(k, step):
@@ -604,6 +609,12 @@
     def send(k, step):
         for cp in copies(k, step):
             cp.start()
+
+    def total(parts):
+        parts = [v.astype(F32) for v in parts]
+        while len(parts) > 1:
+            parts = [a + b for a, b in zip(parts[::2], parts[1::2])] + parts[len(parts) // 2 * 2 :]
+        return parts[0]
 
     def reduce_step(k, step):
         if k == "s":
@@ -614,23 +625,20 @@
             elif step == 2:
                 s.s0[z] += (s.s1[0] + s.s1[1]) + s.s1[2]
             elif step == 3:
-                here = pl.ds(2 * x, 2)
-                s.s0[z, here] += (s.s2[0] + s.s2[1]) + s.s2[2]
-            elif step == 4:
-                small_ref[...] = s.s0[z, 2 * x + yh] + s.s3[...]
+                small_ref[...] = total([s.s0[z, 2 * x + yh]] + [s.s2[i] for i in range(7)])
                 return
             send(k, step)
             return
         rows, w = CHUNKS[k]
         h = w // 2
-        half = rows // 2
         r0 = buf("r0", k)
         lo, hi = pl.ds(0, h), pl.ds(h, h)
         if step == 0:
             sb0 = buf("sb0", k)
 
             def body(i, carry):
-                sb0[i // 4, i % 4] = load_half(k, i, 1 - core).astype(BF)
+                for y in range(2):
+                    sb0[i // 4, i % 4, y] = share(k, 2 * i + y, 1 - core).astype(BF)
                 return carry
 
             lax.fori_loop(0, 16, body, 0)
@@ -639,83 +647,69 @@
             arrived(k, 0)
 
             def body(i, carry):
-                r0[i // 4, i % 4] = (load_half(k, i, core) + r0[i // 4, i % 4].astype(F32)).astype(BF)
+                for y in range(2):
+                    r0[i // 4, i % 4, y] = total([share(k, 2 * i + y, core), r0[i // 4, i % 4, y]]).astype(BF)
                 return carry
 
             lax.fori_loop(0, 16, body, 0)
             send(k, 1)
-            send(k, 2)
+            if k != "c":
+                send(k, 2)
         elif step == 2:
             arrived(k, 1)
             for y in range(2):
                 second = (3, 1)[y]
                 zb, xb = z_flip[second], x_flip[second]
-                r0[zb, :, y, :, lo] = (
-                    r0[zb, :, y, :, lo].astype(F32) + buf("q1z", k)[y].astype(F32)
-                ).astype(BF)
-                r0[:, xb, y, :, hi] = (
-                    r0[:, xb, y, :, hi].astype(F32) + buf("q1x", k)[y].astype(F32)
-                ).astype(BF)
+                r0[zb, :, y, :, lo] = total([r0[zb, :, y, :, lo], buf("q1z", k)[y]]).astype(BF)
+                r0[:, xb, y, :, hi] = total([r0[:, xb, y, :, hi], buf("q1x", k)[y]]).astype(BF)
             send(k, 3)
         elif step == 3:
-            arrived(k, 2)
-            arrived(k, 3)
-            for y in range(2):
-                r0[z, :, y, :, lo] = (
-                    r0[z, :, y, :, lo].astype(F32) + buf("q0z", k)[y].astype(F32)
-                    + buf("q2z", k)[y].astype(F32)
-                ).astype(BF)
-                r0[:, x, y, :, hi] = (
-                    r0[:, x, y, :, hi].astype(F32) + buf("q0x", k)[y].astype(F32)
-                    + buf("q2x", k)[y].astype(F32)
-                ).astype(BF)
+            if k == "c":
+                arrived(k, 1)
+                r0[z, :, :, :, lo] = total([r0[z, :, :, :, lo]] + [buf("qz", k)[i] for i in range(3)]).astype(BF)
+                r0[:, x, :, :, hi] = total([r0[:, x, :, :, hi]] + [buf("qx", k)[i] for i in range(3)]).astype(BF)
+            else:
+                arrived(k, 2)
+                arrived(k, 3)
+                for y in range(2):
+                    r0[z, :, y, :, lo] = total(
+                        [r0[z, :, y, :, lo], buf("q0z", k)[y], buf("q2z", k)[y]]
+                    ).astype(BF)
+                    r0[:, x, y, :, hi] = total(
+                        [r0[:, x, y, :, hi], buf("q0x", k)[y], buf("q2x", k)[y]]
+                    ).astype(BF)
             send(k, 4)
-        elif step == 4:
+        else:
             arrived(k, 4)
-            ra = buf("r2x", k)
-            rb = buf("r2z", k)
-            t3 = buf("t3", k)
-            t3[:, :, lo] = (r0[z, x, :, :, lo].astype(F32) + ra[0].astype(F32)) + (
-                ra[1].astype(F32) + ra[2].astype(F32)
-            )
-            t3[:, :, hi] = (r0[z, x, :, :, hi].astype(F32) + rb[0].astype(F32)) + (
-                rb[1].astype(F32) + rb[2].astype(F32)
-            )
-            buf("sb3", k)[...] = t3[1 - yh].astype(BF)
-            send(k, 5)
-        elif step == 5:
-            arrived(k, 5)
-            buf("t4", k)[...] = buf("t3", k)[yh] + buf("r3", k)[...].astype(F32)
-            send(k, 6)
-        else:
-            arrived(k, 6)
-            quarter = rows // 4
-            mine = buf("t4", k)[pl.ds(core * quarter, quarter), :]
-            other = buf("r4", k)[...]
-
-            def put(ref, start, width, part):
-                for c, v in ((core, mine), (1 - core, other)):
-                    ref[0, :, pl.ds(pl.multiple_of(start + c * width, 128), width)] = v[:, part : part + width]
-
+            left = total([r0[z, x, yh, :, lo]] + [buf("px", k)[i] for i in range(7)])
+            right = total([r0[z, x, yh, :, hi]] + [buf("pz", k)[i] for i in range(7)])
+            mine = jnp.concatenate([left, right], axis=1)
             if k == "a":
-                put(gdn_ref, 0, 256, 0)
+                gdn_ref[0] = mine
                 piece = s.wdn[pl.ds(dp * 32, 32), :].astype(F32)
-                adn_ref[0] = AVG_DECAY * avgdn_ref[0] + (1.0 - AVG_DECAY) * (
-                    piece - LEARN_RATE * gdn_ref[0]
-                )
+                adn_ref[0] = AVG_DECAY * avgdn_ref[0] + (1.0 - AVG_DECAY) * (piece - LEARN_RATE * mine)
             elif k == "b":
-                put(gin_ref, 2048, 1024, 0)
-                put(gin_ref, 1536, 256, 1024)
+                gin_ref[0, :, 2048:3072] = mine[0:8]
+                gin_ref[0, :, 3072:4096] = mine[8:16]
             else:
-                put(gin_ref, 0, 768, 0)
+                gin_ref[0, :, 0:768] = mine[0:8, :768]
+                gin_ref[0, :, 768:1536] = mine[8:16, :768]
+                gin_ref[0, :, 1536:1792] = mine[0:8, 768:]
+                gin_ref[0, :, 1792:2048] = mine[8:16, 768:]
 
     def code_copy(c):
         return pltpu.make_async_remote_copy(
-            src_ref=s.cxs.at[c], dst_ref=s.cxr.at[c], send_sem=send_sems.at[N_SEM - 2 + c],
+            src_ref=s.fcs.at[c], dst_ref=s.fcr.at[c], send_sem=send_sems.at[N_SEM - 2 + c],
             recv_sem=recv_sems.at[N_SEM - 2 + c], device_id=sec_dev, device_id_type=MESH,
         )
 
-    ag_start(0)
+    def grad_copy(c):
+        return pltpu.make_async_remote_copy(
+            src_ref=s.cxs.at[c], dst_ref=s.cxr.at[c], send_sem=send_sems.at[N_SEM - 4 + c],
+            recv_sem=recv_sems.at[N_SEM - 4 + c], device_id=sec_dev, device_id_type=MESH,
+        )
+
+    book_start()
 
     @pl.when(is_e)
     def _():
@@ -740,48 +734,28 @@
             def _():
                 loads[4].wait()
 
-            for f in range(2):
-                rows = slice(GRID * f, GRID * f + GRID)
-                norm_qkv(c, rows, nn(s.perm[c], s.xs[c, rows]))
+            raster = [s.xs[c, 0:GRID], s.xs[c, GRID:CLIP]]
+            norm_qkv(c, jnp.concatenate([nn(s.perm[c], v) for v in raster], axis=0))
+            window_forward(c, 0)
+            window_forward(c, 1)
 
             @pl.when(c == 0)
             def _():
-                ag_wait(0)
-                ag_start(1)
-
-            window_forward(c, 0)
-
-            @pl.when(c == 0)
-            def _():
-                ag_wait(1)
-                ag_start(2)
-
-            window_forward(c, 1)
-
-            @pl.when(c == 0)
-            def _():
-                ag_wait(2)
-                ag_start(3)
                 loads[2].wait()
                 loads[3].wait()
 
-            def put(rows, acc):
-                s.eb[c, rows] = acc.astype(BF)
+            def put(acc):
+                s.eb[c] = acc.astype(BF)
 
             feed_forward(c, put)
-
-            @pl.when(c == 0)
-            def _():
-                ag_wait(3)
-
-            entries(c)
-            entry = s.ent[c]
             vec = nt(proj_t, s.eb[c])
+            hi = vec.astype(BF).astype(F32)
+            mid = (vec - hi).astype(BF).astype(F32)
+            parts = jnp.concatenate([hi, mid, vec - hi - mid, jnp.zeros((8, CLIP), F32)], axis=0).astype(BF)
             for f in range(2):
                 cols = slice(GRID * f, GRID * f + GRID)
-                entry_enc = nt(pad16(entry[:, cols]), s.perm[c])[0:8]
-                sent = pad16(vec[:, cols] + entry_enc)
-                s.cxs[c, :, cols] = nn(sent, s.perm[c]).astype(BF)
+                moved = nn(parts[:, cols], s.perm[c])
+                s.fcs[c, :, cols] = (moved[0:8] + moved[8:16]) + moved[16:24]
             code_copy(c).start()
             return carry
 
@@ -789,10 +763,7 @@
 
     @pl.when(is_d)
     def _():
-        for step in range(4):
-            ag_wait(step)
-            if step < 3:
-                ag_start(step + 1)
+        gather_book()
         for c in range(2):
             entries(c)
         for load in loads:
@@ -800,28 +771,22 @@
 
         def both(c, carry):
             code_copy(c).wait_recv()
-            quant = s.cxr[c][0:8].astype(F32) + s.ent[c]
-            s.cvec[c] = pad16(quant)
-            for f in range(2):
-                rows = slice(GRID * f, GRID * f + GRID)
-                h = tn(s.cvec[c][0:8, rows], proj_t)
-                norm_qkv(c, rows, h)
+            sent = (s.fcr[c] + s.ent[c, 0]).astype(BF).astype(F32)
+            s.cvec[c] = pad16(sent + s.ent[c, 1])
+            norm_qkv(c, tn(s.cvec[c][0:8], proj_t))
             frames_forward(c)
 
-            def put(rows, acc):
-                s.bo[pl.ds(c * CLIP + rows.start, rows.size), :] = acc.astype(BF)
+            def put(acc):
+                s.bo[pl.ds(c * CLIP, CLIP), :] = acc.astype(BF)
 
             feed_forward(c, put)
             bout_copy(c).start()
-            back_ff(c, lambda rows: s.xs[c, rows].astype(F32))
+            back_down(c)
+            back_up(c, lambda: s.xs[c].astype(F32))
             frames_backward(c)
-
-            def put_back(rows, acc):
-                s.eb[c, rows] = acc.astype(BF)
-
-            back_in(c, put_back)
+            s.eb[c] = back_in(c).astype(BF)
             s.cxs[c] = pad16(nt(proj_t, s.eb[c]))
-            code_copy(c).start()
+            grad_copy(c).start()
             return carry
 
         lax.fori_loop(0, 2, both, 0)
@@ -844,28 +809,29 @@
 
         lax.fori_loop(0, 2, ups, 0)
         reduce_step("b", 0)
-        reduce_step("a", 2)
 
         def attns(c, carry):
             grad_attn(c)
 
             @pl.when(c == 0)
             def _():
+                reduce_step("a", 2)
                 reduce_step("b", 1)
 
             return carry
 
         lax.fori_loop(0, 2, attns, 0)
         reduce_step("c", 0)
-        reduce_step("a", 3)
         reduce_step("b", 2)
         for c in range(2):
             book_proj_terms(c, s.cxs[c][0:8].astype(F32), s.eb[c], s.cvec[c][0:8].astype(F32))
+        reduce_step("c", 1)
+        reduce_step("a", 3)
 
     @pl.when(is_e)
     def _():
         def backward(c, carry):
-            code_copy(c).wait_recv()
+            grad_copy(c).wait_recv()
             for f in range(2):
                 cols = slice(GRID * f, GRID * f + GRID)
                 s.cvec[c, :, cols] = nt(s.cxr[c, :, cols], s.perm[c]).astype(BF)
@@ -878,52 +844,50 @@
             def _():
                 reduce_step("a", 0)
 
-            back_ff(c, lambda rows: s.hb[rows])
+            back_down(c)
+            grad_up(c)
 
             @pl.when(c == 1)
             def _():
                 reduce_step("a", 1)
-
-            grad_up(c)
-
-            @pl.when(c == 1)
-            def _():
                 reduce_step("b", 0)
-                reduce_step("a", 2)
-
-            window_backward(c, 0)
+
+            back_up(c, lambda: s.hb[...])
 
             @pl.when(c == 1)
             def _():
                 reduce_step("b", 1)
 
-            window_backward(c, 1)
+            window_backward(c, 0)
 
             @pl.when(c == 1)
             def _():
-                reduce_step("a", 3)
-
-            def put_back(rows, acc):
-                s.gob[rows] = acc.astype(BF)
-
-            back_in(c, put_back)
+                reduce_step("a", 2)
+
+            window_backward(c, 1)
+            grad_attn(c)
+
+            @pl.when(c == 1)
+            def _():
+                reduce_step("c", 0)
+                reduce_step("b", 2)
+
+            s.gob[...] = back_in(c).astype(BF)
             for f in range(2):
                 back = tn(s.perm[c], s.gob[GRID * f : GRID * f + GRID])
                 s.bo[pl.ds(c * CLIP + GRID * f, GRID), :] = back.astype(BF)
             bout_copy(c).start()
-            grad_attn(c)
 
             @pl.when(c == 1)
             def _():
-                reduce_step("c", 0)
-                reduce_step("b", 2)
+                reduce_step("c", 1)
+                reduce_step("a", 3)
 
             book_proj_terms(c, s.cxr[c][0:8].astype(F32), s.eb[c], s.cvec[c][0:8].astype(F32))
             return carry
 
         lax.fori_loop(0, 2, backward, 0)
 
-    reduce_step("c", 1)
     sums = jnp.concatenate(
         [
             jnp.sum(s.gacc[0], axis=0, keepdims=True),
@@ -934,9 +898,7 @@
     )
     wide_sums = jnp.concatenate([jnp.zeros((72, D), F32), sums, jnp.zeros((48, D), F32)], axis=0)
     s.s_acc[...] += jnp.transpose(wide_sums).reshape(4, 8, 2, 8, 128)
-    order = [
-        "s0", "a4", "b3", "s1", "c2", "a5", "s2", "c3", "b4", "s3", "a6", "b5", "c4", "s4", "b6", "c5", "c6",
-    ]
+    order = ["s0", "b3", "s1", "c3", "a4", "s2", "b4", "c4", "s3"]
     for item in order:
         reduce_step(item[0], int(item[1]))
 
@@ -945,10 +907,19 @@
     ain_ref[0] = AVG_DECAY * avgin_ref[0] + (1.0 - AVG_DECAY) * (piece - LEARN_RATE * gin_ref[0])
 
     for c in range(2):
-        code_copy(c).wait_send()
         bout_copy(c).wait()
+
+        @pl.when(is_e)
+        def _():
+            code_copy(c).wait_send()
+
+        @pl.when(is_d)
+        def _():
+            grad_copy(c).wait_send()
+
+    book_finish()
     for k in ("a", "b", "c", "s"):
-        for step in range(4 if k == "s" else 7):
+        for step in {"s": (0, 1, 2), "c": (0, 1, 4)}.get(k, (0, 1, 2, 3, 4)):
             for cp in copies(k, step):
                 cp.wait_send()
 

time: 94 us -> 87 us (0.926)
  Pallas kernels: 93.1 us -> 85.8 us
    pallas_call x1, Pallas kernels: 90.6 us -> 83.3 us  [body(): pl.pallas_call(mega, out_shape=outs, in_specs=[hbm, hbm, hbm, vmem, vmem,...]
where the time goes in v3:
time: 87 us; the launch traced here: 86.5 us
  Pallas kernels  85.8 us (99%)
    pallas_call x1, Pallas kernels, body(): pl.pallas_call(mega, out_shape=outs, in_specs=[hbm, hbm, hbm, vmem, vmem,...  83.3 us
    pallas_call x1, Pallas kernels, body(): pl.pallas_call(split_outputs, out_shape=(outs[0], outs[1], outs[2], jax.S...  2.44 us

profile of v3, /device:TPU:1, one launch (start us, length us, event | category | flops | bytes accessed | tf_op | source)
XLA Modules:
  0.0 86.5 jit_solution(12183362654289809863)
XLA Ops:
  0.6 83.3 %both_sections.1 = (bf16[1,1024,512]{2,1,0:T(8,128)(2,1)}, f32[1,8,4096]{2,1,0:T(8,128)}, f32[1,32,512]{2,1,0:T(8,128)}, f32[8,128]{1,0:T(8,128)}, f32[1,8,4096]{2,1,0:T(8,128)}, /*index=5*/f32[1,32,512]{2,1,0:T(8,128)}) custom-call(bf16[1,1024,512]{2,1,0:T(8,128)(2,1)} %x_hbm.1, bf16[1,512,4096]{2,1,0:T(8,128)(2,1)} %win_hbm.1, ...), custom_call_target="tpu_custom_call" | custom-call | tf_op jit(solution)/shard_map/both_sections/pallas_call | solution.py:943
  84.0 2.4 %split_outputs.1 = (bf16[1,1024,512]{2,1,0:T(8,128)(2,1)}, f32[1,8,4096]{2,1,0:T(8,128)}, f32[1,32,512]{2,1,0:T(8,128)}, f32[1,2,8]{2,1,0:T(2,128)}, f32[1,8,8]{...) custom-call(bf16[1,1024,512]{2,1,0:T(8,128)(2,1)} %get-tuple-element.14.bout_in, ...), custom_call_target="tpu_custom_call" | custom-call | tf_op jit(solution)/shard_map/split_outputs/pallas_call | solution.py:957

commit v4 on v3

--- a/solution.py
+++ b/solution.py
@@ -24,7 +24,7 @@
 SCALE = 0.125
 WB = 4
 
-CHUNKS = {"a": (32, 512), "b": (16, 1024), "c": (16, 1024)}
+CHUNKS = {"a": (32, 512), "b": (16, 1024), "c": (16, 768), "o": (16, 256)}
 
 
 def nn(left, right):
@@ -81,7 +81,7 @@
         "bd1": ((256, 256), BF),
         "bds": ((256, 256), BF),
         "bdf": ((256, 256), F32),
-        "tbl": ((32, 2, 16, 128), BF),
+        "tbl": ((32, 16, 128), BF),
         "pre": ((2, 2, 8, 128), F32),
         "cds": ((2, 8, CLIP), I32),
         "cxs": ((2, 16, CLIP), BF),
@@ -92,6 +92,8 @@
         "cvec": ((2, 16, CLIP), BF),
         "hb": ((CLIP, D), F32),
         "bo": ((2 * CLIP, D), BF),
+        "avi": ((8, 4 * D + FF), F32),
+        "avd": ((32, D), F32),
         "gob": ((CLIP, D), BF),
         "xh1": ((2, CLIP, D), F32),
         "xh2": ((2, CLIP, D), F32),
@@ -121,7 +123,7 @@
         shapes["sb0" + k] = ((4, 4, 2, rows, w), BF)
         shapes["r0" + k] = ((4, 4, 2, rows, w), BF)
         for ax in "zx":
-            if k == "c":
+            if k in "co":
                 shapes["q" + ax + k] = ((3, 4, 2, rows, h), BF)
             else:
                 for slot in "012":
@@ -131,7 +133,7 @@
 
 
 SHAPES = ten_shapes()
-N_SEM = 130
+N_SEM = 160
 
 
 class Refs:
@@ -140,7 +142,7 @@
 
 def mega(
     x_hbm, win_hbm, wdn_hbm, gains_ref, proj_ref, book_ref, codes_ref, grids_ref, orders_ref,
-    avgin_ref, avgdn_ref,
+    avgin_hbm, avgdn_hbm,
     bout_hbm, gin_ref, gdn_ref, small_ref, ain_ref, adn_ref,
     *scratch,
 ):
@@ -197,7 +199,11 @@
         pltpu.make_async_copy(wdn_hbm.at[0], s.wdn, load_sems.at[3]),
         pltpu.make_async_copy(x_hbm.at[0, pl.ds(CLIP, CLIP)], s.xs.at[1], load_sems.at[4]),
     ]
-    for load in loads:
+    averages = [
+        pltpu.make_async_copy(avgin_hbm.at[0], s.avi, load_sems.at[7]),
+        pltpu.make_async_copy(avgdn_hbm.at[0], s.avd, load_sems.at[8]),
+    ]
+    for load in loads + averages:
         load.start()
 
     def bout_copy(c):
@@ -205,7 +211,9 @@
         return pltpu.make_async_copy(s.bo.at[rows], bout_hbm.at[0, rows], load_sems.at[5 + c])
 
     barrier = pltpu.get_barrier_semaphore()
-    peers = [core_dev, sec_dev, sec_core_dev] + zy_dev + xy_dev[1:]
+    far = [(i, j, y) for i in range(4) for j in range(4) for y in range(2) if i + j + y > 0]
+    far_dev = [place((z + i) % 4, (x + j) % 4, (yh + y) % 2, core) for i, j, y in far]
+    peers = [core_dev, sec_dev, sec_core_dev] + far_dev
     for dev in peers:
         pl.semaphore_signal(barrier, inc=1, device_id=dev, device_id_type=MESH)
 
@@ -223,13 +231,15 @@
     gain_one = gains_ref[0, 0:1, :].astype(F32)
     gain_two = gains_ref[0, 1:2, :].astype(F32)
     book = book_ref[...].astype(F32)
-    s.pre[sec, core] = jnp.concatenate([book, jnp.zeros((8, 64), F32)], axis=1)
+    empty = jnp.zeros((8, 64), F32)
+    s.pre[sec, core] = jnp.where(
+        is_e, jnp.concatenate([book, empty], axis=1), jnp.concatenate([empty, book], axis=1)
+    )
     s.gacc[...] = jnp.zeros((2, 8, D), F32)
     s.s_acc[...] = jnp.zeros((4, 8, 2, 8, 128), F32)
 
-    pl.semaphore_wait(barrier, len(peers))
-
     def book_start():
+        pl.semaphore_wait(barrier, len(peers))
         mine = s.pre.at[sec, core]
 
         @pl.when(is_e)
@@ -246,20 +256,13 @@
         rcopy("ag0", s.pre.at[0, core], s.pre.at[0, core], sec_dev).wait_recv()
         rcopy("ag1", s.pre.at[0, 1 - core], s.pre.at[0, 1 - core], sec_core_dev).wait_recv()
         rcopy("ag2", s.pre.at[1, 1 - core], s.pre.at[1, 1 - core], core_dev).wait_recv()
-        for half in range(2):
-            s.tbl[chip, half] = jnp.concatenate([s.pre[half, 0], s.pre[half, 1]], axis=0).astype(BF)
+        s.tbl[chip] = jnp.concatenate([s.pre[0, 0] + s.pre[1, 0], s.pre[0, 1] + s.pre[1, 1]], axis=0).astype(BF)
         part = s.tbl.at[chip]
-        for i in range(7):
-            rcopy("ag3%d" % i, part, part, xy_dev[i]).start()
-        for i, (d, y) in enumerate(around):
-            part = s.tbl.at[(z * 4 + (x + 4 - d) % 4) * 2 + (yh + 2 - y) % 2]
-            rcopy("ag3%d" % i, part, part, xy_dev[i]).wait_recv()
-        part = s.tbl.at[pl.ds(z * 8, 8)]
-        for i in range(3):
-            rcopy("ag4%d" % i, part, part, z_dev[i]).start()
-        for i in range(3):
-            part = s.tbl.at[pl.ds(((z + 3 - i) % 4) * 8, 8)]
-            rcopy("ag4%d" % i, part, part, z_dev[i]).wait_recv()
+        for n in range(31):
+            rcopy("ag3%d" % n, part, part, far_dev[n]).start()
+        for n, (i, j, y) in enumerate(far):
+            part = s.tbl.at[(((z + 4 - i) % 4) * 4 + (x + 4 - j) % 4) * 2 + (yh + 2 - y) % 2]
+            rcopy("ag3%d" % n, part, part, far_dev[n]).wait_recv()
 
     def book_finish():
         mine = s.pre.at[sec, core]
@@ -273,24 +276,21 @@
         def _():
             rcopy("ag2", mine, mine, core_dev).wait_send()
             part = s.tbl.at[dp // 2]
-            for i in range(7):
-                rcopy("ag3%d" % i, part, part, xy_dev[i]).wait_send()
-            part = s.tbl.at[pl.ds(z * 8, 8)]
-            for i in range(3):
-                rcopy("ag4%d" % i, part, part, z_dev[i]).wait_send()
-
-    def onehots(c, half):
+            for n in range(31):
+                rcopy("ag3%d" % n, part, part, far_dev[n]).wait_send()
+
+    def onehots(c, half, shift):
         code_row = s.cds[c][0:1, :] - half * HALF
         hi = code_row >> 6
         lo = code_row & 63
-        lo_one = (iota((128, CLIP), 0) == lo).astype(F32).astype(BF)
+        lo_one = (iota((128, CLIP), 0) == lo + shift).astype(F32).astype(BF)
         hi_mask = (iota((CLIP, CLIP), 0) >> 3) == hi
         return lo_one, hi_mask
 
     def entries(c):
         for half in range(2):
-            lo_one, hi_mask = onehots(c, half)
-            table = s.tbl[:, half].reshape(CLIP, 128)
+            lo_one, hi_mask = onehots(c, half, 64 * half)
+            table = s.tbl[...].reshape(CLIP, 128)
             picked = jnp.where(hi_mask, nn(table, lo_one), 0.0)
             s.ent[c, half] = jnp.sum(picked.reshape(64, 8, CLIP), axis=0)
 
@@ -298,7 +298,7 @@
         return jnp.concatenate([v, jnp.zeros((8, v.shape[1]), F32)], axis=0).astype(BF)
 
     def book_proj_terms(c, code_grad, wide_rows, narrow):
-        lo_one, hi_mask = onehots(c, sec)
+        lo_one, hi_mask = onehots(c, sec, 0)
         spread = jnp.broadcast_to(code_grad[None], (64, 8, CLIP)).reshape(CLIP, CLIP)
         left = jnp.where(hi_mask, spread, 0.0).astype(BF)
         total = nt(left, lo_one)
@@ -308,15 +308,19 @@
         total = total + tt(wide_rows, narrow_wide)
         s.s_acc[...] += total.reshape(4, 8, 2, 8, 128)
 
-    def norm_qkv(c, h):
-        s.hb[...] = h
-        xh, r = normed(h)
-        s.xh1[c] = xh
-        s.r1[c] = r
-        a = (xh * gain_one).astype(BF)
-        s.a1[c] = a
+    def norm_qkv(c, parts):
+        halves = [slice(0, 256), slice(256, 512)]
+        a = []
+        for rows, h in zip(halves, parts):
+            s.hb[rows] = h
+            xh, r = normed(h)
+            s.xh1[c, rows] = xh
+            s.r1[c, rows] = r
+            a.append((xh * gain_one).astype(BF))
+            s.a1[c, rows] = a[-1]
         for j in range(3):
-            s.qkv[c, :, 512 * j : 512 * j + 512] = nn(a, s.win[:, 512 * j : 512 * j + 512]).astype(BF)
+            for rows, v in zip(halves, a):
+                s.qkv[c, rows, 512 * j : 512 * j + 512] = nn(v, s.win[:, 512 * j : 512 * j + 512]).astype(BF)
 
     def feed_forward(c, put):
         m = s.hb[...] + nn(s.att[c], s.win[:, 1536:2048])
@@ -394,81 +398,67 @@
                 s.qkv[c, r, 1024 + o : 1280 + o] = d
 
     def head_sums(v):
-        hi = v.astype(BF)
-        lo = (v - hi.astype(F32)).astype(BF)
-        return nn(hi, s.bd1[...]) + nn(lo, s.bd1[...])
-
-    CR = 128
+        return nn(v, s.bd1[...])
+
+    CR = 256
 
     def frames_forward(c):
         late0 = orders_ref[c, 0] > orders_ref[c, 1]
         sign = jnp.where(late0, 1.0, -1.0).astype(F32)
-
-        def step(i, carry):
-            r0 = pl.ds(i * CR, CR)
-            r1 = pl.ds(GRID + i * CR, CR)
-            for quad in range(2):
-                qc = slice(256 * quad, 256 * quad + 256)
-                kc = slice(512 + 256 * quad, 768 + 256 * quad)
-                vc = slice(1024 + 256 * quad, 1280 + 256 * quad)
-                q_late = jnp.where(late0, s.qkv[c, r0, qc].astype(F32), s.qkv[c, r1, qc].astype(F32))
-                k_diff = sign * (s.qkv[c, r1, kc].astype(F32) - s.qkv[c, r0, kc].astype(F32))
-                v0 = s.qkv[c, r0, vc].astype(F32)
-                v1 = s.qkv[c, r1, vc].astype(F32)
-                d = head_sums(q_late * k_diff) * SCALE
-                e = jnp.exp(-jnp.abs(d))
-                big = 1.0 / (1.0 + e)
-                small = e * big
-                p_other = jnp.where(d > 0.0, big, small)
-                p_self = jnp.where(d > 0.0, small, big)
-                s.prob[c, r0, qc] = p_other
-                s.prob[c, r1, qc] = p_self
-                po = p_other.astype(BF).astype(F32)
-                ps = p_self.astype(BF).astype(F32)
-                v_late = jnp.where(late0, v0, v1)
-                v_early = jnp.where(late0, v1, v0)
-                mix = ps * v_late + po * v_early
-                s.att[c, r0, qc] = jnp.where(late0, mix, v0).astype(BF)
-                s.att[c, r1, qc] = jnp.where(late0, v1, mix).astype(BF)
-            return carry
-
-        lax.fori_loop(0, GRID // CR, step, 0)
+        r0 = slice(0, GRID)
+        r1 = slice(GRID, CLIP)
+        for quad in range(2):
+            qc = slice(256 * quad, 256 * quad + 256)
+            kc = slice(512 + 256 * quad, 768 + 256 * quad)
+            vc = slice(1024 + 256 * quad, 1280 + 256 * quad)
+            q_late = jnp.where(late0, s.qkv[c, r0, qc], s.qkv[c, r1, qc])
+            k_diff = s.qkv[c, r1, kc] - s.qkv[c, r0, kc]
+            v0 = s.qkv[c, r0, vc]
+            v1 = s.qkv[c, r1, vc]
+            d = head_sums(q_late * k_diff) * (sign * SCALE)
+            e = jnp.exp(-jnp.abs(d))
+            big = 1.0 / (1.0 + e)
+            small = e * big
+            p_other = jnp.where(d > 0.0, big, small)
+            p_self = jnp.where(d > 0.0, small, big)
+            s.prob[c, r0, qc] = p_other
+            s.prob[c, r1, qc] = p_self
+            p0 = jnp.where(late0, p_self, p_other).astype(BF)
+            p1 = jnp.where(late0, p_other, p_self).astype(BF)
+            mix = (p0.astype(F32) * v0.astype(F32) + p1.astype(F32) * v1.astype(F32)).astype(BF)
+            s.att[c, r0, qc] = jnp.where(late0, mix, v0)
+            s.att[c, r1, qc] = jnp.where(late0, v1, mix)
 
     def frames_backward(c):
         late0 = orders_ref[c, 0] > orders_ref[c, 1]
-        sign = jnp.where(late0, 1.0, -1.0).astype(F32)
-
-        def step(i, carry):
-            r0 = pl.ds(i * CR, CR)
-            r1 = pl.ds(GRID + i * CR, CR)
-            for quad in range(2):
-                qc = slice(256 * quad, 256 * quad + 256)
-                kc = slice(512 + 256 * quad, 768 + 256 * quad)
-                vc = slice(1024 + 256 * quad, 1280 + 256 * quad)
-                q_late = jnp.where(late0, s.qkv[c, r0, qc].astype(F32), s.qkv[c, r1, qc].astype(F32))
-                k_diff = sign * (s.qkv[c, r1, kc].astype(F32) - s.qkv[c, r0, kc].astype(F32))
-                v_diff = sign * (s.qkv[c, r1, vc].astype(F32) - s.qkv[c, r0, vc].astype(F32))
-                go0 = s.gob[r0, qc].astype(F32)
-                go1 = s.gob[r1, qc].astype(F32)
-                go_late = jnp.where(late0, go0, go1)
-                go_early = jnp.where(late0, go1, go0)
-                p_other = s.prob[c, r0, qc]
-                p_self = s.prob[c, r1, qc]
-                gs = p_other * p_self * head_sums(go_late * v_diff)
-                gs = gs.astype(BF).astype(F32) * SCALE
-                gq = gs * k_diff
-                gk = gs * q_late
-                gv_late = p_self.astype(BF).astype(F32) * go_late
-                gv_early = go_early + p_other.astype(BF).astype(F32) * go_late
-                s.qkv[c, r0, qc] = jnp.where(late0, gq, 0.0).astype(BF)
-                s.qkv[c, r1, qc] = jnp.where(late0, 0.0, gq).astype(BF)
-                s.qkv[c, r0, kc] = (-sign * gk).astype(BF)
-                s.qkv[c, r1, kc] = (sign * gk).astype(BF)
-                s.qkv[c, r0, vc] = jnp.where(late0, gv_late, gv_early).astype(BF)
-                s.qkv[c, r1, vc] = jnp.where(late0, gv_early, gv_late).astype(BF)
-            return carry
-
-        lax.fori_loop(0, GRID // CR, step, 0)
+        r0 = slice(0, GRID)
+        r1 = slice(GRID, CLIP)
+        for quad in range(2):
+            qc = slice(256 * quad, 256 * quad + 256)
+            kc = slice(512 + 256 * quad, 768 + 256 * quad)
+            vc = slice(1024 + 256 * quad, 1280 + 256 * quad)
+            q_late = jnp.where(late0, s.qkv[c, r0, qc], s.qkv[c, r1, qc])
+            k_diff = s.qkv[c, r1, kc] - s.qkv[c, r0, kc]
+            v_diff = s.qkv[c, r1, vc] - s.qkv[c, r0, vc]
+            go0 = s.gob[r0, qc]
+            go1 = s.gob[r1, qc]
+            go_late = jnp.where(late0, go0, go1)
+            go_early = jnp.where(late0, go1, go0)
+            p_other = s.prob[c, r0, qc]
+            p_self = s.prob[c, r1, qc]
+            gs = (p_other * p_self * head_sums(go_late * v_diff)).astype(BF).astype(F32) * SCALE
+            gq = (gs * k_diff.astype(F32)).astype(BF)
+            gk = gs * q_late.astype(F32)
+            late32 = go_late.astype(F32)
+            gv_late = (p_self.astype(BF).astype(F32) * late32).astype(BF)
+            gv_early = (go_early.astype(F32) + p_other.astype(BF).astype(F32) * late32).astype(BF)
+            none = jnp.zeros_like(gq)
+            s.qkv[c, r0, qc] = jnp.where(late0, gq, none)
+            s.qkv[c, r1, qc] = jnp.where(late0, none, gq)
+            s.qkv[c, r0, kc] = (-gk).astype(BF)
+            s.qkv[c, r1, kc] = gk.astype(BF)
+            s.qkv[c, r0, vc] = jnp.where(late0, gv_late, gv_early)
+            s.qkv[c, r1, vc] = jnp.where(late0, gv_early, gv_late)
 
     def gain_terms(which, grad, xhat):
         part = jnp.sum((grad * xhat).reshape(-1, 8, D), axis=0)
@@ -516,26 +506,21 @@
             cols = slice(512 * j, 512 * j + 512)
             add_into(s.acc_up, slice(None), cols, c, tn(s.a2[c], s.gel[c, :, cols]))
 
+    def grad_out(c):
+        add_into(s.acc_out, slice(None), slice(None), c, tn(s.att[c], s.gy[c]))
+
     def grad_attn(c):
         for j in range(3):
             cols = slice(512 * j, 512 * j + 512)
             add_into(s.acc_qkv, slice(None), cols, c, tn(s.a1[c], s.qkv[c, :, cols]))
-        add_into(s.acc_out, slice(None), slice(None), c, tn(s.att[c], s.gy[c]))
 
     def share(k, i, to_core):
         n = 2 * i + to_core
         if k == "a":
             return s.acc_dn[pl.ds(pl.multiple_of(n * 32, 32), 32), :]
         rows = pl.ds(pl.multiple_of(n * 8, 8), 8)
-        if k == "b":
-            return jnp.concatenate([s.acc_up[rows, 0:1024], s.acc_up[rows, 1024:2048]], axis=0)
-        return jnp.concatenate(
-            [
-                jnp.concatenate([s.acc_qkv[rows, 0:768], s.acc_out[rows, 0:256]], axis=1),
-                jnp.concatenate([s.acc_qkv[rows, 768:1536], s.acc_out[rows, 256:512]], axis=1),
-            ],
-            axis=0,
-        )
+        ref, w = {"b": (s.acc_up, 1024), "c": (s.acc_qkv, 768), "o": (s.acc_out, 256)}[k]
+        return jnp.concatenate([ref[rows, 0:w], ref[rows, w : 2 * w]], axis=0)
 
     def buf(name, k):
         return getattr(s, name + k)
@@ -574,7 +559,7 @@
                     )
                 )
             return out
-        if k == "c":
+        if k in "co":
             for i in range(3):
                 out.append(
                     rcopy("%s1z%d" % (k, i), r0.at[(z + 1 + i) % 4, :, :, :, lo], buf("qz", k).at[i], z_dev[i])
@@ -653,7 +638,7 @@
 
             lax.fori_loop(0, 16, body, 0)
             send(k, 1)
-            if k != "c":
+            if k not in "co":
                 send(k, 2)
         elif step == 2:
             arrived(k, 1)
@@ -664,7 +649,7 @@
                 r0[:, xb, y, :, hi] = total([r0[:, xb, y, :, hi], buf("q1x", k)[y]]).astype(BF)
             send(k, 3)
         elif step == 3:
-            if k == "c":
+            if k in "co":
                 arrived(k, 1)
                 r0[z, :, :, :, lo] = total([r0[z, :, :, :, lo]] + [buf("qz", k)[i] for i in range(3)]).astype(BF)
                 r0[:, x, :, :, hi] = total([r0[:, x, :, :, hi]] + [buf("qx", k)[i] for i in range(3)]).astype(BF)
@@ -687,15 +672,11 @@
             if k == "a":
                 gdn_ref[0] = mine
                 piece = s.wdn[pl.ds(dp * 32, 32), :].astype(F32)
-                adn_ref[0] = AVG_DECAY * avgdn_ref[0] + (1.0 - AVG_DECAY) * (piece - LEARN_RATE * mine)
-            elif k == "b":
-                gin_ref[0, :, 2048:3072] = mine[0:8]
-                gin_ref[0, :, 3072:4096] = mine[8:16]
+                adn_ref[0] = AVG_DECAY * s.avd[...] + (1.0 - AVG_DECAY) * (piece - LEARN_RATE * mine)
             else:
-                gin_ref[0, :, 0:768] = mine[0:8, :768]
-                gin_ref[0, :, 768:1536] = mine[8:16, :768]
-                gin_ref[0, :, 1536:1792] = mine[0:8, 768:]
-                gin_ref[0, :, 1792:2048] = mine[8:16, 768:]
+                first = {"b": 2048, "c": 0, "o": 1536}[k]
+                gin_ref[0, :, first : first + w] = mine[0:8]
+                gin_ref[0, :, first + w : first + 2 * w] = mine[8:16]
 
     def code_copy(c):
         return pltpu.make_async_remote_copy(
@@ -708,8 +689,6 @@
             src_ref=s.cxs.at[c], dst_ref=s.cxr.at[c], send_sem=send_sems.at[N_SEM - 4 + c],
             recv_sem=recv_sems.at[N_SEM - 4 + c], device_id=sec_dev, device_id_type=MESH,
         )
-
-    book_start()
 
     @pl.when(is_e)
     def _():
@@ -735,7 +714,12 @@
                 loads[4].wait()
 
             raster = [s.xs[c, 0:GRID], s.xs[c, GRID:CLIP]]
-            norm_qkv(c, jnp.concatenate([nn(s.perm[c], v) for v in raster], axis=0))
+            norm_qkv(c, [nn(s.perm[c], v) for v in raster])
+
+            @pl.when(c == 0)
+            def _():
+                book_start()
+
             window_forward(c, 0)
             window_forward(c, 1)
 
@@ -763,17 +747,17 @@
 
     @pl.when(is_d)
     def _():
+        book_start()
         gather_book()
-        for c in range(2):
-            entries(c)
         for load in loads:
             load.wait()
 
         def both(c, carry):
+            entries(c)
             code_copy(c).wait_recv()
             sent = (s.fcr[c] + s.ent[c, 0]).astype(BF).astype(F32)
             s.cvec[c] = pad16(sent + s.ent[c, 1])
-            norm_qkv(c, tn(s.cvec[c][0:8], proj_t))
+            norm_qkv(c, [tn(s.cvec[c][0:8, 0:256], proj_t), tn(s.cvec[c][0:8, 256:512], proj_t)])
             frames_forward(c)
 
             def put(acc):
@@ -811,6 +795,7 @@
         reduce_step("b", 0)
 
         def attns(c, carry):
+            grad_out(c)
             grad_attn(c)
 
             @pl.when(c == 0)
@@ -822,11 +807,13 @@
 
         lax.fori_loop(0, 2, attns, 0)
         reduce_step("c", 0)
+        reduce_step("o", 0)
+        reduce_step("a", 3)
+        book_proj_terms(0, s.cxs[0][0:8].astype(F32), s.eb[0], s.cvec[0][0:8].astype(F32))
         reduce_step("b", 2)
-        for c in range(2):
-            book_proj_terms(c, s.cxs[c][0:8].astype(F32), s.eb[c], s.cvec[c][0:8].astype(F32))
         reduce_step("c", 1)
-        reduce_step("a", 3)
+        reduce_step("o", 1)
+        book_proj_terms(1, s.cxs[1][0:8].astype(F32), s.eb[1], s.cvec[1][0:8].astype(F32))
 
     @pl.when(is_e)
     def _():
@@ -849,44 +836,52 @@
 
             @pl.when(c == 1)
             def _():
+                reduce_step("b", 0)
                 reduce_step("a", 1)
-                reduce_step("b", 0)
 
             back_up(c, lambda: s.hb[...])
+            grad_out(c)
 
             @pl.when(c == 1)
             def _():
+                reduce_step("o", 0)
                 reduce_step("b", 1)
+                reduce_step("a", 2)
 
             window_backward(c, 0)
 
             @pl.when(c == 1)
             def _():
-                reduce_step("a", 2)
+                reduce_step("o", 1)
 
             window_backward(c, 1)
+
+            @pl.when(c == 1)
+            def _():
+                reduce_step("b", 2)
+
             grad_attn(c)
 
             @pl.when(c == 1)
             def _():
                 reduce_step("c", 0)
-                reduce_step("b", 2)
-
-            s.gob[...] = back_in(c).astype(BF)
+                reduce_step("a", 3)
+
+            s.act[c, :, 0:D] = back_in(c).astype(BF)
+            return carry
+
+        lax.fori_loop(0, 2, backward, 0)
+        reduce_step("c", 1)
+
+        def leave(c, carry):
             for f in range(2):
-                back = tn(s.perm[c], s.gob[GRID * f : GRID * f + GRID])
+                back = tn(s.perm[c], s.act[c, GRID * f : GRID * f + GRID, 0:D])
                 s.bo[pl.ds(c * CLIP + GRID * f, GRID), :] = back.astype(BF)
             bout_copy(c).start()
-
-            @pl.when(c == 1)
-            def _():
-                reduce_step("c", 1)
-                reduce_step("a", 3)
-
             book_proj_terms(c, s.cxr[c][0:8].astype(F32), s.eb[c], s.cvec[c][0:8].astype(F32))
             return carry
 
-        lax.fori_loop(0, 2, backward, 0)
+        lax.fori_loop(0, 2, leave, 0)
 
     sums = jnp.concatenate(
         [
@@ -898,13 +893,15 @@
     )
     wide_sums = jnp.concatenate([jnp.zeros((72, D), F32), sums, jnp.zeros((48, D), F32)], axis=0)
     s.s_acc[...] += jnp.transpose(wide_sums).reshape(4, 8, 2, 8, 128)
-    order = ["s0", "b3", "s1", "c3", "a4", "s2", "b4", "c4", "s3"]
+    order = ["s0", "b3", "o3", "s1", "a4", "s2", "c3", "b4", "o4", "s3", "c4"]
+    for load in averages:
+        load.wait()
     for item in order:
         reduce_step(item[0], int(item[1]))
 
     half_rows = s.win[pl.ds(16 * (dp // 2), 16), :].astype(F32)
     piece = jnp.where(core == 0, half_rows[0:8], half_rows[8:16])
-    ain_ref[0] = AVG_DECAY * avgin_ref[0] + (1.0 - AVG_DECAY) * (piece - LEARN_RATE * gin_ref[0])
+    ain_ref[0] = AVG_DECAY * s.avi[...] + (1.0 - AVG_DECAY) * (piece - LEARN_RATE * gin_ref[0])
 
     for c in range(2):
         bout_copy(c).wait()
@@ -918,8 +915,8 @@
             grad_copy(c).wait_send()
 
     book_finish()
-    for k in ("a", "b", "c", "s"):
-        for step in {"s": (0, 1, 2), "c": (0, 1, 4)}.get(k, (0, 1, 2, 3, 4)):
+    for k in ("a", "b", "c", "o", "s"):
+        for step in {"s": (0, 1, 2), "c": (0, 1, 4), "o": (0, 1, 4)}.get(k, (0, 1, 2, 3, 4)):
             for cp in copies(k, step):
                 cp.wait_send()
 
@@ -939,11 +936,11 @@
         jax.ShapeDtypeStruct(avg_down.shape, F32),
     )
     scratch = [pltpu.VMEM(shape, dtype) for shape, dtype in SHAPES.values()]
-    scratch += [pltpu.SemaphoreType.DMA((N_SEM,)), pltpu.SemaphoreType.DMA((N_SEM,)), pltpu.SemaphoreType.DMA((8,))]
+    scratch += [pltpu.SemaphoreType.DMA((N_SEM,)), pltpu.SemaphoreType.DMA((N_SEM,)), pltpu.SemaphoreType.DMA((9,))]
     made = pl.pallas_call(
         mega,
         out_shape=outs,
-        in_specs=[hbm, hbm, hbm, vmem, vmem, vmem, vmem, smem, smem, vmem, vmem],
+        in_specs=[hbm, hbm, hbm, vmem, vmem, vmem, vmem, smem, smem, hbm, hbm],
         out_specs=[hbm] + [vmem] * 5,
         scratch_shapes=scratch,
         compiler_params=pltpu.CompilerParams(

time: 87 us -> 83.2 us (0.956)
  Pallas kernels: 85.8 us -> 81.4 us
    pallas_call x1, Pallas kernels: 83.3 us -> 79 us  [body(): pl.pallas_call(mega, out_shape=outs, in_specs=[hbm, hbm, hbm, vmem, vmem,...]
where the time goes in v4:
time: 83.2 us; the launch traced here: 82.2 us
  Pallas kernels  81.4 us (98%)
    pallas_call x1, Pallas kernels, body(): pl.pallas_call(mega, out_shape=outs, in_specs=[hbm, hbm, hbm, vmem, vmem,...  79 us
    pallas_call x1, Pallas kernels, body(): pl.pallas_call(split_outputs, out_shape=(outs[0], outs[1], outs[2], jax.S...  2.44 us

profile of v4, /device:TPU:1, one launch (start us, length us, event | category | flops | bytes accessed | tf_op | source)
XLA Modules:
  0.0 82.2 jit_solution(7480198494795030114)
XLA Ops:
  0.6 79.0 %both_sections.1 = (bf16[1,1024,512]{2,1,0:T(8,128)(2,1)}, f32[1,8,4096]{2,1,0:T(8,128)}, f32[1,32,512]{2,1,0:T(8,128)}, f32[8,128]{1,0:T(8,128)}, f32[1,8,4096]{2,1,0:T(8,128)}, /*index=5*/f32[1,32,512]{2,1,0:T(8,128)}) custom-call(bf16[1,1024,512]{2,1,0:T(8,128)(2,1)} %x_hbm.1, bf16[1,512,4096]{2,1,0:T(8,128)(2,1)} %win_hbm.1, ...), custom_call_target="tpu_custom_call" | custom-call | tf_op jit(solution)/shard_map/both_sections/pallas_call | solution.py:940
  79.6 2.4 %split_outputs.1 = (bf16[1,1024,512]{2,1,0:T(8,128)(2,1)}, f32[1,8,4096]{2,1,0:T(8,128)}, f32[1,32,512]{2,1,0:T(8,128)}, f32[1,2,8]{2,1,0:T(2,128)}, f32[1,8,8]{...) custom-call(bf16[1,1024,512]{2,1,0:T(8,128)(2,1)} %get-tuple-element.14.bout_in, ...), custom_call_target="tpu_custom_call" | custom-call | tf_op jit(solution)/shard_map/split_outputs/pallas_call | solution.py:954

commit v5 on v4

--- a/solution.py
+++ b/solution.py
@@ -92,6 +92,18 @@
         "cvec": ((2, 16, CLIP), BF),
         "hb": ((CLIP, D), F32),
         "bo": ((2 * CLIP, D), BF),
+        "m8": ((16, FF), BF),
+        "pgt": ((D, 128), F32),
+        "q8": ((2, 8, 768), F32),
+        "q0": ((8, 768), F32),
+        "qs1": ((8, 768), F32),
+        "qz": ((3, 8, 768), F32),
+        "qs2": ((8, 768), F32),
+        "qx": ((3, 8, 768), F32),
+        "qs3": ((8, 768), F32),
+        "qy": ((8, 768), F32),
+        "qs4": ((8, 768), F32),
+        "qg": ((8, 768), F32),
         "avi": ((8, 4 * D + FF), F32),
         "avd": ((32, D), F32),
         "gob": ((CLIP, D), BF),
@@ -123,17 +135,14 @@
         shapes["sb0" + k] = ((4, 4, 2, rows, w), BF)
         shapes["r0" + k] = ((4, 4, 2, rows, w), BF)
         for ax in "zx":
-            if k in "co":
-                shapes["q" + ax + k] = ((3, 4, 2, rows, h), BF)
-            else:
-                for slot in "012":
-                    shapes["q" + slot + ax + k] = ((2, 4, rows, h), BF)
+            for slot in "012":
+                shapes["q" + slot + ax + k] = ((2, 4, rows, h), BF)
             shapes["p" + ax + k] = ((7, rows, h), BF)
     return shapes
 
 
 SHAPES = ten_shapes()
-N_SEM = 160
+N_SEM = 200
 
 
 class Refs:
@@ -251,7 +260,7 @@
         def _():
             rcopy("ag2", mine, mine, core_dev).start()
 
-    def gather_book():
+    def gather_book_start():
         chip = dp // 2
         rcopy("ag0", s.pre.at[0, core], s.pre.at[0, core], sec_dev).wait_recv()
         rcopy("ag1", s.pre.at[0, 1 - core], s.pre.at[0, 1 - core], sec_core_dev).wait_recv()
@@ -260,6 +269,8 @@
         part = s.tbl.at[chip]
         for n in range(31):
             rcopy("ag3%d" % n, part, part, far_dev[n]).start()
+
+    def gather_book_wait():
         for n, (i, j, y) in enumerate(far):
             part = s.tbl.at[(((z + 4 - i) % 4) * 4 + (x + 4 - j) % 4) * 2 + (yh + 2 - y) % 2]
             rcopy("ag3%d" % n, part, part, far_dev[n]).wait_recv()
@@ -293,6 +304,12 @@
             table = s.tbl[...].reshape(CLIP, 128)
             picked = jnp.where(hi_mask, nn(table, lo_one), 0.0)
             s.ent[c, half] = jnp.sum(picked.reshape(64, 8, CLIP), axis=0)
+
+    def total(parts):
+        parts = [v.astype(F32) for v in parts]
+        while len(parts) > 1:
+            parts = [a + b for a, b in zip(parts[::2], parts[1::2])] + parts[len(parts) // 2 * 2 :]
+        return parts[0]
 
     def pad16(v):
         return jnp.concatenate([v, jnp.zeros((8, v.shape[1]), F32)], axis=0).astype(BF)
@@ -322,7 +339,7 @@
             for rows, v in zip(halves, a):
                 s.qkv[c, rows, 512 * j : 512 * j + 512] = nn(v, s.win[:, 512 * j : 512 * j + 512]).astype(BF)
 
-    def feed_forward(c, put):
+    def feed_forward(c, put, ahead=False):
         m = s.hb[...] + nn(s.att[c], s.win[:, 1536:2048])
         xh, r = normed(m)
         s.xh2[c] = xh
@@ -338,7 +355,7 @@
                 nxt = nn(a, s.win[:, 2304 + 256 * j : 2560 + 256 * j])
             value, slope = gelu_pair(u.astype(BF))
             s.act[c, :, cols] = value
-            s.gel[c, :, cols] = slope
+            s.gel[c, :, cols] = s.gel[c, :, cols] * slope if ahead else slope
             acc = acc + nn(value, s.wdn[cols, :])
         put(acc)
 
@@ -464,11 +481,11 @@
         part = jnp.sum((grad * xhat).reshape(-1, 8, D), axis=0)
         s.gacc[which] += part
 
-    def back_down(c):
-        gz = s.xs[c]
+    def back_down_codes(c):
+        twice = jnp.concatenate([s.cvec[c][0:8].astype(F32)] * 2, axis=0).astype(BF)
         for j in range(4):
             cols = slice(512 * j, 512 * j + 512)
-            s.gel[c, :, cols] = (nt(gz, s.wdn[cols, :]) * s.gel[c, :, cols].astype(F32)).astype(BF)
+            s.gel[c, :, cols] = (tn(twice, s.m8[:, cols]) * s.gel[c, :, cols].astype(F32)).astype(BF)
 
     def back_up(c, grad_of):
         acc = None
@@ -501,6 +518,23 @@
             cols = slice(512 * j, 512 * j + 512)
             add_into(s.acc_dn, cols, slice(None), c, tn(s.act[c, :, cols], s.xs[c]))
 
+    def grad_down_codes(c):
+        code = s.cvec[c][0:8].astype(F32)
+        wide = jnp.concatenate([jnp.zeros((80, CLIP), F32)] + [code] * 4 + [jnp.zeros((16, CLIP), F32)], axis=0)
+        wide = wide.astype(BF)
+        lanes = (iota((8, 128), 1) >> 3) - 10
+        for j in range(4):
+            v = tt(s.act[c, :, 512 * j : 512 * j + 512], wide).reshape(16, 4, 8, 128)
+            picked = [jnp.where(lanes == m, v[:, m], 0.0) for m in range(4)]
+            s.s_acc[j] += total(picked).reshape(8, 2, 8, 128)
+
+    def grad_qkv_codes(c):
+        norm_row = jnp.transpose(jnp.broadcast_to(s.r1[c], (CLIP, 128)))[0:1, :]
+        part = nn(pad16(s.cvec[c][0:8].astype(F32) * norm_row), s.qkv[c])[0:8]
+        for half in range(2):
+            v = part[:, 768 * half : 768 * half + 768]
+            s.q8[half] = jnp.where(c == 0, v, s.q8[half] + v)
+
     def grad_up(c):
         for j in range(4):
             cols = slice(512 * j, 512 * j + 512)
@@ -537,6 +571,16 @@
                 )
                 for i, (d, y) in enumerate(around)
             ]
+        if k == "q":
+            if step == 0:
+                return [rcopy("q0", s.q8.at[1 - core], s.q0, core_dev)]
+            if step == 1:
+                return [rcopy("q1%d" % i, s.qs1, s.qz.at[i], z_dev[i]) for i in range(3)]
+            if step == 2:
+                return [rcopy("q2%d" % i, s.qs2, s.qx.at[i], x_dev[i]) for i in range(3)]
+            if step == 3:
+                return [rcopy("q3", s.qs3, s.qy, y_dev)]
+            return [rcopy("q4", s.qs4, s.qg, core_dev)]
         rows, w = CHUNKS[k]
         h = w // 2
         r0 = buf("r0", k)
@@ -559,15 +603,6 @@
                     )
                 )
             return out
-        if k in "co":
-            for i in range(3):
-                out.append(
-                    rcopy("%s1z%d" % (k, i), r0.at[(z + 1 + i) % 4, :, :, :, lo], buf("qz", k).at[i], z_dev[i])
-                )
-                out.append(
-                    rcopy("%s1x%d" % (k, i), r0.at[:, (x + 1 + i) % 4, :, :, hi], buf("qx", k).at[i], x_dev[i])
-                )
-            return out
         for y in range(2):
             first, second = ((1, 3), (3, 1))[y]
             hop = second if step == 3 else first
@@ -595,11 +630,10 @@
         for cp in copies(k, step):
             cp.start()
 
-    def total(parts):
-        parts = [v.astype(F32) for v in parts]
-        while len(parts) > 1:
-            parts = [a + b for a, b in zip(parts[::2], parts[1::2])] + parts[len(parts) // 2 * 2 :]
-        return parts[0]
+    def put_down(mine):
+        gdn_ref[0] = mine
+        piece = s.wdn[pl.ds(dp * 32, 32), :].astype(F32)
+        adn_ref[0] = AVG_DECAY * s.avd[...] + (1.0 - AVG_DECAY) * (piece - LEARN_RATE * mine)
 
     def reduce_step(k, step):
         if k == "s":
@@ -610,7 +644,39 @@
             elif step == 2:
                 s.s0[z] += (s.s1[0] + s.s1[1]) + s.s1[2]
             elif step == 3:
-                small_ref[...] = total([s.s0[z, 2 * x + yh]] + [s.s2[i] for i in range(7)])
+                small = total([s.s0[z, 2 * x + yh]] + [s.s2[i] for i in range(7)])
+                small_ref[...] = small
+
+                @pl.when(is_e)
+                def _():
+                    narrow = proj_t.astype(F32)
+                    shares = [
+                        total([small[:, n : n + 1] * narrow[n % 8 : n % 8 + 1, :] for n in range(80 + 8 * m, 88 + 8 * m)])
+                        for m in range(4)
+                    ]
+                    put_down(jnp.concatenate(shares, axis=0))
+
+                return
+            send(k, step)
+            return
+        if k == "q":
+            if step > 0:
+                arrived(k, step - 1)
+            if step == 1:
+                s.qs1[...] = s.q8[core] + s.q0[...]
+            elif step == 2:
+                s.qs2[...] = total([s.qs1[...]] + [s.qz[i] for i in range(3)])
+            elif step == 3:
+                s.qs3[...] = total([s.qs2[...]] + [s.qx[i] for i in range(3)])
+            elif step == 4:
+                s.qs4[...] = s.qs3[...] + s.qy[...]
+            elif step == 5:
+                mine, other = s.qs4[...], s.qg[...]
+                narrow = s.pgt[pl.ds(pl.multiple_of(dp * 8, 8), 8), :]
+                for half, v in enumerate((jnp.where(core == 0, mine, other), jnp.where(core == 0, other, mine))):
+                    gin_ref[0, :, 768 * half : 768 * half + 768] = total(
+                        [narrow[:, n : n + 1] * v[n : n + 1, :] for n in range(8)]
+                    )
                 return
             send(k, step)
             return
@@ -638,8 +704,7 @@
 
             lax.fori_loop(0, 16, body, 0)
             send(k, 1)
-            if k not in "co":
-                send(k, 2)
+            send(k, 2)
         elif step == 2:
             arrived(k, 1)
             for y in range(2):
@@ -649,20 +714,15 @@
                 r0[:, xb, y, :, hi] = total([r0[:, xb, y, :, hi], buf("q1x", k)[y]]).astype(BF)
             send(k, 3)
         elif step == 3:
-            if k in "co":
-                arrived(k, 1)
-                r0[z, :, :, :, lo] = total([r0[z, :, :, :, lo]] + [buf("qz", k)[i] for i in range(3)]).astype(BF)
-                r0[:, x, :, :, hi] = total([r0[:, x, :, :, hi]] + [buf("qx", k)[i] for i in range(3)]).astype(BF)
-            else:
-                arrived(k, 2)
-                arrived(k, 3)
-                for y in range(2):
-                    r0[z, :, y, :, lo] = total(
-                        [r0[z, :, y, :, lo], buf("q0z", k)[y], buf("q2z", k)[y]]
-                    ).astype(BF)
-                    r0[:, x, y, :, hi] = total(
-                        [r0[:, x, y, :, hi], buf("q0x", k)[y], buf("q2x", k)[y]]
-                    ).astype(BF)
+            arrived(k, 2)
+            arrived(k, 3)
+            for y in range(2):
+                r0[z, :, y, :, lo] = total(
+                    [r0[z, :, y, :, lo], buf("q0z", k)[y], buf("q2z", k)[y]]
+                ).astype(BF)
+                r0[:, x, y, :, hi] = total(
+                    [r0[:, x, y, :, hi], buf("q0x", k)[y], buf("q2x", k)[y]]
+                ).astype(BF)
             send(k, 4)
         else:
             arrived(k, 4)
@@ -670,13 +730,23 @@
             right = total([r0[z, x, yh, :, hi]] + [buf("pz", k)[i] for i in range(7)])
             mine = jnp.concatenate([left, right], axis=1)
             if k == "a":
-                gdn_ref[0] = mine
-                piece = s.wdn[pl.ds(dp * 32, 32), :].astype(F32)
-                adn_ref[0] = AVG_DECAY * s.avd[...] + (1.0 - AVG_DECAY) * (piece - LEARN_RATE * mine)
+                put_down(mine)
             else:
                 first = {"b": 2048, "c": 0, "o": 1536}[k]
                 gin_ref[0, :, first : first + w] = mine[0:8]
                 gin_ref[0, :, first + w : first + 2 * w] = mine[8:16]
+
+    def add_gains():
+        sums = jnp.concatenate(
+            [
+                jnp.sum(s.gacc[0], axis=0, keepdims=True),
+                jnp.sum(s.gacc[1], axis=0, keepdims=True),
+                jnp.zeros((6, D), F32),
+            ],
+            axis=0,
+        )
+        wide_sums = jnp.concatenate([jnp.zeros((72, D), F32), sums, jnp.zeros((48, D), F32)], axis=0)
+        s.s_acc[...] += jnp.transpose(wide_sums).reshape(4, 8, 2, 8, 128)
 
     def code_copy(c):
         return pltpu.make_async_remote_copy(
@@ -744,13 +814,30 @@
             return carry
 
         lax.fori_loop(0, 2, forward, 0)
+        for j in range(4):
+            cols = slice(512 * j, 512 * j + 512)
+            m = nt(proj_t, s.wdn[cols, :])
+            hi = m.astype(BF).astype(F32)
+            s.m8[:, cols] = jnp.concatenate([hi, m - hi], axis=0).astype(BF)
 
     @pl.when(is_d)
     def _():
         book_start()
-        gather_book()
+        gather_book_start()
         for load in loads:
             load.wait()
+
+        def ahead(c, carry):
+            for j in range(4):
+                cols = slice(512 * j, 512 * j + 512)
+                s.gel[c, :, cols] = nt(s.xs[c], s.wdn[cols, :]).astype(BF)
+            return carry
+
+        lax.fori_loop(0, 2, ahead, 0)
+        narrow = proj_t.astype(F32)
+        narrow = (narrow - jnp.mean(narrow, axis=-1, keepdims=True)) * gain_one
+        s.pgt[...] = jnp.transpose(jnp.concatenate([narrow, jnp.zeros((120, D), F32)], axis=0))
+        gather_book_wait()
 
         def both(c, carry):
             entries(c)
@@ -763,9 +850,8 @@
             def put(acc):
                 s.bo[pl.ds(c * CLIP, CLIP), :] = acc.astype(BF)
 
-            feed_forward(c, put)
+            feed_forward(c, put, ahead=True)
             bout_copy(c).start()
-            back_down(c)
             back_up(c, lambda: s.xs[c].astype(F32))
             frames_backward(c)
             s.eb[c] = back_in(c).astype(BF)
@@ -779,41 +865,39 @@
             grad_down(c)
             return carry
 
+        def ups(c, carry):
+            grad_up(c)
+            return carry
+
+        def outs(c, carry):
+            grad_out(c)
+            return carry
+
+        def codes_of(c, carry):
+            grad_qkv_codes(c)
+            return carry
+
+        def books(c):
+            book_proj_terms(c, s.cxs[c][0:8].astype(F32), s.eb[c], s.cvec[c][0:8].astype(F32))
+
         lax.fori_loop(0, 2, downs, 0)
         reduce_step("a", 0)
-
-        def ups(c, carry):
-            grad_up(c)
-
-            @pl.when(c == 0)
-            def _():
-                reduce_step("a", 1)
-
-            return carry
-
         lax.fori_loop(0, 2, ups, 0)
         reduce_step("b", 0)
-
-        def attns(c, carry):
-            grad_out(c)
-            grad_attn(c)
-
-            @pl.when(c == 0)
-            def _():
-                reduce_step("a", 2)
-                reduce_step("b", 1)
-
-            return carry
-
-        lax.fori_loop(0, 2, attns, 0)
-        reduce_step("c", 0)
+        reduce_step("a", 1)
+        lax.fori_loop(0, 2, outs, 0)
         reduce_step("o", 0)
-        reduce_step("a", 3)
-        book_proj_terms(0, s.cxs[0][0:8].astype(F32), s.eb[0], s.cvec[0][0:8].astype(F32))
-        reduce_step("b", 2)
-        reduce_step("c", 1)
+        books(0)
         reduce_step("o", 1)
-        book_proj_terms(1, s.cxs[1][0:8].astype(F32), s.eb[1], s.cvec[1][0:8].astype(F32))
+        reduce_step("b", 1)
+        books(1)
+        reduce_step("a", 2)
+        add_gains()
+        lax.fori_loop(0, 2, codes_of, 0)
+        for load in averages:
+            load.wait()
+        for item in ["q0", "s0", "q1", "b2", "o2", "a3", "s1", "q2", "b3", "o3", "s2", "q3", "a4", "q4", "o4", "s3", "b4", "q5"]:
+            reduce_step(item[0], int(item[1]))
 
     @pl.when(is_e)
     def _():
@@ -824,80 +908,63 @@
                 s.cvec[c, :, cols] = nt(s.cxr[c, :, cols], s.perm[c]).astype(BF)
             g = tn(s.cvec[c][0:8], proj_t)
             s.hb[...] = g
-            s.xs[c] = g.astype(BF)
-            grad_down(c)
-
-            @pl.when(c == 1)
-            def _():
-                reduce_step("a", 0)
-
-            back_down(c)
+            back_down_codes(c)
             grad_up(c)
 
             @pl.when(c == 1)
             def _():
                 reduce_step("b", 0)
-                reduce_step("a", 1)
 
             back_up(c, lambda: s.hb[...])
+            window_backward(c, 0)
+
+            @pl.when(c == 1)
+            def _():
+                reduce_step("b", 1)
+
+            window_backward(c, 1)
+            grad_attn(c)
+
+            @pl.when(c == 1)
+            def _():
+                reduce_step("c", 0)
+                reduce_step("b", 2)
+
             grad_out(c)
 
             @pl.when(c == 1)
             def _():
                 reduce_step("o", 0)
-                reduce_step("b", 1)
-                reduce_step("a", 2)
-
-            window_backward(c, 0)
-
-            @pl.when(c == 1)
-            def _():
-                reduce_step("o", 1)
-
-            window_backward(c, 1)
-
-            @pl.when(c == 1)
-            def _():
-                reduce_step("b", 2)
-
-            grad_attn(c)
-
-            @pl.when(c == 1)
-            def _():
-                reduce_step("c", 0)
-                reduce_step("a", 3)
-
-            s.act[c, :, 0:D] = back_in(c).astype(BF)
+                reduce_step("c", 1)
+
+            s.a2[c] = back_in(c).astype(BF)
             return carry
 
         lax.fori_loop(0, 2, backward, 0)
-        reduce_step("c", 1)
+        reduce_step("o", 1)
 
         def leave(c, carry):
             for f in range(2):
-                back = tn(s.perm[c], s.act[c, GRID * f : GRID * f + GRID, 0:D])
+                back = tn(s.perm[c], s.a2[c, GRID * f : GRID * f + GRID])
                 s.bo[pl.ds(c * CLIP + GRID * f, GRID), :] = back.astype(BF)
             bout_copy(c).start()
             book_proj_terms(c, s.cxr[c][0:8].astype(F32), s.eb[c], s.cvec[c][0:8].astype(F32))
             return carry
 
         lax.fori_loop(0, 2, leave, 0)
-
-    sums = jnp.concatenate(
-        [
-            jnp.sum(s.gacc[0], axis=0, keepdims=True),
-            jnp.sum(s.gacc[1], axis=0, keepdims=True),
-            jnp.zeros((6, D), F32),
-        ],
-        axis=0,
-    )
-    wide_sums = jnp.concatenate([jnp.zeros((72, D), F32), sums, jnp.zeros((48, D), F32)], axis=0)
-    s.s_acc[...] += jnp.transpose(wide_sums).reshape(4, 8, 2, 8, 128)
-    order = ["s0", "b3", "o3", "s1", "a4", "s2", "c3", "b4", "o4", "s3", "c4"]
-    for load in averages:
-        load.wait()
-    for item in order:
-        reduce_step(item[0], int(item[1]))
+        reduce_step("c", 2)
+        reduce_step("b", 3)
+
+        def downs(c, carry):
+            grad_down_codes(c)
+            return carry
+
+        lax.fori_loop(0, 2, downs, 0)
+        add_gains()
+        for load in averages:
+            load.wait()
+        for item in ["o2", "s0", "s1", "c3", "o3", "s2", "c4", "b4", "o4", "s3"]:
+            reduce_step(item[0], int(item[1]))
 
     half_rows = s.win[pl.ds(16 * (dp // 2), 16), :].astype(F32)
     piece = jnp.where(core == 0, half_rows[0:8], half_rows[8:16])
@@ -915,10 +982,19 @@
             grad_copy(c).wait_send()
 
     book_finish()
-    for k in ("a", "b", "c", "o", "s"):
-        for step in {"s": (0, 1, 2), "c": (0, 1, 4), "o": (0, 1, 4)}.get(k, (0, 1, 2, 3, 4)):
-            for cp in copies(k, step):
-                cp.wait_send()
+    def finish(chunks):
+        for k in chunks:
+            for step in {"s": (0, 1, 2)}.get(k, (0, 1, 2, 3, 4)):
+                for cp in copies(k, step):
+                    cp.wait_send()
+
+    @pl.when(is_e)
+    def _():
+        finish("bcos")
+
+    @pl.when(is_d)
+    def _():
+        finish("abosq")
 
 
 def body(

time: 83.2 us -> 77 us (0.925); the launches traced: 82.2 us -> 76.8 us
  Pallas kernels: 81.4 us -> 76.1 us
    pallas_call x1, Pallas kernels: 79 us -> 73.6 us  [body(): pl.pallas_call(mega, out_shape=outs, in_specs=[hbm, hbm, hbm, vmem, vmem,...]
where the time goes in v5:
time: 77 us; the launch traced here: 76.8 us
  Pallas kernels  76.1 us (99%)
    pallas_call x1, Pallas kernels, body(): pl.pallas_call(mega, out_shape=outs, in_specs=[hbm, hbm, hbm, vmem, vmem,...  73.6 us
    pallas_call x1, Pallas kernels, body(): pl.pallas_call(split_outputs, out_shape=(outs[0], outs[1], outs[2], jax.S...  2.44 us

profile of v5, /device:TPU:1, one launch (start us, length us, event | category | flops | bytes accessed | tf_op | source)
XLA Modules:
  0.0 76.8 jit_solution(2054987031309235792)
XLA Ops:
  0.6 73.6 %both_sections.1 = (bf16[1,1024,512]{2,1,0:T(8,128)(2,1)}, f32[1,8,4096]{2,1,0:T(8,128)}, f32[1,32,512]{2,1,0:T(8,128)}, f32[8,128]{1,0:T(8,128)}, f32[1,8,4096]{2,1,0:T(8,128)}, /*index=5*/f32[1,32,512]{2,1,0:T(8,128)}) custom-call(bf16[1,1024,512]{2,1,0:T(8,128)(2,1)} %x_hbm.1, bf16[1,512,4096]{2,1,0:T(8,128)(2,1)} %win_hbm.1, ...), custom_call_target="tpu_custom_call" | custom-call | tf_op jit(solution)/shard_map/both_sections/pallas_call | solution.py:1016
  74.3 2.4 %split_outputs.1 = (bf16[1,1024,512]{2,1,0:T(8,128)(2,1)}, f32[1,8,4096]{2,1,0:T(8,128)}, f32[1,32,512]{2,1,0:T(8,128)}, f32[1,2,8]{2,1,0:T(2,128)}, f32[1,8,8]{...) custom-call(bf16[1,1024,512]{2,1,0:T(8,128)(2,1)} %get-tuple-element.14.bout_in, ...), custom_call_target="tpu_custom_call" | custom-call | tf_op jit(solution)/shard_map/split_outputs/pallas_call | solution.py:1030

commit v6 on v5

--- a/solution.py
+++ b/solution.py
@@ -182,7 +182,7 @@
     x_dev = [place(z, (x + d) % 4, yh, core) for d in (1, 2, 3)]
     sec_dev = (1 - sec, dp)
     sec_core_dev = (1 - sec, dp + 1 - 2 * core)
-    around = [(d, y) for d in range(4) for y in range(2) if d + y > 0]
+    around = [(2, 1), (1, 1), (3, 1), (0, 1), (2, 0), (1, 0), (3, 0)]
     zy_dev = [place((z + d) % 4, x, (yh + y) % 2, core) for d, y in around]
     xy_dev = [place(z, (x + d) % 4, (yh + y) % 2, core) for d, y in around]
 
@@ -198,6 +198,25 @@
             src_ref=src, dst_ref=dst, send_sem=send_sems.at[i], recv_sem=recv_sems.at[i],
             device_id=dev, device_id_type=MESH,
         )
+
+    def bout_copy(c):
+        rows = pl.ds(c * CLIP, CLIP)
+        return pltpu.make_async_copy(s.bo.at[rows], bout_hbm.at[0, rows], load_sems.at[5 + c])
+
+    barrier = pltpu.get_barrier_semaphore()
+    far = [(i, j, y) for i in range(4) for j in range(4) for y in range(2) if i + j + y > 0]
+    far.sort(key=lambda p: -(min(p[0], 4 - p[0]) + min(p[1], 4 - p[1]) + 2 * p[2]))
+    wide = [n for n, (i, j, y) in enumerate(far) if i > 0 and j > 0]
+    far_dev = [place((z + i) % 4, (x + j) % 4, (yh + y) % 2, core) for i, j, y in far]
+    plane_dev = [dev for n, dev in enumerate(far_dev) if n not in wide]
+    near_dev = [sec_core_dev, sec_dev, core_dev]
+    @pl.when(is_d)
+    def _():
+        for n in wide:
+            pl.semaphore_signal(barrier, inc=1, device_id=far_dev[n], device_id_type=MESH)
+
+    for dev in plane_dev + near_dev:
+        pl.semaphore_signal(barrier, inc=1, device_id=dev, device_id_type=MESH)
 
     loads = [
         pltpu.make_async_copy(x_hbm.at[0, pl.ds(0, CLIP)], s.xs.at[0], load_sems.at[0]),
@@ -215,17 +234,6 @@
     for load in loads + averages:
         load.start()
 
-    def bout_copy(c):
-        rows = pl.ds(c * CLIP, CLIP)
-        return pltpu.make_async_copy(s.bo.at[rows], bout_hbm.at[0, rows], load_sems.at[5 + c])
-
-    barrier = pltpu.get_barrier_semaphore()
-    far = [(i, j, y) for i in range(4) for j in range(4) for y in range(2) if i + j + y > 0]
-    far_dev = [place((z + i) % 4, (x + j) % 4, (yh + y) % 2, core) for i, j, y in far]
-    peers = [core_dev, sec_dev, sec_core_dev] + far_dev
-    for dev in peers:
-        pl.semaphore_signal(barrier, inc=1, device_id=dev, device_id_type=MESH)
-
     rows_i = iota((256, 256), 0)
     cols_i = iota((256, 256), 1)
     same = ((rows_i >> 6) == (cols_i >> 6)).astype(F32)
@@ -248,7 +256,7 @@
     s.s_acc[...] = jnp.zeros((4, 8, 2, 8, 128), F32)
 
     def book_start():
-        pl.semaphore_wait(barrier, len(peers))
+        pl.semaphore_wait(barrier, len(plane_dev + near_dev) + sec * len(wide))
         mine = s.pre.at[sec, core]
 
         @pl.when(is_e)
@@ -823,7 +831,6 @@
     @pl.when(is_d)
     def _():
         book_start()
-        gather_book_start()
         for load in loads:
             load.wait()
 
@@ -834,6 +841,7 @@
             return carry
 
         lax.fori_loop(0, 2, ahead, 0)
+        gather_book_start()
         narrow = proj_t.astype(F32)
         narrow = (narrow - jnp.mean(narrow, axis=-1, keepdims=True)) * gain_one
         s.pgt[...] = jnp.transpose(jnp.concatenate([narrow, jnp.zeros((120, D), F32)], axis=0))

time: 77 us -> 75.5 us (0.981)
  Pallas kernels: 76.1 us -> 74.6 us
    pallas_call x1, Pallas kernels: 73.6 us -> 72.1 us  [body(): pl.pallas_call(mega, out_shape=outs, in_specs=[hbm, hbm, hbm, vmem, vmem,...]
where the time goes in v6:
time: 75.5 us; the launch traced here: 75.3 us
  Pallas kernels  74.6 us (99%)
  between operations  0.76 us (1%)
    pallas_call x1, Pallas kernels, body(): pl.pallas_call(mega, out_shape=outs, in_specs=[hbm, hbm, hbm, vmem, vmem,...  72.1 us
    pallas_call x1, Pallas kernels, body(): pl.pallas_call(split_outputs, out_shape=(outs[0], outs[1], outs[2], jax.S...  2.44 us

profile of v6, /device:TPU:1, one launch (start us, length us, event | category | flops | bytes accessed | tf_op | source)
XLA Modules:
  0.0 75.3 jit_solution(2166438596784799984)
XLA Ops:
  0.6 72.1 %both_sections.1 = (bf16[1,1024,512]{2,1,0:T(8,128)(2,1)}, f32[1,8,4096]{2,1,0:T(8,128)}, f32[1,32,512]{2,1,0:T(8,128)}, f32[8,128]{1,0:T(8,128)}, f32[1,8,4096]{2,1,0:T(8,128)}, /*index=5*/f32[1,32,512]{2,1,0:T(8,128)}) custom-call(bf16[1,1024,512]{2,1,0:T(8,128)(2,1)} %x_hbm.1, bf16[1,512,4096]{2,1,0:T(8,128)(2,1)} %win_hbm.1, ...), custom_call_target="tpu_custom_call" | custom-call | tf_op jit(solution)/shard_map/both_sections/pallas_call | solution.py:1024
  72.8 2.4 %split_outputs.1 = (bf16[1,1024,512]{2,1,0:T(8,128)(2,1)}, f32[1,8,4096]{2,1,0:T(8,128)}, f32[1,32,512]{2,1,0:T(8,128)}, f32[1,2,8]{2,1,0:T(2,128)}, f32[1,8,8]{...) custom-call(bf16[1,1024,512]{2,1,0:T(8,128)(2,1)} %get-tuple-element.14.bout_in, ...), custom_call_target="tpu_custom_call" | custom-call | tf_op jit(solution)/shard_map/split_outputs/pallas_call | solution.py:1038

commit v7 on v6

--- a/solution.py
+++ b/solution.py
@@ -792,11 +792,11 @@
                 loads[4].wait()
 
             raster = [s.xs[c, 0:GRID], s.xs[c, GRID:CLIP]]
-            norm_qkv(c, [nn(s.perm[c], v) for v in raster])
-
             @pl.when(c == 0)
             def _():
                 book_start()
+
+            norm_qkv(c, [nn(s.perm[c], v) for v in raster])
 
             window_forward(c, 0)
             window_forward(c, 1)
@@ -831,6 +831,7 @@
     @pl.when(is_d)
     def _():
         book_start()
+        gather_book_start()
         for load in loads:
             load.wait()
 
@@ -841,7 +842,6 @@
             return carry
 
         lax.fori_loop(0, 2, ahead, 0)
-        gather_book_start()
         narrow = proj_t.astype(F32)
         narrow = (narrow - jnp.mean(narrow, axis=-1, keepdims=True)) * gain_one
         s.pgt[...] = jnp.transpose(jnp.concatenate([narrow, jnp.zeros((120, D), F32)], axis=0))

time: 75.5 us -> 75.2 us (level)
  no operation moved by 1% of the time
where the time goes in v7:
time: 75.2 us; the launch traced here: 75 us
  Pallas kernels  74.2 us (99%)
  between operations  0.76 us (1%)
    pallas_call x1, Pallas kernels, body(): pl.pallas_call(mega, out_shape=outs, in_specs=[hbm, hbm, hbm, vmem, vmem,...  71.8 us
    pallas_call x1, Pallas kernels, body(): pl.pallas_call(split_outputs, out_shape=(outs[0], outs[1], outs[2], jax.S...  2.44 us

profile of v7, /device:TPU:1, one launch (start us, length us, event | category | flops | bytes accessed | tf_op | source)
XLA Modules:
  0.0 75.0 jit_solution(17303875967820760965)
XLA Ops:
  0.6 71.8 %both_sections.1 = (bf16[1,1024,512]{2,1,0:T(8,128)(2,1)}, f32[1,8,4096]{2,1,0:T(8,128)}, f32[1,32,512]{2,1,0:T(8,128)}, f32[8,128]{1,0:T(8,128)}, f32[1,8,4096]{2,1,0:T(8,128)}, /*index=5*/f32[1,32,512]{2,1,0:T(8,128)}) custom-call(bf16[1,1024,512]{2,1,0:T(8,128)(2,1)} %x_hbm.1, bf16[1,512,4096]{2,1,0:T(8,128)(2,1)} %win_hbm.1, ...), custom_call_target="tpu_custom_call" | custom-call | tf_op jit(solution)/shard_map/both_sections/pallas_call | solution.py:1024
  72.4 2.4 %split_outputs.1 = (bf16[1,1024,512]{2,1,0:T(8,128)(2,1)}, f32[1,8,4096]{2,1,0:T(8,128)}, f32[1,32,512]{2,1,0:T(8,128)}, f32[1,2,8]{2,1,0:T(2,128)}, f32[1,8,8]{...) custom-call(bf16[1,1024,512]{2,1,0:T(8,128)(2,1)} %get-tuple-element.14.bout_in, ...), custom_call_target="tpu_custom_call" | custom-call | tf_op jit(solution)/shard_map/split_outputs/pallas_call | solution.py:1038

commit v8 on v7

--- a/solution.py
+++ b/solution.py
@@ -909,6 +909,13 @@
 
     @pl.when(is_e)
     def _():
+        def leave(c):
+            for f in range(2):
+                back = tn(s.perm[c], s.a2[c, GRID * f : GRID * f + GRID])
+                s.bo[pl.ds(c * CLIP + GRID * f, GRID), :] = back.astype(BF)
+            bout_copy(c).start()
+            book_proj_terms(c, s.cxr[c][0:8].astype(F32), s.eb[c], s.cvec[c][0:8].astype(F32))
+
         def backward(c, carry):
             grad_copy(c).wait_recv()
             for f in range(2):
@@ -936,13 +943,14 @@
             @pl.when(c == 1)
             def _():
                 reduce_step("c", 0)
-                reduce_step("b", 2)
 
             grad_out(c)
 
             @pl.when(c == 1)
             def _():
                 reduce_step("o", 0)
+                leave(0)
+                reduce_step("b", 2)
                 reduce_step("c", 1)
 
             s.a2[c] = back_in(c).astype(BF)
@@ -951,15 +959,7 @@
         lax.fori_loop(0, 2, backward, 0)
         reduce_step("o", 1)
 
-        def leave(c, carry):
-            for f in range(2):
-                back = tn(s.perm[c], s.a2[c, GRID * f : GRID * f + GRID])
-                s.bo[pl.ds(c * CLIP + GRID * f, GRID), :] = back.astype(BF)
-            bout_copy(c).start()
-            book_proj_terms(c, s.cxr[c][0:8].astype(F32), s.eb[c], s.cvec[c][0:8].astype(F32))
-            return carry
-
-        lax.fori_loop(0, 2, leave, 0)
+        leave(1)
         reduce_step("c", 2)
         reduce_step("b", 3)
 

time: 75.2 us -> 75.1 us (level)
  no operation moved by 1% of the time
where the time goes in v8:
time: 75.1 us; the launch traced here: 74.9 us
  Pallas kernels  74.2 us (99%)
  between operations  0.76 us (1%)
    pallas_call x1, Pallas kernels, body(): pl.pallas_call(mega, out_shape=outs, in_specs=[hbm, hbm, hbm, vmem, vmem,...  71.7 us
    pallas_call x1, Pallas kernels, body(): pl.pallas_call(split_outputs, out_shape=(outs[0], outs[1], outs[2], jax.S...  2.44 us

profile of v8, /device:TPU:1, one launch (start us, length us, event | category | flops | bytes accessed | tf_op | source)
XLA Modules:
  0.0 74.9 jit_solution(15423241994596776149)
XLA Ops:
  0.6 71.7 %both_sections.1 = (bf16[1,1024,512]{2,1,0:T(8,128)(2,1)}, f32[1,8,4096]{2,1,0:T(8,128)}, f32[1,32,512]{2,1,0:T(8,128)}, f32[8,128]{1,0:T(8,128)}, f32[1,8,4096]{2,1,0:T(8,128)}, /*index=5*/f32[1,32,512]{2,1,0:T(8,128)}) custom-call(bf16[1,1024,512]{2,1,0:T(8,128)(2,1)} %x_hbm.1, bf16[1,512,4096]{2,1,0:T(8,128)(2,1)} %win_hbm.1, ...), custom_call_target="tpu_custom_call" | custom-call | tf_op jit(solution)/shard_map/both_sections/pallas_call | solution.py:1024
  72.4 2.4 %split_outputs.1 = (bf16[1,1024,512]{2,1,0:T(8,128)(2,1)}, f32[1,8,4096]{2,1,0:T(8,128)}, f32[1,32,512]{2,1,0:T(8,128)}, f32[1,2,8]{2,1,0:T(2,128)}, f32[1,8,8]{...) custom-call(bf16[1,1024,512]{2,1,0:T(8,128)(2,1)} %get-tuple-element.14.bout_in, ...), custom_call_target="tpu_custom_call" | custom-call | tf_op jit(solution)/shard_map/split_outputs/pallas_call | solution.py:1038
